TPU v7x, 256 devices: a whole 4x4x8 slice. The times are simulated.
256 devices in a mesh: gx: 4 (over x), gy: 8 (over z), gz: 8 (over y, core).
Axes of the slice: x: 4, y: 4, z: 8, core: 2. Of those that a mesh axis runs over, the one named last changes fastest.
Arguments:
- solution: float32 [4, 8, 32, 64, 1024], P(None, None, 'gx', 'gy', 'gz'), may hold values from -6 to 6
- residual: float32 [4, 8, 32, 64, 1024], P(None, None, 'gx', 'gy', 'gz'), may hold values from -21 to 21
- permeability: float32 [4, 32, 64, 1024], P(None, 'gx', 'gy', 'gz'), may hold values from 0.1 to 1
- storage: float32 [4, 32, 64, 1024], P(None, 'gx', 'gy', 'gz'), may hold values from 0.5 to 2
- tissue_mask: int32 [32, 64, 1024], P('gx', 'gy', 'gz'), may hold values 0 or 1
- tissue_label: int32 [32, 64, 1024], P('gx', 'gy', 'gz'), may hold values from 0 to 2
- exchange_table: float32 [3, 6], replicated, may hold values from 0.2 to 1
Outputs:
- new_solution: float32 [4, 8, 32, 64, 1024], P(None, None, 'gx', 'gy', 'gz')
- new_residual: float32 [4, 8, 32, 64, 1024], P(None, None, 'gx', 'gy', 'gz')
- basis: float32 [4, 32, 32, 64, 1024], P(None, None, 'gx', 'gy', 'gz')
All inputs are finite; a program needn't handle non-finite values. No bound on the sum of `tissue_mask` on one device may be relied on, other than what follows from the above.
Results may differ from a plain program's by a relative error of at most 0.027.
Values sent between devices are 32-bit elements; how exact they have to be, the bound alone decides.
No kernel may reach another device: no remote copies, remote signals or barrier semaphores. Data moves between devices by JAX's collectives and lax.ppermute only.
A program may use at most 128 MiB of HBM per device.

v0:
```python
import jax
import jax.numpy as jnp
import numpy as np
from jax import lax
from jax.sharding import PartitionSpec as P

RHS = 8
S = 4


PAIRS = ((0, 1), (0, 2), (0, 3), (1, 2), (1, 3), (2, 3))
SHIFTS = (2.0, 14.0, 6.0, 10.0)
NEWTON_SCALE = 8.0
HIGHEST_PRECISION = lax.Precision.HIGHEST


def padded(cells, sides, width):
    for axis, dim in sides:
        count = lax.axis_size(axis)
        ends = count - 1
        head = lax.slice_in_dim(cells, 0, width, axis=dim)
        tail = lax.slice_in_dim(cells, cells.shape[dim] - width, cells.shape[dim], axis=dim)
        cells = jnp.concatenate(
            [
                lax.ppermute(tail, axis, [(i, (i + 1) % count) for i in range(ends)]),
                cells,
                lax.ppermute(head, axis, [((i + 1) % count, i) for i in range(ends)]),
            ],
            axis=dim,
        )
    return cells


def shifted(array, direction, offset):
    leading = array.ndim - 3
    index = [slice(None)] * leading
    for dimension in range(3):
        length = array.shape[leading + dimension]
        if dimension == direction:
            index.append(slice(offset, length - 2 + offset))
        else:
            index.append(slice(1, length - 1))
    return array[tuple(index)]


def interior(array):
    return shifted(array, 0, 1)


def stencil(field, perm_pad, mask_pad, store_pad, rate_pad):
    centre = interior(field)
    perm_mid = interior(perm_pad)
    mask_mid = interior(mask_pad)
    result = interior(store_pad)[:, None] * centre
    for direction in range(3):
        for offset in (0, 2):
            faces = (
                0.5
                * (perm_mid + shifted(perm_pad, direction, offset))
                * (mask_mid * shifted(mask_pad, direction, offset))
            )
            result = result + faces[:, None] * (centre - shifted(field, direction, offset))
    rate_mid = interior(rate_pad)
    pieces = [result[number] for number in range(4)]
    for number, pair in enumerate(PAIRS):
        flow = rate_mid[number] * (centre[pair[0]] - centre[pair[1]])
        pieces[pair[0]] = pieces[pair[0]] + flow
        pieces[pair[1]] = pieces[pair[1]] - flow
    return jnp.stack(pieces)


def apply_padded(field_pad, coeff_pad):
    return stencil(field_pad, coeff_pad[0:4], coeff_pad[14], coeff_pad[4:8], coeff_pad[8:14])


def build_coefficients(permeability, storage, tissue_mask, tissue_label, exchange_table):
    mask_float = tissue_mask.astype(jnp.float32)
    rates = jnp.zeros((6,) + tissue_mask.shape, jnp.float32)
    for level in range(3):
        weight = (tissue_label == level).astype(jnp.float32)
        rates = rates + exchange_table[level][:, None, None, None] * weight[None]
    rates = rates * mask_float[None]
    return jnp.concatenate([permeability, storage, rates, mask_float[None]], 0)


def newton_table(steps, rhs_count):
    table = np.zeros(((steps + 1) * rhs_count, steps * rhs_count), np.float32)
    for index in range(steps):
        table[
            index * rhs_count : (index + 1) * rhs_count, index * rhs_count : (index + 1) * rhs_count
        ] = SHIFTS[index] * np.eye(rhs_count)
        table[
            (index + 1) * rhs_count : (index + 2) * rhs_count,
            index * rhs_count : (index + 1) * rhs_count,
        ] = NEWTON_SCALE * np.eye(rhs_count)
    return jnp.asarray(table)


def local_gram(blocks):
    stacked = jnp.stack(blocks)
    flat = stacked.reshape(stacked.shape[0], stacked.shape[1], stacked.shape[2], -1)
    gram = jnp.einsum("kcjm,lcim->kjli", flat, flat, precision=HIGHEST_PRECISION)
    total = stacked.shape[0] * stacked.shape[2]
    return gram.reshape(total, total)


def lower_factor(matrix):
    extent = matrix.shape[0]
    positions = jnp.arange(extent)
    columns = []
    for col_index in range(extent):
        column = matrix[:, col_index]
        for inner in range(col_index):
            column = column - columns[inner] * columns[inner][col_index]
        pivot_value = jnp.sqrt(column[col_index])
        column = jnp.where(positions >= col_index, column / pivot_value, jnp.zeros_like(column))
        columns.append(column)
    return jnp.stack(columns, 1)


def lower_inverse(lower):
    extent = lower.shape[0]
    identity = jnp.eye(extent, dtype=lower.dtype)
    solved_rows = []
    for row_index in range(extent):
        current_row = identity[row_index]
        for inner in range(row_index):
            current_row = current_row - lower[row_index, inner] * solved_rows[inner]
        solved_rows.append(current_row / lower[row_index, row_index])
    return jnp.stack(solved_rows, 0)


def matmul(left, right):
    return jnp.dot(left, right, precision=HIGHEST_PRECISION)


def project(gram, steps, rhs_count):
    width = steps * rhs_count
    table = newton_table(steps, rhs_count)
    leading = gram[:width, :width]
    leading = 0.5 * (leading + leading.T)
    lower_inv = lower_inverse(lower_factor(leading))
    moment = matmul(gram[:width, :], table)
    moment = 0.5 * (moment + moment.T)
    projected = matmul(matmul(lower_inv, moment), lower_inv.T)
    projected = 0.5 * (projected + projected.T)
    right_part = matmul(lower_inv, gram[:width, :rhs_count])
    proj_inv = lower_inverse(lower_factor(projected))
    solved = matmul(proj_inv.T, matmul(proj_inv, right_part))
    inverse = lower_inv.T
    coeff = matmul(inverse, solved)
    extended = matmul(table, coeff)
    return (inverse, coeff, extended)


def finish(solution, residual, blocks, inverse, coeff, extended, steps, rhs_count):
    stacked = jnp.stack(blocks)
    flat = stacked.reshape(stacked.shape[0], stacked.shape[1], stacked.shape[2], -1)
    basis = jnp.einsum(
        "kcjm,kjq->cqm",
        flat[:steps],
        inverse.reshape(steps, rhs_count, -1),
        precision=HIGHEST_PRECISION,
    )
    basis = basis.reshape((stacked.shape[1], steps * rhs_count) + stacked.shape[3:])
    update = jnp.einsum(
        "kcjm,kji->cim",
        flat[:steps],
        coeff.reshape(steps, rhs_count, rhs_count),
        precision=HIGHEST_PRECISION,
    )
    image = jnp.einsum(
        "kcjm,kji->cim",
        flat,
        extended.reshape(steps + 1, rhs_count, rhs_count),
        precision=HIGHEST_PRECISION,
    )
    return (
        solution + update.reshape(solution.shape),
        residual - image.reshape(residual.shape),
        basis,
    )


def body(solution, residual, permeability, storage, tissue_mask, tissue_label, exchange_table):
    coefficients = build_coefficients(
        permeability, storage, tissue_mask, tissue_label, exchange_table
    )
    blocks = [residual]
    coeff_rim = padded(coefficients, (("gx", 1), ("gy", 2), ("gz", 3)), 1)
    current = residual
    for index in range(S):
        field_pad = padded(current, (("gx", 2), ("gy", 3), ("gz", 4)), 1)
        applied = apply_padded(field_pad, coeff_rim)
        current = (applied - SHIFTS[index] * current) / NEWTON_SCALE
        blocks.append(current)
    gram = lax.psum(local_gram(blocks), ("gx", "gy", "gz"))
    inverse, coeff, extended = project(gram, S, RHS)
    return finish(solution, residual, blocks, inverse, coeff, extended, S, RHS)


def solution(mesh):
    return jax.shard_map(
        body,
        mesh=mesh,
        in_specs=(
            P(None, None, "gx", "gy", "gz"),
            P(None, None, "gx", "gy", "gz"),
            P(None, "gx", "gy", "gz"),
            P(None, "gx", "gy", "gz"),
            P("gx", "gy", "gz"),
            P("gx", "gy", "gz"),
            P(),
        ),
        out_specs=(
            P(None, None, "gx", "gy", "gz"),
            P(None, None, "gx", "gy", "gz"),
            P(None, None, "gx", "gy", "gz"),
        ),
        check_vma=False,
    )
```

profile of v0, /device:TPU:1, one launch (start us, length us, event | category | flops | bytes accessed | tf_op | source)
XLA Modules:
  0.0 1804.3 jit_solution(12916086023873227692)
XLA Ops:
  157.0 5.2 collective-permute-start.20
  164.7 5.0 collective-permute-done.21
  182.9 6.5 collective-permute-start.22
  237.1 7.7 collective-permute-start.28
  262.7 8.3 fusion.4
  271.1 76.1 %psum.7 = f32[40,40]{1,0:T(8,128)S(1)} all-reduce(f32[40,40]{1,0:T(8,128)S(1)} %fusion.4), channel_id=1, replica_groups=mesh['gx'=4,'gy'=8,'gz'=8] {'gx','gy','gz'}, use_global_device_ids=true, to_apply=%region_0.0 | all-reduce | flops 1600 | bytes 12800 | tf_op jit(solution)/shard_map/psum | solution.py:197
  364.4 6.0 fusion.186
  404.0 5.7 multiply_subtract_fusion.51
  411.7 6.2 multiply_subtract_fusion.50
  420.0 6.8 multiply_subtract_fusion.49
  432.5 7.5 multiply_subtract_fusion.48
  442.2 6.1 fusion.177
  448.3 8.1 multiply_subtract_fusion.47
  458.5 8.7 multiply_subtract_fusion.46
  469.1 9.5 multiply_subtract_fusion.45
  480.6 9.6 multiply_subtract_fusion.44
  492.4 10.8 multiply_subtract_fusion.43
  505.1 10.9 multiply_subtract_fusion.42
  518.2 11.8 multiply_subtract_fusion.41
  532.0 12.5 multiply_subtract_fusion.40
  546.4 12.9 multiply_subtract_fusion.39
  561.3 6.0 fusion.168
  567.2 13.7 multiply_subtract_fusion.38
  582.9 14.4 multiply_subtract_fusion.37
  599.4 14.9 multiply_subtract_fusion.36
  616.2 15.8 multiply_subtract_fusion.35
  634.0 16.6 multiply_subtract_fusion.34
  652.6 16.6 multiply_subtract_fusion.33
  671.2 17.2 multiply_subtract_fusion.32
  690.5 18.4 %multiply_subtract_fusion.31 = f32[32]{0:T(128)S(1)} fusion(f32[32]{0:T(128)S(1)} %get-tuple-element.34, f32[]{:T(128)} %bitcast.543, f32[]{:T(128)} %bitcast.542, f32[]{:T(128)} %bitcast.541, f32[]{:T(128)} %bitcast.540, f32[]{:T(128)} %bitcast.539, f32[]{:T(128)} %bitcast.538, f32[]{:T(128)} %bitcast.537, f32[]{:T(128)} %bitcast.536, f32[]{:T(128)} %bitcast.535, ...), kind=kLoop, calls=%fused_computation.604 | loop fusion | flops 4608 | bytes 4196 | tf_op jit(solution)/shard_map/sub | solution.py:114
  710.9 19.0 %multiply_subtract_fusion.30 = f32[32]{0:T(128)S(1)} fusion(f32[32]{0:T(128)S(1)} %get-tuple-element.33, f32[]{:T(128)} %bitcast.576, f32[]{:T(128)} %bitcast.575, f32[]{:T(128)} %bitcast.574, f32[]{:T(128)} %bitcast.573, f32[]{:T(128)} %bitcast.572, f32[]{:T(128)} %bitcast.571, f32[]{:T(128)} %bitcast.570, f32[]{:T(128)} %bitcast.569, f32[]{:T(128)} %bitcast.568, ...), kind=kLoop, calls=%fused_computation.602 | loop fusion | flops 4768 | bytes 4332 | tf_op jit(solution)/shard_map/sub | solution.py:114
  731.7 65.1 %subtract_divide_fusion.49 = (f32[1,32]{1,0:T(1,128)S(1)}, f32[1,32]{1,0:T(1,128)S(1)}, f32[1,32]{1,0:T(1,128)S(1)}, f32[1,32]{1,0:T(1,128)S(1)}, f32[1,32]{1,0:...) fusion(f32[32,32]{1,0:T(8,128)S(1)} %fusion.206, ...), kind=kLoop, calls=%fused_computation.639 | loop fusion | flops 6272 | bytes 4004 | tf_op jit(solution)/shard_map/div | solution.py:129
  796.8 137.1 %subtract_divide_fusion.38 = (f32[1,32]{1,0:T(1,128)S(1)}, f32[1,32]{1,0:T(1,128)S(1)}, f32[1,32]{1,0:T(1,128)S(1)}, f32[1,32]{1,0:T(1,128)S(1)}, f32[1,32]{1,0:...) fusion(f32[1,32]{1,0:T(1,128)S(1)} %get-tuple-element.113, ...), kind=kLoop, calls=%fused_computation.617 | loop fusion | flops 13728 | bytes 5488 | tf_op jit(solution)/shard_map/div | solution.py:129
  933.9 127.1 %subtract_divide_fusion.31 = (f32[1,32]{1,0:T(1,128)S(1)}, f32[1,32]{1,0:T(1,128)S(1)}, f32[1,32]{1,0:T(1,128)S(1)}, f32[1,32]{1,0:T(1,128)S(1)}, f32[1,32]{1,0:...) fusion(f32[1,32]{1,0:T(1,128)S(1)} %get-tuple-element.102, f32[1,32]{1,0:T(1,128)S(1)} %get-tuple-element.103, ...), kind=kLoop, calls=%fused_computation.603 | loop fusion | flops 12768 | bytes 5804 | tf_op jit(solution)/shard_map/div | solution.py:129
  1078.9 6.4 fusion.154
  1118.9 5.7 multiply_subtract_fusion.21
  1126.6 6.2 multiply_subtract_fusion.20
  1134.9 6.8 multiply_subtract_fusion.19
  1147.2 7.4 multiply_subtract_fusion.18
  1156.8 6.1 fusion.145
  1162.9 8.1 multiply_subtract_fusion.17
  1173.1 8.7 multiply_subtract_fusion.16
  1183.7 9.5 multiply_subtract_fusion.15
  1195.3 9.6 multiply_subtract_fusion.14
  1207.0 10.8 multiply_subtract_fusion.13
  1219.8 10.9 multiply_subtract_fusion.12
  1232.8 11.8 multiply_subtract_fusion.11
  1246.6 12.5 multiply_subtract_fusion.10
  1261.1 12.9 multiply_subtract_fusion.9
  1275.9 6.0 fusion.136
  1281.9 13.7 multiply_subtract_fusion.8
  1297.5 14.4 multiply_subtract_fusion.7
  1314.0 14.9 multiply_subtract_fusion.6
  1330.8 15.8 multiply_subtract_fusion.5
  1348.6 16.6 multiply_subtract_fusion.4
  1367.3 16.6 multiply_subtract_fusion.3
  1385.8 17.2 multiply_subtract_fusion.2
  1405.2 18.4 %multiply_subtract_fusion.1 = f32[32]{0:T(128)S(1)} fusion(f32[32]{0:T(128)S(1)} %get-tuple-element.4, f32[]{:T(128)} %bitcast.1105, f32[]{:T(128)} %bitcast.1104, f32[]{:T(128)} %bitcast.1103, f32[]{:T(128)} %bitcast.1102, f32[]{:T(128)} %bitcast.1101, f32[]{:T(128)} %bitcast.1100, f32[]{:T(128)} %bitcast.1099, f32[]{:T(128)} %bitcast.1098, f32[]{:T(128)} %bitcast.1097, ...), kind=kLoop, calls=%fused_computation.543 | loop fusion | flops 4608 | bytes 4196 | tf_op jit(solution)/shard_map/sub | solution.py:114
  1425.5 19.0 %multiply_subtract_fusion = f32[32]{0:T(128)S(1)} fusion(f32[32]{0:T(128)S(1)} %get-tuple-element.3, f32[]{:T(128)} %bitcast.1138, f32[]{:T(128)} %bitcast.1137, f32[]{:T(128)} %bitcast.1136, f32[]{:T(128)} %bitcast.1135, f32[]{:T(128)} %bitcast.1134, f32[]{:T(128)} %bitcast.1133, f32[]{:T(128)} %bitcast.1132, f32[]{:T(128)} %bitcast.1131, f32[]{:T(128)} %bitcast.1130, ...), kind=kLoop, calls=%fused_computation.541 | loop fusion | flops 4768 | bytes 4332 | tf_op jit(solution)/shard_map/sub | solution.py:114
  1446.3 65.1 %subtract_divide_fusion.18 = (f32[1,32]{1,0:T(1,128)S(1)}, f32[1,32]{1,0:T(1,128)S(1)}, f32[1,32]{1,0:T(1,128)S(1)}, f32[1,32]{1,0:T(1,128)S(1)}, f32[1,32]{1,0:...) fusion(f32[32,32]{1,0:T(8,128)S(1)} %fusion.206, ...), kind=kLoop, calls=%fused_computation.578 | loop fusion | flops 6272 | bytes 4004 | tf_op jit(solution)/shard_map/div | solution.py:129
  1511.5 137.1 %subtract_divide_fusion.7 = (f32[1,32]{1,0:T(1,128)S(1)}, f32[1,32]{1,0:T(1,128)S(1)}, f32[1,32]{1,0:T(1,128)S(1)}, f32[1,32]{1,0:T(1,128)S(1)}, f32[1,32]{1,0:T...) fusion(f32[1,32]{1,0:T(1,128)S(1)} %get-tuple-element.81, ...), kind=kLoop, calls=%fused_computation.556 | loop fusion | flops 13728 | bytes 5488 | tf_op jit(solution)/shard_map/div | solution.py:129
  1648.6 127.1 %subtract_divide_fusion = (f32[1,32]{1,0:T(1,128)S(1)}, f32[1,32]{1,0:T(1,128)S(1)}, f32[1,32]{1,0:T(1,128)S(1)}, f32[1,32]{1,0:T(1,128)S(1)}, f32[1,32]{1,0:T(1...) fusion(f32[1,32]{1,0:T(1,128)S(1)} %get-tuple-element.70, f32[1,32]{1,0:T(1,128)S(1)} %get-tuple-element.71, ...), kind=kLoop, calls=%fused_computation.542 | loop fusion | flops 12768 | bytes 5804 | tf_op jit(solution)/shard_map/div | solution.py:129
  1776.6 11.7 fusion.131
  1788.3 7.5 fusion.3
  (555 shorter events, 399.0 us)
Async XLA Ops:
  0.6 8.7 copy-start
  2.2 55.6 %copy-start.49 = (f32[1,8,8,128]{3,2,1,0:T(8,128)}, f32[1,8,8,128]{3,2,1,0:T(8,128)S(1)}, u32[]{:S(2)}) copy-start(f32[1,8,8,128]{3,2,1,0:T(8,128)S(1)} %get-tuple-element.202) | copy-start | bytes 98308
  3.9 12.6 copy-start.9
  3.9 12.6 copy-start.10
  3.9 17.9 collective-permute-start
  8.0 13.8 collective-permute-start.1
  10.0 18.1 %collective-permute-start.7 = (f32[4,8,1,8,128]{4,1,3,2,0:T(8,128)S(1)}, f32[4,8,1,8,128]{4,1,3,2,0:T(8,128)S(1)}, u32[]{:S(2)}, u32[]{:S(2)}) collective-permute-start(f32[4,8,1,8,128]{4,1,3,2,0:T(8,128)S(1)} %get-tuple-element.169), channel_id=1, source_target_pairs={{64,0},{128,64},{192,128},{65,1},{129,65},{193,129},{66,2},{130,66... | collective-permute-start | bytes 393224 | tf_op jit(solution)/shard_map/ppermute | solution.py:27
  11.3 16.1 collective-permute-start.6
  16.6 74.7 %copy-start.32 = (f32[8,8,128]{2,1,0:T(8,128)}, f32[8,8,128]{2,1,0:T(8,128)S(1)}, u32[]{:S(2)}) copy-start(f32[8,8,128]{2,1,0:T(8,128)S(1)} %get-tuple-element.183) | copy-start | bytes 98308
  16.6 74.7 %copy-start.36 = (f32[8,8,128]{2,1,0:T(8,128)}, f32[8,8,128]{2,1,0:T(8,128)S(1)}, u32[]{:S(2)}) copy-start(f32[8,8,128]{2,1,0:T(8,128)S(1)} %get-tuple-element.184) | copy-start | bytes 98308
  16.6 74.7 %copy-start.40 = (f32[8,8,128]{2,1,0:T(8,128)}, f32[8,8,128]{2,1,0:T(8,128)S(1)}, u32[]{:S(2)}) copy-start(f32[8,8,128]{2,1,0:T(8,128)S(1)} %get-tuple-element.185) | copy-start | bytes 98308
  16.6 74.7 %copy-start.44 = (f32[8,8,128]{2,1,0:T(8,128)}, f32[8,8,128]{2,1,0:T(8,128)S(1)}, u32[]{:S(2)}) copy-start(f32[8,8,128]{2,1,0:T(8,128)S(1)} %get-tuple-element.188) | copy-start | bytes 98308
  21.8 36.0 %copy-start.48 = (f32[15,1,8,128]{3,2,1,0:T(8,128)}, f32[15,1,8,128]{3,2,1,0:T(8,128)S(1)}, u32[]{:S(2)}) copy-start(f32[15,1,8,128]{3,2,1,0:T(8,128)S(1)} %collective-permute-done.1) | copy-start | bytes 184324
  21.9 6.2 collective-permute-start.3
  23.2 5.6 collective-permute-start.2
  28.2 29.6 %copy-start.50 = (f32[15,10,1,128]{3,2,1,0:T(1,128)}, f32[15,10,1,128]{3,2,1,0:T(1,128)S(1)}, u32[]{:S(2)}) copy-start(f32[15,10,1,128]{3,2,1,0:T(1,128)S(1)} %copy.194) | copy-start | bytes 230404
  29.3 25.8 %copy-start.51 = (f32[15,10,1,128]{3,2,1,0:T(1,128)}, f32[15,10,1,128]{3,2,1,0:T(1,128)S(1)}, u32[]{:S(2)}) copy-start(f32[15,10,1,128]{3,2,1,0:T(1,128)S(1)} %copy.193) | copy-start | bytes 230404
  36.0 17.0 collective-permute-start.5
  40.1 10.8 collective-permute-start.4
  44.9 14.5 collective-permute-start.8
  49.6 9.8 collective-permute-start.9
  57.8 29.5 %copy-start.30 = (f32[4,8,8,128]{3,2,1,0:T(8,128)}, f32[4,8,8,128]{3,2,1,0:T(8,128)S(1)}, u32[]{:S(2)}) copy-start(f32[4,8,8,128]{3,2,1,0:T(8,128)S(1)} %get-tuple-element.175) | copy-start | bytes 393220
  57.8 29.5 %copy-start.31 = (f32[4,8,8,128]{3,2,1,0:T(8,128)}, f32[4,8,8,128]{3,2,1,0:T(8,128)S(1)}, u32[]{:S(2)}) copy-start(f32[4,8,8,128]{3,2,1,0:T(8,128)S(1)} %get-tuple-element.176) | copy-start | bytes 393220
  59.4 27.9 %copy-start.25 = (f32[4,8,8,128]{3,2,1,0:T(8,128)}, f32[4,8,8,128]{3,2,1,0:T(8,128)S(1)}, u32[]{:S(2)}) copy-start(f32[4,8,8,128]{3,2,1,0:T(8,128)S(1)} %get-tuple-element.182) | copy-start | bytes 393220
  71.0 12.2 collective-permute-start.11
  73.0 6.2 collective-permute-start.10
  77.7 9.6 copy-start.27
  77.7 9.6 copy-start.29
  77.7 9.6 copy-start.74
  77.7 9.6 copy-start.76
  92.8 5.6 collective-permute-start.12
  96.5 6.0 collective-permute-start.13
  98.4 16.8 copy-start.55
  102.5 12.7 copy-start.57
  102.5 8.0 collective-permute-start.14
  106.5 8.6 collective-permute-start.15
  110.5 4.7 copy-start.70
  121.4 10.0 collective-permute-start.16
  129.4 6.6 collective-permute-start.17
  139.2 4.3 copy-start.45
  139.2 4.3 copy-start.64
  147.9 5.8 collective-permute-start.18
  151.0 5.9 collective-permute-start.19
  153.7 9.8 copy-start.7
  153.7 16.1 copy-start.54
  156.9 12.8 copy-start.56
  157.0 7.8 collective-permute-start.20
  162.2 7.6 collective-permute-start.21
  164.7 5.0 copy-start.69
  180.9 15.0 collective-permute-start.23
  182.9 9.0 collective-permute-start.22
  189.4 10.7 copy-start.2
  189.4 10.7 copy-start.26
  189.4 10.7 copy-start.28
  205.7 3.9 collective-permute-start.24
  207.3 5.7 collective-permute-start.25
  209.6 14.3 copy-start.52
  213.0 11.0 copy-start.53
  213.0 7.2 collective-permute-start.26
  217.9 6.1 collective-permute-start.27
  235.1 15.8 collective-permute-start.29
  237.1 9.8 collective-permute-start.28
  262.7 169.6 %copy-start.77 = (f32[40,32]{1,0:T(8,128)S(1)}, f32[40,32]{1,0:T(8,128)}, u32[]{:S(2)}) copy-start(f32[40,32]{1,0:T(8,128)} %constant.92.clone) | copy-start | bytes 15364
  1776.6 11.7 copy-start.8
  (44 other events, 98.0 us)
where the time goes:
time: 1830 us; the launch traced here: 1800 us
  other arithmetic  1320 us (72%)
  local copies, waits for them, and re-layouts  207 us (11%)
  starting transfers between devices  90.5 us (5%)
  blocking collectives  76.1 us (4%)
  between operations  47.1 us (3%)
  waiting for transfers between devices  34.7 us (2%)
  matrix products  32.4 us (2%)
    div x6, other arithmetic, lower_inverse(): solved_rows.append(current_row / lower[row_index, row_index])  659 us
    sub x68, other arithmetic, lower_factor(): column = column - columns[inner] * columns[inner][col_index]  621 us
    psum x1, blocking collectives, body(): gram = lax.psum(local_gram(blocks), ('gx', 'gy', 'gz'))  76.1 us
    ppermute x15, starting transfers between devices, padded(): lax.ppermute(tail, axis, [(i, (i + 1) % count) for i in range(ends)])  65.6 us
    slice x64, local copies, waits for them, and re-layouts, lower_factor(): pivot_value = jnp.sqrt(column[col_index])  39.9 us
    slice x54, local copies, waits for them, and re-layouts, lower_inverse(): current_row = current_row - lower[row_index, inner] * solved_rows[inner]  38.3 us
  transfers between devices with their start and end apart: 30, of which 14 were waited for; matrix products, arithmetic and copies ran while one was open for 2% of the time, Pallas kernels for 0%

commit v1 on v0

v1 whole, which is shorter than its diff:
```python
import jax
import jax.numpy as jnp
from jax import lax
from jax.experimental import pallas as pl
from jax.experimental.pallas import tpu as pltpu
from jax.sharding import PartitionSpec as P

COMP = 4
RHS = 8
S = 4
PAIRS = ((0, 1), (0, 2), (0, 3), (1, 2), (1, 3), (2, 3))
SHIFTS = (2.0, 14.0, 6.0, 10.0)
SCALE = 8.0
F32 = jnp.float32
BF16 = jnp.bfloat16

NX, NY, NZ = 8, 8, 128
FACE = COMP * 8
BLOCKS = tuple((a, b) for b in range(5) for a in range(min(b, 3) + 1))
VMEM = pl.BlockSpec(memory_space=pltpu.VMEM)
SMEM = pl.BlockSpec(memory_space=pltpu.SMEM)


def pair_index(a, b):
    return PAIRS.index((min(a, b), max(a, b)))


def lane_ids(shape):
    return lax.broadcasted_iota(jnp.int32, shape, len(shape) - 1)


def put_ends(acc, tile, lane, slot):
    return jnp.where((lane >> 1) == slot, pltpu.roll(tile, 2 * slot + 1, 1), acc)


def fetch(pairs, sems):
    copies = [pltpu.make_async_copy(src, dst, sems.at[i]) for i, (src, dst) in enumerate(pairs)]
    for copy in copies:
        copy.start()
    return copies


def pack_kernel(edge, res_hbm, perm_hbm, mask_hbm, v0, xlo, xhi, ylo, yhi, ends, pm, res, mask, sems):
    lane = lane_ids((8, NZ))
    copies = fetch(
        [(perm_hbm, pm.at[pl.ds(0, COMP)]), (mask_hbm, mask), (res_hbm, res)], sems
    )
    for f in range(COMP + 5):
        ends[f] = jnp.zeros((8, NZ), F32)
    copies[0].wait()
    copies[1].wait()

    def loop_coef(x, _):
        pm[COMP, x] = mask[x].astype(F32)
        for f in range(5):
            tile = pm[f, x]
            ylo[FACE + f, pl.ds(x, 1), :] = tile[0:1]
            yhi[FACE + f, pl.ds(x, 1), :] = tile[7:8]
            acc = put_ends(jnp.zeros((8, NZ), F32), tile, lane, 0)
            ends[COMP + f] = jnp.where((lane >> 1) == x, pltpu.roll(acc, 2 * x, 1), ends[COMP + f])
        return 0

    lax.fori_loop(0, NX, loop_coef, 0)
    for f in range(5):
        xlo[FACE + f] = pm[f, 0]
        xhi[FACE + f] = pm[f, NX - 1]
    copies[2].wait()

    def loop(x, _):
        for c in range(COMP):
            acc = jnp.zeros((8, NZ), F32)
            for y in range(NY):
                tile = res[pl.ds(c * 512 + x * 8 + y, 8, stride=64), :]
                v0[c, x, y] = tile
                acc = put_ends(acc, tile, lane, y)
                if y == 0:
                    ylo[c * 8 + x] = tile
                if y == NY - 1:
                    yhi[c * 8 + x] = tile
            ends[c] = jnp.where((lane >> 4) == x, pltpu.roll(acc, 16 * x, 1), ends[c])
        return 0

    lax.fori_loop(0, NX, loop, 0)
    for c in range(COMP):
        for y in range(NY):
            xlo[c * 8 + y] = v0[c, 0, y]
            xhi[c * 8 + y] = v0[c, NX - 1, y]


def prepare_kernel(table, pm, sol_hbm, store_hbm, label_hbm, sol, rate, base, label, sems):
    copies = fetch([(store_hbm, base), (label_hbm, label), (sol_hbm, sol)], sems)
    copies[0].wait()
    copies[1].wait()

    def loop(x, _):
        m = pm[COMP, x] * (1.0 / SCALE)
        kind = label[x]
        rates = []
        for q in range(6):
            value = jnp.where(kind == 0, table[0, q], jnp.where(kind == 1, table[1, q], table[2, q]))
            rates.append(m * value)
            rate[q, x] = rates[q]
        for c in range(COMP):
            total = base[c, x] * (1.0 / SCALE)
            for b in range(COMP):
                if b != c:
                    total = total + rates[pair_index(c, b)]
            base[c, x] = total
        return 0

    lax.fori_loop(0, NX, loop, 0)
    copies[2].wait()


def coefficients(edge, inner, base, halo, tx, ty, tz, diag, pm, ghost):
    xl, xh, yl, yh, zl, zh = halo
    lane = lane_ids((8, NZ))
    sub = lax.broadcasted_iota(jnp.int32, (8, NZ), 0)
    keep = [edge[i].astype(F32) for i in range(6)]
    for f in range(5):
        last = f == 4
        pm[f, 0] = xl[FACE + f] * keep[0] if last else xl[FACE + f]
        pm[f, NX + 1] = xh[FACE + f] * keep[1] if last else xh[FACE + f]
        for x in range(NX):
            pm[f, x + 1] = inner[f, x]
        below, above = zl[COMP + f], zh[COMP + f]
        if last:
            below, above = below * keep[4], above * keep[5]
        ghost[f] = jnp.where((lane & 1) == 0, below, above)

    def loop(x, _):
        m = pm[4, x + 1]
        def near(f, own):
            g = pltpu.roll(ghost[f], (127 - 2 * x) & 127, 1)
            row_lo = yl[FACE + f, pl.ds(x, 1), :]
            row_hi = yh[FACE + f, pl.ds(x, 1), :]
            if f == 4:
                row_lo, row_hi = row_lo * keep[2], row_hi * keep[3]
            y_lo = jnp.where(sub == 0, row_lo, pltpu.roll(own, 1, 0))
            y_hi = jnp.where(sub == 7, row_hi, pltpu.roll(own, 7, 0))
            z_lo = pltpu.roll(jnp.where(lane == 127, g, own), 1, 1)
            z_hi = pltpu.roll(jnp.where(lane == 0, g, own), 127, 1)
            return y_lo, y_hi, z_lo, z_hi

        masks = [m * n for n in near(4, m)]
        for c in range(COMP):
            own = pm[c, x + 1]
            values = [
                (-0.5 / SCALE) * (own + n) * mm for n, mm in zip(near(c, own), masks)
            ]
            x_lo = (-0.5 / SCALE) * (own + pm[c, x]) * (m * pm[4, x])
            x_hi = (-0.5 / SCALE) * (own + pm[c, x + 2]) * (m * pm[4, x + 2])
            tx[c, x] = x_lo
            tx[c, x + 1] = x_hi
            ty[c, x], ty[COMP + c, x] = values[0], values[1]
            tz[c, x], tz[COMP + c, x] = values[2], values[3]
            diag[c, x] = base[c, x] - values[0] - values[1] - values[2] - values[3] - x_lo - x_hi
        return 0

    lax.fori_loop(0, NX, loop, 0)


def apply_step(shift, cur, halo, tx, ty, tz, diag, rate, vp, ghost, out, sends):
    xl, xh, yl, yh, zl, zh = halo
    lane = lane_ids((8, NZ))
    first, last = lane == 0, lane == 127
    for c in range(COMP):
        for y in range(NY):
            vp[c, 0, y] = xl[c * 8 + y]
            vp[c, NX + 1, y] = xh[c * 8 + y]
        ghost[c] = jnp.where((lane & 1) == 0, zl[c], zh[c])

    def copy(x, _):
        for c in range(COMP):
            for y in range(NY):
                vp[c, x + 1, y] = cur[c, x, y]
        return 0

    lax.fori_loop(0, NX, copy, 0)
    if sends is not None:
        for c in range(COMP):
            sends[4][c] = jnp.zeros((8, NZ), F32)

    def loop(x, _):
        near_z = [pltpu.roll(ghost[c], (128 - 16 * x) & 127, 1) for c in range(COMP)]
        acc = [jnp.zeros((8, NZ), F32) for _ in range(COMP)]
        low = [yl[c * 8 + x] for c in range(COMP)]
        own = [vp[c, x + 1, 0] for c in range(COMP)]
        for y in range(NY):
            if y < NY - 1:
                high = [vp[c, x + 1, y + 1] for c in range(COMP)]
            else:
                high = [yh[c * 8 + x] for c in range(COMP)]
            rates = [rate[q, x, pl.ds(y, 1), :] for q in range(6)]
            for c in range(COMP):
                p = own[c]
                g = pltpu.roll(near_z[c], 127 - 2 * y, 1)
                z_lo = pltpu.roll(jnp.where(last, g, p), 1, 1)
                z_hi = pltpu.roll(jnp.where(first, g, p), 127, 1)
                row = pl.ds(y, 1)
                value = (diag[c, x, row, :] - shift / SCALE) * p
                side = tx[c, x, row, :] * vp[c, x, y] + tx[c, x + 1, row, :] * vp[c, x + 2, y]
                value = value + ty[c, x, row, :] * low[c]
                side = side + ty[COMP + c, x, row, :] * high[c]
                value = value + tz[c, x, row, :] * z_lo
                side = side + tz[COMP + c, x, row, :] * z_hi
                others = [b for b in range(COMP) if b != c]
                flow = rates[pair_index(c, others[0])] * own[others[0]]
                for b in others[1:]:
                    flow = flow + rates[pair_index(c, b)] * own[b]
                value = (value + side) - flow
                out[c, x, y] = value
                if sends is not None:
                    acc[c] = put_ends(acc[c], value, lane, y)
                    if y == 0:
                        sends[2][c * 8 + x] = value
                    if y == NY - 1:
                        sends[3][c * 8 + x] = value
            low, own = own, high
        if sends is not None:
            for c in range(COMP):
                sends[4][c] = jnp.where((lane >> 4) == x, pltpu.roll(acc[c], 16 * x, 1), sends[4][c])
        return 0

    lax.fori_loop(0, NX, loop, 0)
    if sends is not None:
        for c in range(COMP):
            for y in range(NY):
                sends[0][c * 8 + y] = out[c, 0, y]
                sends[1][c * 8 + y] = out[c, NX - 1, y]


def first_kernel(edge, piece, cur, inner, base, rate, *refs):
    halo, refs = refs[:6], refs[6:]
    out, sends, coef, scratch = refs[0], refs[1:6], refs[6:10], refs[10:]
    vp, ghost, pm, ghost_c = scratch
    coefficients(edge, inner, base, halo, *coef, pm, ghost_c)
    apply_step(SHIFTS[0], cur, halo, *coef, rate, vp, ghost, out, sends)


def step_kernel(index, piece, cur, *refs):
    halo, coef, refs = refs[:6], refs[6:11], refs[11:]
    out, refs = refs[0], refs[1:]
    sends = None
    if index < S - 1:
        sends, refs = refs[:5], refs[5:]
    apply_step(SHIFTS[index], cur, halo, *coef, *refs, out, sends)


def gram_kernel(index, cur, *refs):
    older, refs = refs[:index], refs[index:]
    before = None
    if index:
        before, refs = refs[0], refs[1:]
    split, out = refs
    lane = lane_ids((8, NZ))
    count = min(index, 3) + 1
    tall = 16 * count

    def loop(x, total):
        tiles = []
        for c in range(COMP):
            for y in range(NY):
                v = cur[c, x, y]
                high = v.astype(BF16).astype(F32)
                tile = jnp.concatenate([high, v - high], 0).astype(BF16)
                split[c, x, y] = tile
                tiles.append(tile)
        right = jnp.concatenate(tiles, 1)
        lefts = [
            jnp.concatenate([older[k][c, x, y] for c in range(COMP) for y in range(NY)], 1)
            for k in range(min(index, count))
        ]
        if count > index:
            lefts.append(right)
        left = jnp.concatenate(lefts, 0) if len(lefts) > 1 else lefts[0]
        return total + lax.dot_general(
            left, right, (((1,), (1,)), ((), ())), preferred_element_type=F32
        )

    total = lax.fori_loop(0, NX, loop, jnp.zeros((tall, 16), F32))
    wide = jnp.concatenate([total, jnp.zeros((tall, NZ - 16), F32)], 1)
    value = jnp.zeros((8, NZ), F32)
    for a in range(count):
        both = wide[16 * a : 16 * a + 8] + wide[16 * a + 8 : 16 * a + 16]
        both = both + pltpu.roll(both, NZ - 8, 1)
        slot = BLOCKS.index((a, index))
        value = jnp.where((lane >> 3) == slot, pltpu.roll(both, 8 * slot, 1), value)
    if index:
        value = value + before[...]
    if index < S:
        out[...] = value
    else:
        for copy in range(out.shape[0]):
            out[copy] = value


def relay_kernel(parts, out):
    total = parts[0]
    for i in range(1, parts.shape[0]):
        total = total + parts[i]
    for copy in range(out.shape[0]):
        out[copy] = total


def lane_group(tile, source, target):
    return pltpu.roll(tile, (8 * (target - source)) % NZ, 1)


def factor(packed, weight):
    lane8 = lane_ids((8, NZ)) >> 3
    turned = jnp.transpose(jnp.concatenate([packed, jnp.zeros((NZ - 8, NZ), F32)], 0))
    rows = []
    for a in range(S):
        line = jnp.zeros((8, NZ), F32)
        for b in range(S + 1):
            if a <= b:
                block = lane_group(packed, BLOCKS.index((a, b)), b)
            else:
                slot = BLOCKS.index((b, a))
                block = lane_group(turned[8 * slot : 8 * slot + 8], 0, b)
            if a == b:
                slot = BLOCKS.index((a, a))
                other = lane_group(turned[8 * slot : 8 * slot + 8], 0, b)
                block = 0.5 * (block + other)
            line = jnp.where(lane8 == b, block, line)
        rows.append(line)
    gram = jnp.concatenate(rows, 0)
    lane = lane_ids((32, NZ))
    row = lax.broadcasted_iota(jnp.int32, (32, NZ), 0)
    group = lane >> 3
    sigma = jnp.where(
        group == 0, SHIFTS[0], jnp.where(group == 1, SHIFTS[1], jnp.where(group == 2, SHIFTS[2], SHIFTS[3]))
    )
    moment = jnp.where(lane < 32, sigma * gram + SCALE * pltpu.roll(gram, NZ - 8, 1), 0.0)
    flipped = jnp.transpose(jnp.concatenate([moment, jnp.zeros((NZ - 32, NZ), F32)], 0))[:32]
    moment = 0.5 * (moment + flipped)
    left = jnp.where(lane < 32, gram, jnp.where(lane == row + 32, 1.0, 0.0))
    right = jnp.where(lane < 32, moment, jnp.where(group == 4, pltpu.roll(gram, 32, 1), 0.0))
    inverse = jnp.zeros((32, NZ), F32)
    for j in range(0, 32, 2):
        kept = []
        for matrix in (left, right):
            c0 = jnp.broadcast_to(matrix[:, j : j + 1], (32, NZ))
            c1 = jnp.broadcast_to(matrix[:, j + 1 : j + 2], (32, NZ))
            r0, r1 = matrix[j : j + 1], matrix[j + 1 : j + 2]
            p, q, r = c0[j : j + 1], c1[j : j + 1], c1[j + 1 : j + 2]
            inv = 1.0 / (p * r - q * q)
            n0, n1 = (r * r0 - q * r1) * inv, (p * r1 - q * r0) * inv
            kept.append((matrix - c0 * n0 - c1 * n1, r0, r1, p, q, r, n0, n1))
        left, r0, r1, p, q, r, _, _ = kept[0]
        ratio = q / p
        inverse = jnp.where(row == j, r0 * lax.rsqrt(p), inverse)
        inverse = jnp.where(row == j + 1, (r1 - ratio * r0) * lax.rsqrt(r - q * ratio), inverse)
        right, n0, n1 = kept[1][0], kept[1][6], kept[1][7]
        right = jnp.where(row == j, n0, jnp.where(row == j + 1, n1, right))
    inverse = pltpu.roll(inverse, NZ - 32, 1)
    coeff = pltpu.roll(right, NZ - 32, 1)
    coeff = jnp.transpose(jnp.concatenate([coeff, jnp.zeros((NZ - 32, NZ), F32)], 0))[:8]
    coeff = jnp.where(lane8 < S, coeff, 0.0)
    ext = SCALE * pltpu.roll(coeff, 8, 1)
    for k in range(S):
        ext = jnp.where(lane8 == k, ext + SHIFTS[k] * coeff, ext)
    full = jnp.concatenate([jnp.where(lane < 32, inverse, 0.0), coeff, ext], 0)
    lanes = lane_ids((48, NZ))
    spread = jnp.zeros((48, NZ), F32)
    for k in range(S + 1):
        for part in range(2):
            spread = jnp.where(
                (lanes >> 3) == 2 * k + part, pltpu.roll(full, (8 * (2 * k + part - k)) % NZ, 1), spread
            )
    high = spread.astype(BF16)
    low = (spread - high.astype(F32)).astype(BF16)
    weight[0:48] = high
    weight[48:96] = low


def finish_kernel(packed, s0, s1, s2, s3, s4, sol, v0, new_sol, new_res, basis, weight):
    c = pl.program_id(0)

    @pl.when(c == 0)
    def _():
        total = packed[0]
        for i in range(1, packed.shape[0]):
            total = total + packed[i]
        factor(total, weight)

    def loop(i, _):
        spots = [(4 * i + u, y) for u in range(4) for y in range(NY)]
        lines = [jnp.concatenate([s[c, x, y] for x, y in spots], 1) for s in (s0, s1, s2, s3, s4)]
        stack = jnp.concatenate(lines, 0)
        both = jnp.dot(weight[:, 0:80], stack, preferred_element_type=F32)
        both = both[0:48] + both[48:96]
        for number, (x, y) in enumerate(spots):
            part = both[:, number * NZ : (number + 1) * NZ]
            for q in range(4):
                basis[pl.ds(512 * q + x * 8 + y, 8, stride=64), :] = part[8 * q : 8 * q + 8]
            spot = pl.ds(x * 8 + y, 8, stride=64)
            new_sol[spot, :] = sol[pl.ds(c * 512 + x * 8 + y, 8, stride=64), :] + part[32:40]
            new_res[spot, :] = v0[c, x, y] - part[40:48]
        return 0

    lax.fori_loop(0, 2, loop, 0)


def shaped(*shape, dtype=F32):
    return jax.ShapeDtypeStruct(shape, dtype)


def near(*shape, dtype=F32):
    return pltpu.VMEM(shape, dtype)


def far(array):
    return pltpu.with_memory_space_constraint(array, pltpu.HBM)


def params(mib):
    return pltpu.CompilerParams(vmem_limit_bytes=mib << 20)


def exchange(sends):
    moved = []
    for number, (axis, up) in enumerate((("gx", 1), ("gx", 0), ("gy", 1), ("gy", 0), ("gz", 1), ("gz", 0))):
        count = lax.axis_size(axis)
        if up:
            links = [(i, (i + 1) % count) for i in range(count)]
        else:
            links = [((i + 1) % count, i) for i in range(count)]
        if axis == "gz":
            source = sends[4]
        else:
            source = sends[number + 1 if up else number - 1]
        moved.append(lax.ppermute(source, axis, links))
    return moved


def body(solution, residual, permeability, storage, tissue_mask, tissue_label, exchange_table):
    flat = residual.reshape(-1, NZ)
    edge = []
    for axis in ("gx", "gy", "gz"):
        place = lax.axis_index(axis)
        edge += [place > 0, place < lax.axis_size(axis) - 1]
    edge = jnp.stack(edge).astype(jnp.int32)
    field = near(COMP, NX, NY, RHS, NZ)
    face = near(FACE + 5, 8, NZ)
    total = COMP * RHS * NX * NY
    in_hbm = pl.BlockSpec(memory_space=pltpu.HBM)
    v0, *sends, inner = pl.pallas_call(
        pack_kernel,
        out_shape=(field, face, face, face, face, face, near(5, NX, NY, NZ)),
        in_specs=[SMEM] + [in_hbm] * 3,
        out_specs=[VMEM] * 7,
        scratch_shapes=[
            pltpu.VMEM((total, NZ), F32),
            pltpu.VMEM((NX, NY, NZ), jnp.int32),
            pltpu.SemaphoreType.DMA((3,)),
        ],
        compiler_params=params(5),
        name="pack",
    )(edge, far(flat), far(permeability), far(tissue_mask))

    wide, tall = lax.axis_size("gx") * lax.axis_size("gz"), lax.axis_size("gy")

    def gram(index, current, older, before):
        inputs = [current, *older, *before]
        return pl.pallas_call(
            lambda *refs: gram_kernel(index, *refs),
            out_shape=(
                near(COMP, NX, NY, 16, NZ, dtype=BF16),
                near(8, NZ) if index < S else near(wide, 8, NZ),
            ),
            in_specs=[VMEM] * len(inputs),
            out_specs=[VMEM] * 2,
            compiler_params=params(5),
            cost_estimate=pl.CostEstimate(
                flops=2 * 16 * 16 * (index + 1) * 32768, bytes_accessed=(3 + index) << 20, transcendentals=0
            ),
            name=f"gram{index}",
        )(*inputs)

    halo = exchange(sends)
    splits = []
    sol, rate, base = pl.pallas_call(
        prepare_kernel,
        out_shape=(near(total, NZ), near(6, NX, NY, NZ), near(COMP, NX, NY, NZ)),
        in_specs=[SMEM, VMEM] + [in_hbm] * 3,
        out_specs=[VMEM] * 3,
        scratch_shapes=[pltpu.VMEM((NX, NY, NZ), jnp.int32), pltpu.SemaphoreType.DMA((3,))],
        compiler_params=params(5),
        name="prepare",
    )(exchange_table, inner, far(solution.reshape(total, NZ)), far(storage), far(tissue_label))
    split, piece = gram(0, v0, [], [])
    splits.append(split)
    face = near(FACE, 8, NZ)
    side_outs = [face] * 5
    coef_shapes = [
        near(COMP, NX + 1, NY, NZ),
        near(2 * COMP, NX, NY, NZ),
        near(2 * COMP, NX, NY, NZ),
        near(COMP, NX, NY, NZ),
    ]
    work = [pltpu.VMEM((COMP, NX + 2, NY, RHS, NZ), F32), pltpu.VMEM((COMP, 8, NZ), F32)]
    results = pl.pallas_call(
        first_kernel,
        out_shape=[field] + side_outs + coef_shapes,
        in_specs=[SMEM] + [VMEM] * 11,
        out_specs=[VMEM] * 10,
        scratch_shapes=work + [pltpu.VMEM((5, NX + 2, NY, NZ), F32), pltpu.VMEM((5, 8, NZ), F32)],
        compiler_params=params(8),
        name="step1",
    )(edge, piece, v0, inner, base, rate, *halo)
    current, sends, coef = results[0], results[1:6], list(results[6:10]) + [rate]
    for index in range(1, S):
        halo = exchange(sends)
        split, piece = gram(index, current, splits, [piece])
        splits.append(split)
        outs = [field] + (side_outs if index < S - 1 else [])
        results = pl.pallas_call(
            lambda *refs, index=index: step_kernel(index, *refs),
            out_shape=outs,
            in_specs=[VMEM] * 13,
            out_specs=[VMEM] * len(outs),
            scratch_shapes=work,
            compiler_params=params(6),
            name=f"step{index + 1}",
        )(piece, current, *halo, *coef)
        current, sends = results[0], results[1:]
    split, piece = gram(S, current, splits, [piece])
    splits.append(split)
    parts = lax.all_to_all(piece, ("gx", "gz"), 0, 0)
    parts = pl.pallas_call(
        relay_kernel,
        out_shape=near(tall, 8, NZ),
        in_specs=[VMEM],
        out_specs=VMEM,
        compiler_params=params(2),
        name="relay",
    )(parts)
    packed = lax.all_to_all(parts, ("gy",), 0, 0)
    rows = pl.BlockSpec((RHS * NX * NY, NZ), lambda c: (c, 0))
    new_sol, new_res, basis = pl.pallas_call(
        finish_kernel,
        grid=(COMP,),
        out_shape=(shaped(total, NZ), shaped(total, NZ), shaped(total * S, NZ)),
        in_specs=[VMEM] * 8,
        out_specs=(rows, rows, pl.BlockSpec((S * RHS * NX * NY, NZ), lambda c: (c, 0))),
        scratch_shapes=[pltpu.VMEM((96, NZ), BF16)],
        compiler_params=params(14),
        name="finish",
    )(packed, *splits, sol, v0)
    return (
        new_sol.reshape(solution.shape),
        new_res.reshape(residual.shape),
        basis.reshape((COMP, S * RHS) + solution.shape[2:]),
    )


def solution(mesh):
    wide = P(None, None, "gx", "gy", "gz")
    return jax.shard_map(
        body,
        mesh=mesh,
        in_specs=(
            wide,
            wide,
            P(None, "gx", "gy", "gz"),
            P(None, "gx", "gy", "gz"),
            P("gx", "gy", "gz"),
            P("gx", "gy", "gz"),
            P(),
        ),
        out_specs=(wide, wide, wide),
        check_vma=False,
    )
```

time: 1830 us -> 108 us (0.06); the launches traced: 1800 us -> 108 us
  other arithmetic: 1320 us -> 0.01 us
  local copies, waits for them, and re-layouts: 207 us -> 0.79 us
  blocking collectives: 76.1 us -> 25.7 us
  starting transfers between devices: 90.5 us -> 40.7 us
  between operations: 47.1 us -> 0.82 us
  Pallas kernels: 0 us -> 39.8 us
  waiting for transfers between devices: 34.7 us -> 0.34 us
  matrix products: 32.4 us -> 0 us
    div x14 -> x0, other arithmetic: 662 us -> none  [the longest x6 659 us: lower_inverse(): solved_rows.append(current_row / lower[row_index, row_index])]
    sub x69 -> x0, other arithmetic: 623 us -> none  [the longest x68 621 us: lower_factor(): column = column - columns[inner] * columns[inner][col_index]]
    slice x178 -> x0, local copies, waits for them, and re-layouts: 151 us -> none  [the longest x64 39.9 us: lower_factor(): pivot_value = jnp.sqrt(column[col_index])]
    psum x1 -> x0, blocking collectives: 76.1 us -> none  [body(): gram = lax.psum(local_gram(blocks), ('gx', 'gy', 'gz'))]
    ppermute x30 -> x24, starting transfers between devices: 90.5 us -> 40.7 us  [exchange(): moved.append(lax.ppermute(source, axis, links))]
    pallas_call x0 -> x13, Pallas kernels: none -> 39.8 us  [the longest x5 9.95 us: gram(): pl.pallas_call(lambda *refs: gram_kernel(index, *refs), out_shape=(near(C...]
    ppermute x12 -> x0, local copies, waits for them, and re-layouts: 35.1 us -> none  [the longest x6 17.6 us: padded(): lax.ppermute(tail, axis, [(i, (i + 1) % count) for i in range(ends)])]
    ppermute x30 -> x24, waiting for transfers between devices: 34.7 us -> 0.34 us  [exchange(): moved.append(lax.ppermute(source, axis, links))]
  transfers between devices with their start and end apart: 30 -> 24, of which waited for: 14 -> 1; matrix products, arithmetic and copies ran while one was open for 2% -> 0% of each run, Pallas kernels for 0% -> 9%
where the time goes in v1:
time: 108 us
  starting transfers between devices  40.7 us (38%)
  Pallas kernels  39.8 us (37%)
  blocking collectives  25.7 us (24%)
    ppermute x24, starting transfers between devices, exchange(): moved.append(lax.ppermute(source, axis, links))  40.7 us
    all_to_all x1, blocking collectives, body(): parts = lax.all_to_all(piece, ('gx', 'gz'), 0, 0)  13.7 us
    all_to_all x1, blocking collectives, body(): packed = lax.all_to_all(parts, ('gy',), 0, 0)  12 us
    pallas_call x5, Pallas kernels, gram(): pl.pallas_call(lambda *refs: gram_kernel(index, *refs), out_shape=(near(C...  9.95 us
    pallas_call x3, Pallas kernels, body(): pl.pallas_call(lambda *refs, index=index: step_kernel(index, *refs), out_...  9.48 us
    pallas_call x1, Pallas kernels, body(): pl.pallas_call(finish_kernel, grid=(COMP,), out_shape=(shaped(total, NZ),...  8.72 us
    pallas_call x1, Pallas kernels, body(): pl.pallas_call(first_kernel, out_shape=[field] + side_outs + coef_shapes,...  5.32 us
    pallas_call x1, Pallas kernels, body(): pl.pallas_call(pack_kernel, out_shape=(field, face, face, face, face, fac...  4.38 us
  transfers between devices with their start and end apart: 24, of which 1 were waited for; matrix products, arithmetic and copies ran while one was open for 0% of the time, Pallas kernels for 9%

profile of v1, /device:TPU:1, one launch (start us, length us, event | category | flops | bytes accessed | tf_op | source)
XLA Modules:
  0.0 108.1 jit_solution(10276268166642457718)
XLA Ops:
  0.6 0.1 stack.27
  0.8 4.4 %pack.1 = (f32[4,8,8,8,128]{4,3,2,1,0:T(8,128)S(1)}, f32[37,8,128]{2,1,0:T(8,128)S(1)}, f32[37,8,128]{2,1,0:T(8,128)S(1)}, f32[37,8,128]{2,1,0:T(8,128)S(1)}, f3...) custom-call(s32[6]{0:T(128)S(1)} %convert_element_type.3.edge, ...), custom_call_target="tpu_custom_call" | custom-call | tf_op jit(solution)/shard_map/pack/pallas_call | solution.py:449
  5.1 2.1 %collective-permute-start = (f32[37,8,128]{2,1,0:T(8,128)S(1)}, f32[37,8,128]{2,1,0:T(8,128)S(1)}, u32[]{:S(2)}, u32[]{:S(2)}) collective-permute-start(f32[37,8,128]{2,1,0:T(8,128)S(1)} %get-tuple-element.53), channel_id=1, source_target_pairs={{0,64},{64,128},{128,192},{192,0},{1,65},{65,129},{129,193},{193,1... | collective-permute-start | bytes 454664 | tf_op jit(solution)/shard_map/ppermute | solution.py:434
  7.3 1.4 %collective-permute-start.1 = (f32[37,8,128]{2,1,0:T(8,128)S(1)}, f32[37,8,128]{2,1,0:T(8,128)S(1)}, u32[]{:S(2)}, u32[]{:S(2)}) collective-permute-start(f32[37,8,128]{2,1,0:T(8,128)S(1)} %get-tuple-element.54), channel_id=1, source_target_pairs={{64,0},{128,64},{192,128},{0,192},{65,1},{129,65},{193,129},{1,193... | collective-permute-start | bytes 454664 | tf_op jit(solution)/shard_map/ppermute | solution.py:434
  8.6 1.7 %collective-permute-start.2 = (f32[37,8,128]{2,1,0:T(8,128)S(1)}, f32[37,8,128]{2,1,0:T(8,128)S(1)}, u32[]{:S(2)}, u32[]{:S(2)}) collective-permute-start(f32[37,8,128]{2,1,0:T(8,128)S(1)} %get-tuple-element.55), channel_id=1, source_target_pairs={{0,8},{8,16},{16,24},{24,32},{32,40},{40,48},{48,56},{56,0},{1,9},... | collective-permute-start | bytes 454664 | tf_op jit(solution)/shard_map/ppermute | solution.py:434
  10.4 3.9 %collective-permute-start.3 = (f32[37,8,128]{2,1,0:T(8,128)S(1)}, f32[37,8,128]{2,1,0:T(8,128)S(1)}, u32[]{:S(2)}, u32[]{:S(2)}) collective-permute-start(f32[37,8,128]{2,1,0:T(8,128)S(1)} %get-tuple-element.56), channel_id=1, source_target_pairs={{8,0},{16,8},{24,16},{32,24},{40,32},{48,40},{56,48},{0,56},{9,1},... | collective-permute-start | bytes 454664 | tf_op jit(solution)/shard_map/ppermute | solution.py:434
  14.3 1.5 %collective-permute-start.5 = (f32[37,8,128]{2,1,0:T(8,128)S(1)}, f32[37,8,128]{2,1,0:T(8,128)S(1)}, u32[]{:S(2)}, u32[]{:S(2)}) collective-permute-start(f32[37,8,128]{2,1,0:T(8,128)S(1)} %get-tuple-element.57), channel_id=1, source_target_pairs={{1,0},{2,1},{3,2},{4,3},{5,4},{6,5},{7,6},{0,7},{9,8},{10,9},{11,1... | collective-permute-start | bytes 454664 | tf_op jit(solution)/shard_map/ppermute | solution.py:434
  15.8 0.0 collective-permute-done.refs_0_
  15.8 1.2 %collective-permute-start.4 = (f32[37,8,128]{2,1,0:T(8,128)S(1)}, f32[37,8,128]{2,1,0:T(8,128)S(1)}, u32[]{:S(2)}, u32[]{:S(2)}) collective-permute-start(f32[37,8,128]{2,1,0:T(8,128)S(1)} %get-tuple-element.57), channel_id=1, source_target_pairs={{0,1},{1,2},{2,3},{3,4},{4,5},{5,6},{6,7},{7,0},{8,9},{9,10},{10,1... | collective-permute-start | bytes 454664 | tf_op jit(solution)/shard_map/ppermute | solution.py:434
  17.0 0.7 copy-done
  17.7 1.9 %prepare.1 = (f32[2048,128]{1,0:T(8,128)S(1)}, f32[6,8,8,128]{3,2,1,0:T(8,128)S(1)}, f32[4,8,8,128]{3,2,1,0:T(8,128)S(1)}) custom-call(f32[3,6]{1,0:T(4,128)S(1)} %copy-done, f32[5,8,8,128]{3,2,1,0:T(8,128)S(1)} %get-tuple-element.50.pm.inner, f32[2048,128]{1,0:T(8,128)} %bitcast.12, f32[4,8,8,128]{3,2,1,0:T(8,128)} %store_hbm.1, s32[8,8,128]{2,1,0:T(8,128)} %label_hbm.1), custom_call_target="tpu_custom_call" | custom-call | tf_op jit(solution)/shard_map/prepare/pallas_call | solution.py:484
  19.6 1.4 %gram0.1 = (bf16[4,8,8,16,128]{4,3,2,1,0:T(8,128)(2,1)S(1)}, f32[8,128]{1,0:T(8,128)S(1)}) custom-call(f32[4,8,8,8,128]{4,3,2,1,0:T(8,128)S(1)} %get-tuple-element.48.refs_0_.cur.v0), custom_call_target="tpu_custom_call" | custom-call | flops 16777216 | bytes 3145728 | tf_op jit(solution)/shard_map/gram0/pallas_call | solution.py:467
  21.0 0.0 collective-permute-done.1.refs_1_
  21.0 0.0 collective-permute-done.2.refs_2_
  21.0 0.0 collective-permute-done.3.refs_3_
  21.0 0.0 collective-permute-done.5.refs_5_
  21.1 0.0 collective-permute-done.4.refs_4_
  21.1 5.3 %step1.1 = (f32[4,8,8,8,128]{4,3,2,1,0:T(8,128)S(1)}, f32[32,8,128]{2,1,0:T(8,128)S(1)}, f32[32,8,128]{2,1,0:T(8,128)S(1)}, f32[32,8,128]{2,1,0:T(8,128)S(1)}, f...) custom-call(s32[6]{0:T(128)S(1)} %convert_element_type.3.edge, ...), custom_call_target="tpu_custom_call" | custom-call | tf_op jit(solution)/shard_map/step1/pallas_call | solution.py:504
  26.4 0.1 collective-permute-start.6
  26.5 2.7 %collective-permute-start.7 = (f32[32,8,128]{2,1,0:T(8,128)S(1)}, f32[32,8,128]{2,1,0:T(8,128)S(1)}, u32[]{:S(2)}, u32[]{:S(2)}) collective-permute-start(f32[32,8,128]{2,1,0:T(8,128)S(1)} %get-tuple-element.62), channel_id=1, source_target_pairs={{64,0},{128,64},{192,128},{0,192},{65,1},{129,65},{193,129},{1,193... | collective-permute-start | bytes 393224 | tf_op jit(solution)/shard_map/ppermute | solution.py:434
  29.1 0.0 collective-permute-start.8
  29.1 3.4 %collective-permute-start.9 = (f32[32,8,128]{2,1,0:T(8,128)S(1)}, f32[32,8,128]{2,1,0:T(8,128)S(1)}, u32[]{:S(2)}, u32[]{:S(2)}) collective-permute-start(f32[32,8,128]{2,1,0:T(8,128)S(1)} %get-tuple-element.64), channel_id=1, source_target_pairs={{8,0},{16,8},{24,16},{32,24},{40,32},{48,40},{56,48},{0,56},{9,1},... | collective-permute-start | bytes 393224 | tf_op jit(solution)/shard_map/ppermute | solution.py:434
  32.5 2.6 %collective-permute-start.11 = (f32[32,8,128]{2,1,0:T(8,128)S(1)}, f32[32,8,128]{2,1,0:T(8,128)S(1)}, u32[]{:S(2)}, u32[]{:S(2)}) collective-permute-start(f32[32,8,128]{2,1,0:T(8,128)S(1)} %get-tuple-element.65), channel_id=1, source_target_pairs={{1,0},{2,1},{3,2},{4,3},{5,4},{6,5},{7,6},{0,7},{9,8},{10,9},{11,1... | collective-permute-start | bytes 393224 | tf_op jit(solution)/shard_map/ppermute | solution.py:434
  35.1 0.0 collective-permute-done.6.refs_2_
  35.1 0.0 collective-permute-start.10
  35.1 1.8 %gram1.1 = (bf16[4,8,8,16,128]{4,3,2,1,0:T(8,128)(2,1)S(1)}, f32[8,128]{1,0:T(8,128)S(1)}) custom-call(f32[4,8,8,8,128]{4,3,2,1,0:T(8,128)S(1)} %get-tuple-element.58.refs_0_.refs_1_, bf16[4,8,8,16,128]{4,3,2,1,0:T(8,128)(2,1)S(1)} %get-tuple-element.59.refs_1_.s0, f32[8,128]{1,0:T(8,128)S(1)} %get-tuple-element.49.piece.refs_2_), custom_call_target="tpu_custom_call" | custom-call | flops 33554432 | bytes 4194304 | tf_op jit(solution)/shard_map/gram1/pallas_call | solution.py:467
  36.9 0.0 collective-permute-done.7.refs_3_
  36.9 0.0 collective-permute-done.8.refs_4_
  36.9 0.0 collective-permute-done.9.refs_5_
  36.9 0.3 collective-permute-done.11.refs_7_
  37.2 0.0 collective-permute-done.10.refs_6_
  37.2 3.5 %step2.1 = (f32[4,8,8,8,128]{4,3,2,1,0:T(8,128)S(1)}, f32[32,8,128]{2,1,0:T(8,128)S(1)}, f32[32,8,128]{2,1,0:T(8,128)S(1)}, f32[32,8,128]{2,1,0:T(8,128)S(1)}, f...) custom-call(f32[8,128]{1,0:T(8,128)S(1)} %get-tuple-element.60.refs_0_.refs_3_, ...), custom_call_target="tpu_custom_call" | custom-call | tf_op jit(solution)/shard_map/step2/pallas_call | solution.py:519
  40.7 0.0 collective-permute-start.12
  40.7 2.7 %collective-permute-start.13 = (f32[32,8,128]{2,1,0:T(8,128)S(1)}, f32[32,8,128]{2,1,0:T(8,128)S(1)}, u32[]{:S(2)}, u32[]{:S(2)}) collective-permute-start(f32[32,8,128]{2,1,0:T(8,128)S(1)} %get-tuple-element.74), channel_id=1, source_target_pairs={{64,0},{128,64},{192,128},{0,192},{65,1},{129,65},{193,129},{1,193... | collective-permute-start | bytes 393224 | tf_op jit(solution)/shard_map/ppermute | solution.py:434
  43.4 0.0 collective-permute-start.14
  43.4 2.7 %collective-permute-start.15 = (f32[32,8,128]{2,1,0:T(8,128)S(1)}, f32[32,8,128]{2,1,0:T(8,128)S(1)}, u32[]{:S(2)}, u32[]{:S(2)}) collective-permute-start(f32[32,8,128]{2,1,0:T(8,128)S(1)} %get-tuple-element.76), channel_id=1, source_target_pairs={{8,0},{16,8},{24,16},{32,24},{40,32},{48,40},{56,48},{0,56},{9,1},... | collective-permute-start | bytes 393224 | tf_op jit(solution)/shard_map/ppermute | solution.py:434
  46.1 4.7 %collective-permute-start.17 = (f32[32,8,128]{2,1,0:T(8,128)S(1)}, f32[32,8,128]{2,1,0:T(8,128)S(1)}, u32[]{:S(2)}, u32[]{:S(2)}) collective-permute-start(f32[32,8,128]{2,1,0:T(8,128)S(1)} %get-tuple-element.77), channel_id=1, source_target_pairs={{1,0},{2,1},{3,2},{4,3},{5,4},{6,5},{7,6},{0,7},{9,8},{10,9},{11,1... | collective-permute-start | bytes 393224 | tf_op jit(solution)/shard_map/ppermute | solution.py:434
  50.8 0.0 collective-permute-done.12.refs_2_
  50.8 0.0 collective-permute-start.16
  50.8 2.1 %gram2.1 = (bf16[4,8,8,16,128]{4,3,2,1,0:T(8,128)(2,1)S(1)}, f32[8,128]{1,0:T(8,128)S(1)}) custom-call(f32[4,8,8,8,128]{4,3,2,1,0:T(8,128)S(1)} %get-tuple-element.70.refs_0_.refs_1_, bf16[4,8,8,16,128]{4,3,2,1,0:T(8,128)(2,1)S(1)} %get-tuple-element.59.refs_1_.s0, bf16[4,8,8,16,128]{4,3,2,1,0:T(8,128)(2,1)S(1)} %get-tuple-element.71.refs_2_.s1, ...), custom_call_target="tpu_custom_call" | custom-call | flops 50331648 | bytes 5242880 | tf_op jit(solution)/shard_map/gram2/pallas_call | solution.py:467
  52.9 0.0 collective-permute-done.13.refs_3_
  52.9 0.0 collective-permute-done.14.refs_4_
  52.9 0.0 collective-permute-done.15.refs_5_
  52.9 0.0 collective-permute-done.17.refs_7_
  52.9 0.0 collective-permute-done.16.refs_6_
  52.9 3.5 %step3.1 = (f32[4,8,8,8,128]{4,3,2,1,0:T(8,128)S(1)}, f32[32,8,128]{2,1,0:T(8,128)S(1)}, f32[32,8,128]{2,1,0:T(8,128)S(1)}, f32[32,8,128]{2,1,0:T(8,128)S(1)}, f...) custom-call(f32[8,128]{1,0:T(8,128)S(1)} %get-tuple-element.72.refs_0_.refs_4_, ...), custom_call_target="tpu_custom_call" | custom-call | tf_op jit(solution)/shard_map/step3/pallas_call | solution.py:519
  56.5 0.0 collective-permute-start.18
  56.5 2.7 %collective-permute-start.19 = (f32[32,8,128]{2,1,0:T(8,128)S(1)}, f32[32,8,128]{2,1,0:T(8,128)S(1)}, u32[]{:S(2)}, u32[]{:S(2)}) collective-permute-start(f32[32,8,128]{2,1,0:T(8,128)S(1)} %get-tuple-element.82), channel_id=1, source_target_pairs={{64,0},{128,64},{192,128},{0,192},{65,1},{129,65},{193,129},{1,193... | collective-permute-start | bytes 393224 | tf_op jit(solution)/shard_map/ppermute | solution.py:434
  59.2 0.0 collective-permute-start.20
  59.2 2.7 %collective-permute-start.21 = (f32[32,8,128]{2,1,0:T(8,128)S(1)}, f32[32,8,128]{2,1,0:T(8,128)S(1)}, u32[]{:S(2)}, u32[]{:S(2)}) collective-permute-start(f32[32,8,128]{2,1,0:T(8,128)S(1)} %get-tuple-element.84), channel_id=1, source_target_pairs={{8,0},{16,8},{24,16},{32,24},{40,32},{48,40},{56,48},{0,56},{9,1},... | collective-permute-start | bytes 393224 | tf_op jit(solution)/shard_map/ppermute | solution.py:434
  61.8 4.6 %collective-permute-start.23 = (f32[32,8,128]{2,1,0:T(8,128)S(1)}, f32[32,8,128]{2,1,0:T(8,128)S(1)}, u32[]{:S(2)}, u32[]{:S(2)}) collective-permute-start(f32[32,8,128]{2,1,0:T(8,128)S(1)} %get-tuple-element.85), channel_id=1, source_target_pairs={{1,0},{2,1},{3,2},{4,3},{5,4},{6,5},{7,6},{0,7},{9,8},{10,9},{11,1... | collective-permute-start | bytes 393224 | tf_op jit(solution)/shard_map/ppermute | solution.py:434
  66.5 0.0 collective-permute-done.18.refs_2_
  66.5 0.0 collective-permute-start.22
  66.5 2.3 %gram3.1 = (bf16[4,8,8,16,128]{4,3,2,1,0:T(8,128)(2,1)S(1)}, f32[8,128]{1,0:T(8,128)S(1)}) custom-call(f32[4,8,8,8,128]{4,3,2,1,0:T(8,128)S(1)} %get-tuple-element.78.refs_0_.refs_1_, bf16[4,8,8,16,128]{4,3,2,1,0:T(8,128)(2,1)S(1)} %get-tuple-element.59.refs_1_.s0, bf16[4,8,8,16,128]{4,3,2,1,0:T(8,128)(2,1)S(1)} %get-tuple-element.71.refs_2_.s1, ...), custom_call_target="tpu_custom_call" | custom-call | flops 67108864 | bytes 6291456 | tf_op jit(solution)/shard_map/gram3/pallas_call | solution.py:467
  68.8 0.0 collective-permute-done.19.refs_3_
  68.8 0.0 collective-permute-done.20.refs_4_
  68.8 0.0 collective-permute-done.21.refs_5_
  68.8 0.0 collective-permute-done.23.refs_7_
  68.8 0.0 collective-permute-done.22.refs_6_
  68.9 2.4 %step4.1.refs_0_ = f32[4,8,8,8,128]{4,3,2,1,0:T(8,128)S(1)} custom-call(f32[8,128]{1,0:T(8,128)S(1)} %get-tuple-element.80.refs_0_.refs_5_, f32[4,8,8,8,128]{4,3,2,1,0:T(8,128)S(1)} %get-tuple-element.78.refs_0_.refs_1_, f32[32,8,128]{2,1,0:T(8,128)S(1)} %collective-permute-done.18.refs_2_, f32[32,8,128]{2,1,0:T(8,128)S(1)} %collective-permute-done.19.refs_3_, ...), custom_call_target="tpu_custom_call" | custom-call | tf_op jit(solution)/shard_map/step4/pallas_call | solution.py:519
  71.3 2.4 %gram4.1 = (bf16[4,8,8,16,128]{4,3,2,1,0:T(8,128)(2,1)S(1)}, f32[32,8,128]{2,1,0:T(8,128)S(1)}) custom-call(f32[4,8,8,8,128]{4,3,2,1,0:T(8,128)S(1)} %step4.1.refs_0_, bf16[4,8,8,16,128]{4,3,2,1,0:T(8,128)(2,1)S(1)} %get-tuple-element.59.refs_1_.s0, bf16[4,8,8,16,128]{4,3,2,1,0:T(8,128)(2,1)S(1)} %get-tuple-element.71.refs_2_.s1, ...), custom_call_target="tpu_custom_call" | custom-call | flops 83886080 | bytes 7340032 | tf_op jit(solution)/shard_map/gram4/pallas_call | solution.py:467
  73.7 13.7 %all_to_all.10.parts = f32[32,8,128]{2,1,0:T(8,128)S(1)} all-to-all(f32[32,8,128]{2,1,0:T(8,128)S(1)} %get-tuple-element.87), channel_id=1, replica_groups=mesh['gx'=4,'gy'=8,'gz'=8] {'gx','gz'}, dimensions={0} | all-to-all | bytes 262144 | tf_op jit(solution)/shard_map/all_to_all | solution.py:531
  87.4 12.0 %all_to_all.11.packed = f32[8,8,128]{2,1,0:T(8,128)S(1)} all-to-all(f32[8,8,128]{2,1,0:T(8,128)S(1)} %relay.1), channel_id=1, replica_groups=mesh['gx'=4,'gy'=8,'gz'=8] {'gy'}, dimensions={0} | all-to-all | bytes 65536 | tf_op jit(solution)/shard_map/all_to_all | solution.py:540
  99.4 8.7 %finish.1 = (f32[2048,128]{1,0:T(8,128)}, f32[2048,128]{1,0:T(8,128)}, f32[8192,128]{1,0:T(8,128)}) custom-call(f32[8,8,128]{2,1,0:T(8,128)S(1)} %all_to_all.11.packed, bf16[4,8,8,16,128]{4,3,2,1,0:T(8,128)(2,1)S(1)} %get-tuple-element.59.refs_1_.s0, bf16[4,8,8,16,128]{4,3,2,1,0:T(8,128)(2,1)S(1)} %get-tuple-element.71.refs_2_.s1, ...), custom_call_target="tpu_custom_call" | custom-call | tf_op jit(solution)/shard_map/finish/pallas_call | solution.py:542
  (3 shorter events, 0.0 us)
Async XLA Ops:
  5.1 10.7 %collective-permute-start = (f32[37,8,128]{2,1,0:T(8,128)S(1)}, f32[37,8,128]{2,1,0:T(8,128)S(1)}, u32[]{:S(2)}, u32[]{:S(2)}) collective-permute-start(f32[37,8,128]{2,1,0:T(8,128)S(1)} %get-tuple-element.53), channel_id=1, source_target_pairs={{0,64},{64,128},{128,192},{192,0},{1,65},{65,129},{129,193},{193,1... | collective-permute-start | bytes 454664 | tf_op jit(solution)/shard_map/ppermute | solution.py:434
  7.3 13.8 %collective-permute-start.1 = (f32[37,8,128]{2,1,0:T(8,128)S(1)}, f32[37,8,128]{2,1,0:T(8,128)S(1)}, u32[]{:S(2)}, u32[]{:S(2)}) collective-permute-start(f32[37,8,128]{2,1,0:T(8,128)S(1)} %get-tuple-element.54), channel_id=1, source_target_pairs={{64,0},{128,64},{192,128},{0,192},{65,1},{129,65},{193,129},{1,193... | collective-permute-start | bytes 454664 | tf_op jit(solution)/shard_map/ppermute | solution.py:434
  8.6 12.4 %collective-permute-start.2 = (f32[37,8,128]{2,1,0:T(8,128)S(1)}, f32[37,8,128]{2,1,0:T(8,128)S(1)}, u32[]{:S(2)}, u32[]{:S(2)}) collective-permute-start(f32[37,8,128]{2,1,0:T(8,128)S(1)} %get-tuple-element.55), channel_id=1, source_target_pairs={{0,8},{8,16},{16,24},{24,32},{32,40},{40,48},{48,56},{56,0},{1,9},... | collective-permute-start | bytes 454664 | tf_op jit(solution)/shard_map/ppermute | solution.py:434
  10.4 10.7 %collective-permute-start.3 = (f32[37,8,128]{2,1,0:T(8,128)S(1)}, f32[37,8,128]{2,1,0:T(8,128)S(1)}, u32[]{:S(2)}, u32[]{:S(2)}) collective-permute-start(f32[37,8,128]{2,1,0:T(8,128)S(1)} %get-tuple-element.56), channel_id=1, source_target_pairs={{8,0},{16,8},{24,16},{32,24},{40,32},{48,40},{56,48},{0,56},{9,1},... | collective-permute-start | bytes 454664 | tf_op jit(solution)/shard_map/ppermute | solution.py:434
  14.3 6.7 %collective-permute-start.5 = (f32[37,8,128]{2,1,0:T(8,128)S(1)}, f32[37,8,128]{2,1,0:T(8,128)S(1)}, u32[]{:S(2)}, u32[]{:S(2)}) collective-permute-start(f32[37,8,128]{2,1,0:T(8,128)S(1)} %get-tuple-element.57), channel_id=1, source_target_pairs={{1,0},{2,1},{3,2},{4,3},{5,4},{6,5},{7,6},{0,7},{9,8},{10,9},{11,1... | collective-permute-start | bytes 454664 | tf_op jit(solution)/shard_map/ppermute | solution.py:434
  15.8 5.2 %collective-permute-start.4 = (f32[37,8,128]{2,1,0:T(8,128)S(1)}, f32[37,8,128]{2,1,0:T(8,128)S(1)}, u32[]{:S(2)}, u32[]{:S(2)}) collective-permute-start(f32[37,8,128]{2,1,0:T(8,128)S(1)} %get-tuple-element.57), channel_id=1, source_target_pairs={{0,1},{1,2},{2,3},{3,4},{4,5},{5,6},{6,7},{7,0},{8,9},{9,10},{10,1... | collective-permute-start | bytes 454664 | tf_op jit(solution)/shard_map/ppermute | solution.py:434
  17.0 0.7 copy-start
  26.4 8.7 %collective-permute-start.6 = (f32[32,8,128]{2,1,0:T(8,128)S(1)}, f32[32,8,128]{2,1,0:T(8,128)S(1)}, u32[]{:S(2)}, u32[]{:S(2)}) collective-permute-start(f32[32,8,128]{2,1,0:T(8,128)S(1)} %get-tuple-element.61), channel_id=1, source_target_pairs={{0,64},{64,128},{128,192},{192,0},{1,65},{65,129},{129,193},{193,1... | collective-permute-start | bytes 393224 | tf_op jit(solution)/shard_map/ppermute | solution.py:434
  26.5 10.4 %collective-permute-start.7 = (f32[32,8,128]{2,1,0:T(8,128)S(1)}, f32[32,8,128]{2,1,0:T(8,128)S(1)}, u32[]{:S(2)}, u32[]{:S(2)}) collective-permute-start(f32[32,8,128]{2,1,0:T(8,128)S(1)} %get-tuple-element.62), channel_id=1, source_target_pairs={{64,0},{128,64},{192,128},{0,192},{65,1},{129,65},{193,129},{1,193... | collective-permute-start | bytes 393224 | tf_op jit(solution)/shard_map/ppermute | solution.py:434
  29.1 7.8 %collective-permute-start.8 = (f32[32,8,128]{2,1,0:T(8,128)S(1)}, f32[32,8,128]{2,1,0:T(8,128)S(1)}, u32[]{:S(2)}, u32[]{:S(2)}) collective-permute-start(f32[32,8,128]{2,1,0:T(8,128)S(1)} %get-tuple-element.63), channel_id=1, source_target_pairs={{0,8},{8,16},{16,24},{24,32},{32,40},{40,48},{48,56},{56,0},{1,9},... | collective-permute-start | bytes 393224 | tf_op jit(solution)/shard_map/ppermute | solution.py:434
  29.1 7.8 %collective-permute-start.9 = (f32[32,8,128]{2,1,0:T(8,128)S(1)}, f32[32,8,128]{2,1,0:T(8,128)S(1)}, u32[]{:S(2)}, u32[]{:S(2)}) collective-permute-start(f32[32,8,128]{2,1,0:T(8,128)S(1)} %get-tuple-element.64), channel_id=1, source_target_pairs={{8,0},{16,8},{24,16},{32,24},{40,32},{48,40},{56,48},{0,56},{9,1},... | collective-permute-start | bytes 393224 | tf_op jit(solution)/shard_map/ppermute | solution.py:434
  32.5 4.7 %collective-permute-start.11 = (f32[32,8,128]{2,1,0:T(8,128)S(1)}, f32[32,8,128]{2,1,0:T(8,128)S(1)}, u32[]{:S(2)}, u32[]{:S(2)}) collective-permute-start(f32[32,8,128]{2,1,0:T(8,128)S(1)} %get-tuple-element.65), channel_id=1, source_target_pairs={{1,0},{2,1},{3,2},{4,3},{5,4},{6,5},{7,6},{0,7},{9,8},{10,9},{11,1... | collective-permute-start | bytes 393224 | tf_op jit(solution)/shard_map/ppermute | solution.py:434
  35.1 2.1 %collective-permute-start.10 = (f32[32,8,128]{2,1,0:T(8,128)S(1)}, f32[32,8,128]{2,1,0:T(8,128)S(1)}, u32[]{:S(2)}, u32[]{:S(2)}) collective-permute-start(f32[32,8,128]{2,1,0:T(8,128)S(1)} %get-tuple-element.65), channel_id=1, source_target_pairs={{0,1},{1,2},{2,3},{3,4},{4,5},{5,6},{6,7},{7,0},{8,9},{9,10},{10,1... | collective-permute-start | bytes 393224 | tf_op jit(solution)/shard_map/ppermute | solution.py:434
  40.7 10.1 %collective-permute-start.12 = (f32[32,8,128]{2,1,0:T(8,128)S(1)}, f32[32,8,128]{2,1,0:T(8,128)S(1)}, u32[]{:S(2)}, u32[]{:S(2)}) collective-permute-start(f32[32,8,128]{2,1,0:T(8,128)S(1)} %get-tuple-element.73), channel_id=1, source_target_pairs={{0,64},{64,128},{128,192},{192,0},{1,65},{65,129},{129,193},{193,1... | collective-permute-start | bytes 393224 | tf_op jit(solution)/shard_map/ppermute | solution.py:434
  40.7 12.2 %collective-permute-start.13 = (f32[32,8,128]{2,1,0:T(8,128)S(1)}, f32[32,8,128]{2,1,0:T(8,128)S(1)}, u32[]{:S(2)}, u32[]{:S(2)}) collective-permute-start(f32[32,8,128]{2,1,0:T(8,128)S(1)} %get-tuple-element.74), channel_id=1, source_target_pairs={{64,0},{128,64},{192,128},{0,192},{65,1},{129,65},{193,129},{1,193... | collective-permute-start | bytes 393224 | tf_op jit(solution)/shard_map/ppermute | solution.py:434
  43.4 9.5 %collective-permute-start.14 = (f32[32,8,128]{2,1,0:T(8,128)S(1)}, f32[32,8,128]{2,1,0:T(8,128)S(1)}, u32[]{:S(2)}, u32[]{:S(2)}) collective-permute-start(f32[32,8,128]{2,1,0:T(8,128)S(1)} %get-tuple-element.75), channel_id=1, source_target_pairs={{0,8},{8,16},{16,24},{24,32},{32,40},{40,48},{48,56},{56,0},{1,9},... | collective-permute-start | bytes 393224 | tf_op jit(solution)/shard_map/ppermute | solution.py:434
  43.4 9.5 %collective-permute-start.15 = (f32[32,8,128]{2,1,0:T(8,128)S(1)}, f32[32,8,128]{2,1,0:T(8,128)S(1)}, u32[]{:S(2)}, u32[]{:S(2)}) collective-permute-start(f32[32,8,128]{2,1,0:T(8,128)S(1)} %get-tuple-element.76), channel_id=1, source_target_pairs={{8,0},{16,8},{24,16},{32,24},{40,32},{48,40},{56,48},{0,56},{9,1},... | collective-permute-start | bytes 393224 | tf_op jit(solution)/shard_map/ppermute | solution.py:434
  46.1 6.8 %collective-permute-start.17 = (f32[32,8,128]{2,1,0:T(8,128)S(1)}, f32[32,8,128]{2,1,0:T(8,128)S(1)}, u32[]{:S(2)}, u32[]{:S(2)}) collective-permute-start(f32[32,8,128]{2,1,0:T(8,128)S(1)} %get-tuple-element.77), channel_id=1, source_target_pairs={{1,0},{2,1},{3,2},{4,3},{5,4},{6,5},{7,6},{0,7},{9,8},{10,9},{11,1... | collective-permute-start | bytes 393224 | tf_op jit(solution)/shard_map/ppermute | solution.py:434
  50.8 2.1 %collective-permute-start.16 = (f32[32,8,128]{2,1,0:T(8,128)S(1)}, f32[32,8,128]{2,1,0:T(8,128)S(1)}, u32[]{:S(2)}, u32[]{:S(2)}) collective-permute-start(f32[32,8,128]{2,1,0:T(8,128)S(1)} %get-tuple-element.77), channel_id=1, source_target_pairs={{0,1},{1,2},{2,3},{3,4},{4,5},{5,6},{6,7},{7,0},{8,9},{9,10},{10,1... | collective-permute-start | bytes 393224 | tf_op jit(solution)/shard_map/ppermute | solution.py:434
  56.5 10.0 %collective-permute-start.18 = (f32[32,8,128]{2,1,0:T(8,128)S(1)}, f32[32,8,128]{2,1,0:T(8,128)S(1)}, u32[]{:S(2)}, u32[]{:S(2)}) collective-permute-start(f32[32,8,128]{2,1,0:T(8,128)S(1)} %get-tuple-element.81), channel_id=1, source_target_pairs={{0,64},{64,128},{128,192},{192,0},{1,65},{65,129},{129,193},{193,1... | collective-permute-start | bytes 393224 | tf_op jit(solution)/shard_map/ppermute | solution.py:434
  56.5 12.3 %collective-permute-start.19 = (f32[32,8,128]{2,1,0:T(8,128)S(1)}, f32[32,8,128]{2,1,0:T(8,128)S(1)}, u32[]{:S(2)}, u32[]{:S(2)}) collective-permute-start(f32[32,8,128]{2,1,0:T(8,128)S(1)} %get-tuple-element.82), channel_id=1, source_target_pairs={{64,0},{128,64},{192,128},{0,192},{65,1},{129,65},{193,129},{1,193... | collective-permute-start | bytes 393224 | tf_op jit(solution)/shard_map/ppermute | solution.py:434
  59.2 9.6 %collective-permute-start.20 = (f32[32,8,128]{2,1,0:T(8,128)S(1)}, f32[32,8,128]{2,1,0:T(8,128)S(1)}, u32[]{:S(2)}, u32[]{:S(2)}) collective-permute-start(f32[32,8,128]{2,1,0:T(8,128)S(1)} %get-tuple-element.83), channel_id=1, source_target_pairs={{0,8},{8,16},{16,24},{24,32},{32,40},{40,48},{48,56},{56,0},{1,9},... | collective-permute-start | bytes 393224 | tf_op jit(solution)/shard_map/ppermute | solution.py:434
  59.2 9.7 %collective-permute-start.21 = (f32[32,8,128]{2,1,0:T(8,128)S(1)}, f32[32,8,128]{2,1,0:T(8,128)S(1)}, u32[]{:S(2)}, u32[]{:S(2)}) collective-permute-start(f32[32,8,128]{2,1,0:T(8,128)S(1)} %get-tuple-element.84), channel_id=1, source_target_pairs={{8,0},{16,8},{24,16},{32,24},{40,32},{48,40},{56,48},{0,56},{9,1},... | collective-permute-start | bytes 393224 | tf_op jit(solution)/shard_map/ppermute | solution.py:434
  61.8 7.0 %collective-permute-start.23 = (f32[32,8,128]{2,1,0:T(8,128)S(1)}, f32[32,8,128]{2,1,0:T(8,128)S(1)}, u32[]{:S(2)}, u32[]{:S(2)}) collective-permute-start(f32[32,8,128]{2,1,0:T(8,128)S(1)} %get-tuple-element.85), channel_id=1, source_target_pairs={{1,0},{2,1},{3,2},{4,3},{5,4},{6,5},{7,6},{0,7},{9,8},{10,9},{11,1... | collective-permute-start | bytes 393224 | tf_op jit(solution)/shard_map/ppermute | solution.py:434
  66.5 2.4 %collective-permute-start.22 = (f32[32,8,128]{2,1,0:T(8,128)S(1)}, f32[32,8,128]{2,1,0:T(8,128)S(1)}, u32[]{:S(2)}, u32[]{:S(2)}) collective-permute-start(f32[32,8,128]{2,1,0:T(8,128)S(1)} %get-tuple-element.85), channel_id=1, source_target_pairs={{0,1},{1,2},{2,3},{3,4},{4,5},{5,6},{6,7},{7,0},{8,9},{9,10},{10,1... | collective-permute-start | bytes 393224 | tf_op jit(solution)/shard_map/ppermute | solution.py:434

commit v2 on v1

v2 whole, which is shorter than its diff:
```python
import jax
import jax.numpy as jnp
from jax import lax
from jax.experimental import pallas as pl
from jax.experimental.pallas import tpu as pltpu
from jax.sharding import PartitionSpec as P

COMP = 4
RHS = 8
S = 4
PAIRS = ((0, 1), (0, 2), (0, 3), (1, 2), (1, 3), (2, 3))
SHIFTS = (2.0, 14.0, 6.0, 10.0)
SCALE = 8.0
F32 = jnp.float32
BF16 = jnp.bfloat16

PITCH = 72
NX, NY, NZ = 8, 8, 128
FACE = COMP * 8
BLOCKS = tuple((a, b) for b in range(4) for a in range(b + 1)) + ((3, 4),)
VMEM = pl.BlockSpec(memory_space=pltpu.VMEM)
SMEM = pl.BlockSpec(memory_space=pltpu.SMEM)


def pair_index(a, b):
    return PAIRS.index((min(a, b), max(a, b)))


def lane_ids(shape):
    return lax.broadcasted_iota(jnp.int32, shape, len(shape) - 1)


def put_ends(acc, tile, lane, slot):
    return jnp.where((lane >> 1) == slot, pltpu.roll(tile, 2 * slot + 1, 1), acc)


def join(lines, lane):
    while len(lines) > 1:
        half = 128 // len(lines)
        lines = [
            jnp.where((lane & half) == 0, low, high) for low, high in zip(lines[::2], lines[1::2])
        ]
    return lines[0]


def fetch(pairs, sems):
    copies = [pltpu.make_async_copy(src, dst, sems.at[i]) for i, (src, dst) in enumerate(pairs)]
    for copy in copies:
        copy.start()
    return copies


def pack_kernel(edge, res_hbm, perm_hbm, mask_hbm, v0, xlo, xhi, ylo, yhi, ends, pm, res, mask, sems):
    lane = lane_ids((8, NZ))
    spaced = res.reshape(COMP * RHS, PITCH, NZ)
    spans = [pl.ds(RHS * c, RHS) for c in range(COMP)]
    copies = fetch(
        [(perm_hbm, pm.at[pl.ds(0, COMP)]), (mask_hbm, mask)]
        + [(res_hbm.at[span], spaced.at[span, pl.ds(0, NX * NY)]) for span in spans],
        sems,
    )
    copies[0].wait()
    copies[1].wait()

    for x in range(NX):
        pm[COMP, x] = mask[x].astype(F32)
    for f in range(5):
        acc = jnp.zeros((8, NZ), F32)
        for x in range(NX):
            tile = pm[f, x]
            ylo[FACE + f, x : x + 1, :] = tile[0:1]
            yhi[FACE + f, x : x + 1, :] = tile[7:8]
            acc = put_ends(acc, tile, lane, x)
        ends[COMP + f] = acc
    for f in range(5):
        xlo[FACE + f] = pm[f, 0]
        xhi[FACE + f] = pm[f, NX - 1]

    for c in range(COMP):
        copies[2 + c].wait()
        lines = []
        for x in range(NX):
            acc = jnp.zeros((8, NZ), F32)
            for y in range(NY):
                tile = res[pl.ds(c * RHS * PITCH + x * 8 + y, 8, stride=PITCH), :]
                v0[c, x, y] = tile
                acc = put_ends(acc, tile, lane, x * 8 + y)
                if y in (0, NY - 1):
                    (yhi if y else ylo)[c * 8 + x] = tile
                if x in (0, NX - 1):
                    (xhi if x else xlo)[c * 8 + y] = tile
            lines.append(acc)
        ends[c] = join(lines, lane)


def face(own, other, masks):
    return (-0.5 / SCALE) * (own + other) * masks


def prepare_kernel(table, pm, sol_hbm, store_hbm, label_hbm, sol, tx, ty, tz, diag, rate, label, sems):
    lane = lane_ids((8, NZ))
    sub = lax.broadcasted_iota(jnp.int32, (8, NZ), 0)
    copies = fetch([(store_hbm, diag), (label_hbm, label), (sol_hbm, sol)], sems)
    copies[0].wait()
    copies[1].wait()

    for x in range(NX):
        m = pm[COMP, x]
        kind = label[x]
        rates = []
        for q in range(6):
            value = jnp.where(kind == 0, table[0, q], jnp.where(kind == 1, table[1, q], table[2, q]))
            rates.append((1.0 / SCALE) * m * value)
            rate[q, x] = rates[q]
        below, above = max(x - 1, 0), min(x + 1, NX - 1)
        m_lo = m * pm[COMP, below] if x else jnp.zeros_like(m)
        m_hi = m * pm[COMP, above] if x < NX - 1 else jnp.zeros_like(m)

        def around(own):
            return [pltpu.roll(own, 1, 0), pltpu.roll(own, 7, 0), pltpu.roll(own, 1, 1), pltpu.roll(own, 127, 1)]

        outer = [sub == 0, sub == 7, lane == 0, lane == 127]
        masks = [jnp.where(edge, 0.0, m * n) for edge, n in zip(outer, around(m))]
        for c in range(COMP):
            own = pm[c, x]
            total = diag[c, x] * (1.0 / SCALE)
            for b in range(COMP):
                if b != c:
                    total = total + rates[pair_index(c, b)]
            tx[c, x] = x_lo = face(own, pm[c, below], m_lo)
            tx[COMP + c, x] = x_hi = face(own, pm[c, above], m_hi)
            sides = [face(own, n, mm) for n, mm in zip(around(own), masks)]
            ty[c, x], ty[COMP + c, x], tz[c, x], tz[COMP + c, x] = sides
            diag[c, x] = total - x_lo - x_hi - sides[0] - sides[1] - sides[2] - sides[3]
    copies[2].wait()


def local_kernel(index, cur, tx, ty, tz, diag, rate, out):
    shift = SHIFTS[index] / SCALE

    def loop(x, _):
        below, above = jnp.maximum(x - 1, 0), jnp.minimum(x + 1, NX - 1)
        low = None
        own = [cur[c, x, 0] for c in range(COMP)]
        for y in range(NY):
            row = pl.ds(y, 1)
            high = [cur[c, x, y + 1] for c in range(COMP)] if y < NY - 1 else None
            rates = [rate[q, x, row, :] for q in range(6)]
            for c in range(COMP):
                p = own[c]
                value = (diag[c, x, row, :] - shift) * p
                side = tx[c, x, row, :] * cur[c, below, y] + tx[COMP + c, x, row, :] * cur[c, above, y]
                if y:
                    value = value + ty[c, x, row, :] * low[c]
                if y < NY - 1:
                    side = side + ty[COMP + c, x, row, :] * high[c]
                value = value + tz[c, x, row, :] * pltpu.roll(p, 1, 1)
                side = side + tz[COMP + c, x, row, :] * pltpu.roll(p, 127, 1)
                others = [b for b in range(COMP) if b != c]
                flow = rates[pair_index(c, others[0])] * own[others[0]]
                for b in others[1:]:
                    flow = flow + rates[pair_index(c, b)] * own[b]
                out[c, x, y] = (value + side) - flow
            low, own = own, high
        return 0

    lax.fori_loop(0, NX, loop, 0)


def ghost_tile(place, first, second, lane):
    return jnp.where(((lane + place[6]) & 1) == 0, second, first)


def edge_kernel(place, inner, halo, bx, by, bz):
    xl, xh, yl, yh, z0, z1 = halo
    lane = lane_ids((8, NZ))
    keep = [place[i].astype(F32) for i in range(6)]
    tiles = [ghost_tile(place, z0[COMP + f], z1[COMP + f], lane) for f in range(5)]
    tiles[4] = tiles[4] * jnp.where((lane & 1) == 0, keep[4], keep[5])
    for side, (halo_x, halo_y) in enumerate(((xl, yl), (xh, yh))):
        x = side * (NX - 1)
        mask = inner[COMP, x] * halo_x[FACE + COMP] * keep[side]
        for c in range(COMP):
            bx[side, c] = face(inner[c, x], halo_x[FACE + c], mask)

    for x in range(NX):
        row = pl.ds(x, 1)
        for side, halo_y in enumerate((yl, yh)):
            own = pl.ds(side * (NY - 1), 1)
            mask = inner[COMP, x, own, :] * halo_y[FACE + COMP, row, :] * keep[2 + side]
            for c in range(COMP):
                by[side, c, row, :] = face(inner[c, x, own, :], halo_y[FACE + c, row, :], mask)
        near_x = [pltpu.roll(t, (128 - 2 * x) & 127, 1) for t in tiles]
        ghosts = [jnp.where(lane == 0, t, pltpu.roll(t, 126, 1)) for t in near_x]
        mask = jnp.where((lane == 0) | (lane == 127), inner[COMP, x] * ghosts[4], 0.0)
        for c in range(COMP):
            bz[c, x] = face(inner[c, x], ghosts[c], mask)


def close_step(place, part, cur, halo, bx, by, bz, out, sends):
    xl, xh, yl, yh, z0, z1 = halo
    lane = lane_ids((8, NZ))
    ghosts, lines = [], [[] for _ in range(COMP)]
    for c in range(COMP):
        tile = ghost_tile(place, z0[c], z1[c], lane)
        ghosts.append(jnp.where((lane & 1) == 0, pltpu.roll(tile, 127, 1), pltpu.roll(tile, 1, 1)))
    for x in range(NX):
        accs = [jnp.zeros((8, NZ), F32) for _ in range(COMP)]
        for y in range(NY):
            slot = x * 8 + y
            for c in range(COMP):
                p = cur[c, x, y]
                g = pltpu.roll(ghosts[c], (127 - 2 * slot) & 127, 1)
                value = part[c, x, y] + bz[c, x, pl.ds(y, 1), :] * (g - p)
                if y in (0, NY - 1):
                    side = 1 if y else 0
                    other = (yl, yh)[side][c * 8 + x]
                    value = value + by[side, c, pl.ds(x, 1), :] * (other - p)
                if x in (0, NX - 1):
                    side = 1 if x else 0
                    other = (xl, xh)[side][c * 8 + y]
                    value = value + bx[side, c, pl.ds(y, 1), :] * (other - p)
                out[c, x, y] = value
                if sends is not None:
                    accs[c] = put_ends(accs[c], value, lane, slot)
                    if y in (0, NY - 1):
                        sends[2 + (1 if y else 0)][c * 8 + x] = value
                    if x in (0, NX - 1):
                        sends[1 if x else 0][c * 8 + y] = value
        for c in range(COMP):
            lines[c].append(accs[c])
    if sends is not None:
        for c in range(COMP):
            sends[4][c] = join(lines[c], lane)


def first_kernel(place, part, cur, inner, *refs):
    halo, refs = refs[:6], refs[6:]
    out, sends, faces = refs[0], refs[1:6], refs[6:9]
    edge_kernel(place, inner, halo, *faces)
    close_step(place, part, cur, halo, *faces, out, sends)


def step_kernel(place, piece, part, cur, *refs):
    halo, faces, refs = refs[:6], refs[6:9], refs[9:]
    out, sends = refs[0], refs[1:] or None
    close_step(place, part, cur, halo, *faces, out, sends)


def gram_kernel(index, cur, *refs):
    others = [a for a, b in BLOCKS if b == index]
    count = len(others)
    older, refs = refs[: count - (index < S)], refs[count - (index < S) :]
    before = None
    if index:
        before, refs = refs[0], refs[1:]
    split, out = refs
    lane = lane_ids((8, NZ))
    tall = 16 * count

    def loop(x, total):
        tiles = []
        for c in range(COMP):
            for y in range(NY):
                v = cur[c, x, y]
                high = v.astype(BF16).astype(F32)
                tile = jnp.concatenate([high, v - high], 0).astype(BF16)
                split[c, x, y] = tile
                tiles.append(tile)
        right = jnp.concatenate(tiles, 1)
        lefts = [
            jnp.concatenate([old[c, x, y] for c in range(COMP) for y in range(NY)], 1) for old in older
        ]
        if index < S:
            lefts.append(right)
        left = jnp.concatenate(lefts, 0) if len(lefts) > 1 else lefts[0]
        return total + lax.dot_general(
            left, right, (((1,), (1,)), ((), ())), preferred_element_type=F32
        )

    total = lax.fori_loop(0, NX, loop, jnp.zeros((tall, 16), F32))
    wide = jnp.concatenate([total, jnp.zeros((tall, NZ - 16), F32)], 1)
    value = jnp.zeros((8, NZ), F32)
    for number, a in enumerate(others):
        top = 16 * number
        both = wide[top : top + 8] + wide[top + 8 : top + 16]
        both = both + pltpu.roll(both, NZ - 8, 1)
        slot = BLOCKS.index((a, index))
        value = jnp.where((lane >> 3) == slot, pltpu.roll(both, 8 * slot, 1), value)
    if index:
        value = value + before[...]
    if index < S:
        out[...] = value
    else:
        for copy in range(out.shape[0]):
            out[copy] = value


def relay_kernel(parts, out):
    total = parts[0]
    for i in range(1, parts.shape[0]):
        total = total + parts[i]
    for copy in range(out.shape[0]):
        out[copy] = total


def lane_group(tile, source, target):
    return pltpu.roll(tile, (8 * (target - source)) % NZ, 1)


def factor(packed, weight):
    lane8 = lane_ids((8, NZ)) >> 3
    turned = jnp.transpose(jnp.concatenate([packed, jnp.zeros((NZ - 8, NZ), F32)], 0))
    rows = []
    for a in range(S):
        line = jnp.zeros((8, NZ), F32)
        for b in range(S + 1):
            if b == S and a < S - 1:
                block = lane_group(packed, BLOCKS.index((a + 1, 3)), b)
                block = block + (SHIFTS[a] - SHIFTS[3]) / SCALE * lane_group(
                    packed, BLOCKS.index((a, 3)), b
                )
            elif a <= b:
                block = lane_group(packed, BLOCKS.index((a, b)), b)
            else:
                slot = BLOCKS.index((b, a))
                block = lane_group(turned[8 * slot : 8 * slot + 8], 0, b)
            if a == b:
                slot = BLOCKS.index((a, a))
                other = lane_group(turned[8 * slot : 8 * slot + 8], 0, b)
                block = 0.5 * (block + other)
            line = jnp.where(lane8 == b, block, line)
        rows.append(line)
    gram = jnp.concatenate(rows, 0)
    lane = lane_ids((32, NZ))
    row = lax.broadcasted_iota(jnp.int32, (32, NZ), 0)
    group = lane >> 3
    sigma = jnp.where(
        group == 0, SHIFTS[0], jnp.where(group == 1, SHIFTS[1], jnp.where(group == 2, SHIFTS[2], SHIFTS[3]))
    )
    moment = jnp.where(lane < 32, sigma * gram + SCALE * pltpu.roll(gram, NZ - 8, 1), 0.0)
    flipped = jnp.transpose(jnp.concatenate([moment, jnp.zeros((NZ - 32, NZ), F32)], 0))[:32]
    moment = 0.5 * (moment + flipped)
    left = jnp.where(lane < 32, gram, jnp.where(lane == row + 32, 1.0, 0.0))
    right = jnp.where(lane < 32, moment, jnp.where(group == 4, pltpu.roll(gram, 32, 1), 0.0))
    inverse = jnp.zeros((32, NZ), F32)
    for j in range(0, 32, 2):
        kept = []
        for matrix in (left, right):
            c0 = jnp.broadcast_to(matrix[:, j : j + 1], (32, NZ))
            c1 = jnp.broadcast_to(matrix[:, j + 1 : j + 2], (32, NZ))
            r0, r1 = matrix[j : j + 1], matrix[j + 1 : j + 2]
            p, q, r = c0[j : j + 1], c1[j : j + 1], c1[j + 1 : j + 2]
            inv = 1.0 / (p * r - q * q)
            n0, n1 = (r * r0 - q * r1) * inv, (p * r1 - q * r0) * inv
            kept.append((matrix - c0 * n0 - c1 * n1, r0, r1, p, q, r, n0, n1))
        left, r0, r1, p, q, r, _, _ = kept[0]
        ratio = q / p
        inverse = jnp.where(row == j, r0 * lax.rsqrt(p), inverse)
        inverse = jnp.where(row == j + 1, (r1 - ratio * r0) * lax.rsqrt(r - q * ratio), inverse)
        right, n0, n1 = kept[1][0], kept[1][6], kept[1][7]
        right = jnp.where(row == j, n0, jnp.where(row == j + 1, n1, right))
    inverse = pltpu.roll(inverse, NZ - 32, 1)
    coeff = pltpu.roll(right, NZ - 32, 1)
    coeff = jnp.transpose(jnp.concatenate([coeff, jnp.zeros((NZ - 32, NZ), F32)], 0))[:8]
    coeff = jnp.where(lane8 < S, coeff, 0.0)
    ext = SCALE * pltpu.roll(coeff, 8, 1)
    for k in range(S):
        ext = jnp.where(lane8 == k, ext + SHIFTS[k] * coeff, ext)
    full = jnp.concatenate([jnp.where(lane < 32, inverse, 0.0), coeff, ext], 0)
    lanes = lane_ids((48, NZ))
    spread = jnp.zeros((48, NZ), F32)
    for k in range(S + 1):
        for part in range(2):
            spread = jnp.where(
                (lanes >> 3) == 2 * k + part, pltpu.roll(full, (8 * (2 * k + part - k)) % NZ, 1), spread
            )
    high = spread.astype(BF16)
    low = (spread - high.astype(F32)).astype(BF16)
    weight[0:48] = high
    weight[48:96] = low


def finish_kernel(packed, s0, s1, s2, s3, s4, sol, v0, sol_hbm, res_hbm, basis_hbm, new_sol, new_res, basis, weight, sems):
    total = packed[0]
    for i in range(1, packed.shape[0]):
        total = total + packed[i]
    factor(total, weight)
    copies = []
    for c in range(COMP):
        for half in range(2):
            spots = [(4 * half + u, y) for u in range(4) for y in range(NY)]
            lines = [jnp.concatenate([s[c, x, y] for x, y in spots], 1) for s in (s0, s1, s2, s3, s4)]
            both = jnp.dot(weight[:, 0:80], jnp.concatenate(lines, 0), preferred_element_type=F32)
            both = both[0:48] + both[48:96]
            for number, (x, y) in enumerate(spots):
                place = x * 8 + y
                part = both[:, number * NZ : (number + 1) * NZ]
                for q in range(0, S * RHS, 8):
                    first = (c * S * RHS + q) * PITCH + place
                    basis[pl.ds(first, 8, stride=PITCH), :] = part[q : q + 8]
                spot = pl.ds(c * RHS * PITCH + place, 8, stride=PITCH)
                old = sol[pl.ds(c * RHS * NX * NY + place, 8, stride=NX * NY), :]
                new_sol[spot, :] = old + part[32:40]
                new_res[spot, :] = v0[c, x, y] - part[40:48]
        pieces = ((basis, basis_hbm, S * RHS), (new_sol, sol_hbm, RHS), (new_res, res_hbm, RHS))
        for number, (source, target, count) in enumerate(pieces):
            spaced = source.reshape(source.shape[0] // PITCH, PITCH, NZ)
            span = pl.ds(c * count, count)
            copies.append(
                pltpu.make_async_copy(
                    spaced.at[span, pl.ds(0, NX * NY)], target.at[span], sems.at[c, number]
                )
            )
            copies[-1].start()
    for copy in copies:
        copy.wait()


def shaped(*shape, dtype=F32):
    return jax.ShapeDtypeStruct(shape, dtype)


def near(*shape, dtype=F32):
    return pltpu.VMEM(shape, dtype)


def far(array):
    return pltpu.with_memory_space_constraint(array, pltpu.HBM)


def params(mib):
    return pltpu.CompilerParams(vmem_limit_bytes=mib << 20)


def exchange(sends):
    moved = []
    for number, (axis, up) in enumerate((("gx", 1), ("gx", 0), ("gy", 1), ("gy", 0))):
        count = lax.axis_size(axis)
        if up:
            links = [(i, (i + 1) % count) for i in range(count)]
        else:
            links = [((i + 1) % count, i) for i in range(count)]
        moved.append(lax.ppermute(sends[number + 1 if up else number - 1], axis, links))
    count = lax.axis_size("gz")
    moved.append(lax.ppermute(sends[4], "gz", [(i, i ^ 1) for i in range(count)]))
    links = [(i, (i + (1 if i % 2 else -1)) % count) for i in range(count)]
    moved.append(lax.ppermute(sends[4], "gz", links))
    return moved


def body(solution, residual, permeability, storage, tissue_mask, tissue_label, exchange_table):
    flat = residual.reshape(COMP * RHS, NX * NY, NZ)
    edge = []
    for axis in ("gx", "gy", "gz"):
        place = lax.axis_index(axis)
        edge += [place > 0, place < lax.axis_size(axis) - 1]
    edge.append(place % 2 == 1)
    edge = jnp.stack(edge).astype(jnp.int32)
    field = near(COMP, NX, NY, RHS, NZ)
    face = near(FACE + 5, 8, NZ)
    total = COMP * RHS * NX * NY
    in_hbm = pl.BlockSpec(memory_space=pltpu.HBM)
    v0, *sends, inner = pl.pallas_call(
        pack_kernel,
        out_shape=(field, face, face, face, face, face, near(5, NX, NY, NZ)),
        in_specs=[SMEM] + [in_hbm] * 3,
        out_specs=[VMEM] * 7,
        scratch_shapes=[
            pltpu.VMEM((COMP * RHS * PITCH, NZ), F32),
            pltpu.VMEM((NX, NY, NZ), jnp.int32),
            pltpu.SemaphoreType.DMA((2 + COMP,)),
        ],
        compiler_params=params(5),
        name="pack",
    )(edge, far(flat), far(permeability), far(tissue_mask))

    wide, tall = lax.axis_size("gx") * lax.axis_size("gz"), lax.axis_size("gy")

    def gram(index, current, older, before):
        inputs = [current, *(older if index < S else older[-1:]), *before]
        return pl.pallas_call(
            lambda *refs: gram_kernel(index, *refs),
            out_shape=(
                near(COMP, NX, NY, 16, NZ, dtype=BF16),
                near(8, NZ) if index < S else near(wide, 8, NZ),
            ),
            in_specs=[VMEM] * len(inputs),
            out_specs=[VMEM] * 2,
            compiler_params=params(5),
            cost_estimate=pl.CostEstimate(
                flops=2 * 16 * 16 * (index + 1) * 32768, bytes_accessed=(3 + index) << 20, transcendentals=0
            ),
            name=f"gram{index}",
        )(*inputs)

    halo = exchange(sends)
    splits = []
    plane = near(COMP, NX, NY, NZ)
    double = near(2 * COMP, NX, NY, NZ)
    sol, *coef = pl.pallas_call(
        prepare_kernel,
        out_shape=(near(total, NZ), double, double, double, plane, near(6, NX, NY, NZ)),
        in_specs=[SMEM, VMEM] + [in_hbm] * 3,
        out_specs=[VMEM] * 6,
        scratch_shapes=[pltpu.VMEM((NX, NY, NZ), jnp.int32), pltpu.SemaphoreType.DMA((3,))],
        compiler_params=params(5),
        name="prepare",
    )(exchange_table, inner, far(solution.reshape(total, NZ)), far(storage), far(tissue_label))

    def local(index, current):
        return pl.pallas_call(
            lambda *refs: local_kernel(index, *refs),
            out_shape=field,
            in_specs=[VMEM] * 6,
            out_specs=VMEM,
            compiler_params=params(5),
            cost_estimate=pl.CostEstimate(flops=6 << 20, bytes_accessed=3 << 20, transcendentals=0),
            name=f"local{index + 1}",
        )(current, *coef)

    part = local(0, v0)
    split, piece = gram(0, v0, [], [])
    splits.append(split)
    face = near(FACE, 8, NZ)
    results = pl.pallas_call(
        first_kernel,
        out_shape=[field] + [face] * 5 + [near(2, COMP, NY, NZ), near(2, COMP, NX, NZ), plane],
        in_specs=[SMEM] + [VMEM] * 9,
        out_specs=[VMEM] * 9,
        compiler_params=params(5),
        name="step1",
    )(edge, part, v0, inner, *halo)
    current, sends, faces = results[0], results[1:6], results[6:]
    for index in range(1, S):
        halo = exchange(sends)
        part = local(index, current)
        split, piece = gram(index, current, splits, [piece])
        splits.append(split)
        outs = [field] + ([face] * 5 if index < S - 1 else [])
        results = pl.pallas_call(
            step_kernel,
            out_shape=outs,
            in_specs=[SMEM] + [VMEM] * 12,
            out_specs=[VMEM] * len(outs),
                compiler_params=params(5),
            name=f"step{index + 1}",
        )(edge, piece, part, current, *halo, *faces)
        current, sends = results[0], results[1:]
    split, piece = gram(S, current, splits, [piece])
    splits.append(split)
    parts = lax.all_to_all(piece, ("gx", "gz"), 0, 0)
    parts = pl.pallas_call(
        relay_kernel,
        out_shape=near(tall, 8, NZ),
        in_specs=[VMEM],
        out_specs=VMEM,
        compiler_params=params(2),
        name="relay",
    )(parts)
    packed = lax.all_to_all(parts, ("gy",), 0, 0)
    count = COMP * RHS
    new_sol, new_res, basis = pl.pallas_call(
        finish_kernel,
        out_shape=(shaped(count, NX * NY, NZ), shaped(count, NX * NY, NZ), shaped(S * count, NX * NY, NZ)),
        in_specs=[VMEM] * 8,
        out_specs=[in_hbm] * 3,
        scratch_shapes=[
            pltpu.VMEM((count * PITCH, NZ), F32),
            pltpu.VMEM((count * PITCH, NZ), F32),
            pltpu.VMEM((S * count * PITCH, NZ), F32),
            pltpu.VMEM((96, NZ), BF16),
            pltpu.SemaphoreType.DMA((COMP, 3)),
        ],
        compiler_params=params(24),
        name="finish",
    )(packed, *splits, sol, v0)
    return (
        new_sol.reshape(solution.shape),
        new_res.reshape(residual.shape),
        basis.reshape((COMP, S * RHS) + solution.shape[2:]),
    )


def solution(mesh):
    wide = P(None, None, "gx", "gy", "gz")
    return jax.shard_map(
        body,
        mesh=mesh,
        in_specs=(
            wide,
            wide,
            P(None, "gx", "gy", "gz"),
            P(None, "gx", "gy", "gz"),
            P("gx", "gy", "gz"),
            P("gx", "gy", "gz"),
            P(),
        ),
        out_specs=(wide, wide, wide),
        check_vma=False,
    )
```

time: 108 us -> 91.8 us (0.85)
  Pallas kernels: 39.8 us -> 28.9 us
  starting transfers between devices: 40.7 us -> 36 us
    pallas_call x6 -> x10, Pallas kernels: 25.4 us -> 17.6 us  [the longest x1 5.39 us: body(): pl.pallas_call(finish_kernel, out_shape=(shaped(count, NX * NY, NZ), shap...]
    ppermute x24, starting transfers between devices: 40.7 us -> 36 us  [the longest x16 25.4 us: exchange(): lax.ppermute(sends[number + 1 if up else number - 1], axis, links)]
    pallas_call x1, Pallas kernels: 4.38 us -> 2.2 us  [body(): pl.pallas_call(pack_kernel, out_shape=(field, face, face, face, face, fac...]
    all_to_all x1, blocking collectives: 13.7 us -> 12.4 us  [body(): parts = lax.all_to_all(piece, ('gx', 'gz'), 0, 0)]
  transfers between devices with their start and end apart: 24 -> 24, of which waited for: 1 -> 0; matrix products, arithmetic and copies ran while one was open for 0% -> 0% of each run, Pallas kernels for 9% -> 16%
where the time goes in v2:
time: 91.8 us; the launch traced here: 91.6 us
  starting transfers between devices  36 us (39%)
  Pallas kernels  28.9 us (31%)
  blocking collectives  24.8 us (27%)
  between operations  1.07 us (1%)
    ppermute x16, starting transfers between devices, exchange(): lax.ppermute(sends[number + 1 if up else number - 1], axis, links)  25.4 us
    all_to_all x1, blocking collectives, body(): parts = lax.all_to_all(piece, ('gx', 'gz'), 0, 0)  12.4 us
    all_to_all x1, blocking collectives, body(): packed = lax.all_to_all(parts, ('gy',), 0, 0)  12.3 us
    ppermute x4, starting transfers between devices, exchange(): moved.append(lax.ppermute(sends[4], 'gz', links))  9.77 us
    pallas_call x5, Pallas kernels, gram(): pl.pallas_call(lambda *refs: gram_kernel(index, *refs), out_shape=(near(C...  9.1 us
    pallas_call x1, Pallas kernels, body(): pl.pallas_call(finish_kernel, out_shape=(shaped(count, NX * NY, NZ), shap...  5.39 us
    pallas_call x4, Pallas kernels, local(): pl.pallas_call(lambda *refs: local_kernel(index, *refs), out_shape=field,...  4.81 us
    pallas_call x3, Pallas kernels, body(): pl.pallas_call(step_kernel, out_shape=outs, in_specs=[SMEM] + [VMEM] * 12...  3.94 us
  transfers between devices with their start and end apart: 24, of which 0 were waited for; matrix products, arithmetic and copies ran while one was open for 0% of the time, Pallas kernels for 16%

profile of v2, /device:TPU:1, one launch (start us, length us, event | category | flops | bytes accessed | tf_op | source)
XLA Modules:
  0.0 91.6 jit_solution(2399129796766768958)
XLA Ops:
  0.7 0.1 stack.31
  0.8 2.2 %pack.1 = (f32[4,8,8,8,128]{4,3,2,1,0:T(8,128)S(1)}, f32[37,8,128]{2,1,0:T(8,128)S(1)}, f32[37,8,128]{2,1,0:T(8,128)S(1)}, f32[37,8,128]{2,1,0:T(8,128)S(1)}, f3...) custom-call(s32[7]{0:T(128)S(1)} %convert_element_type.3.edge.place, ...), custom_call_target="tpu_custom_call" | custom-call | tf_op jit(solution)/shard_map/pack/pallas_call | solution.py:464
  3.0 2.1 %collective-permute-start = (f32[37,8,128]{2,1,0:T(8,128)S(1)}, f32[37,8,128]{2,1,0:T(8,128)S(1)}, u32[]{:S(2)}, u32[]{:S(2)}) collective-permute-start(f32[37,8,128]{2,1,0:T(8,128)S(1)} %get-tuple-element.57), channel_id=1, source_target_pairs={{0,64},{64,128},{128,192},{192,0},{1,65},{65,129},{129,193},{193,1... | collective-permute-start | bytes 454664 | tf_op jit(solution)/shard_map/ppermute | solution.py:444
  5.1 1.4 %collective-permute-start.1 = (f32[37,8,128]{2,1,0:T(8,128)S(1)}, f32[37,8,128]{2,1,0:T(8,128)S(1)}, u32[]{:S(2)}, u32[]{:S(2)}) collective-permute-start(f32[37,8,128]{2,1,0:T(8,128)S(1)} %get-tuple-element.58), channel_id=1, source_target_pairs={{64,0},{128,64},{192,128},{0,192},{65,1},{129,65},{193,129},{1,193... | collective-permute-start | bytes 454664 | tf_op jit(solution)/shard_map/ppermute | solution.py:444
  6.5 1.7 %collective-permute-start.2 = (f32[37,8,128]{2,1,0:T(8,128)S(1)}, f32[37,8,128]{2,1,0:T(8,128)S(1)}, u32[]{:S(2)}, u32[]{:S(2)}) collective-permute-start(f32[37,8,128]{2,1,0:T(8,128)S(1)} %get-tuple-element.59), channel_id=1, source_target_pairs={{0,8},{8,16},{16,24},{24,32},{32,40},{40,48},{48,56},{56,0},{1,9},... | collective-permute-start | bytes 454664 | tf_op jit(solution)/shard_map/ppermute | solution.py:444
  8.2 3.9 %collective-permute-start.3 = (f32[37,8,128]{2,1,0:T(8,128)S(1)}, f32[37,8,128]{2,1,0:T(8,128)S(1)}, u32[]{:S(2)}, u32[]{:S(2)}) collective-permute-start(f32[37,8,128]{2,1,0:T(8,128)S(1)} %get-tuple-element.60), channel_id=1, source_target_pairs={{8,0},{16,8},{24,16},{32,24},{40,32},{48,40},{56,48},{0,56},{9,1},... | collective-permute-start | bytes 454664 | tf_op jit(solution)/shard_map/ppermute | solution.py:444
  12.1 2.7 %collective-permute-start.5 = (f32[37,8,128]{2,1,0:T(8,128)S(1)}, f32[37,8,128]{2,1,0:T(8,128)S(1)}, u32[]{:S(2)}, u32[]{:S(2)}) collective-permute-start(f32[37,8,128]{2,1,0:T(8,128)S(1)} %get-tuple-element.61), channel_id=1, source_target_pairs={{0,7},{1,2},{2,1},{3,4},{4,3},{5,6},{6,5},{7,0},{8,15},{9,10},{10,... | collective-permute-start | bytes 454664 | tf_op jit(solution)/shard_map/ppermute | solution.py:448
  14.8 0.0 collective-permute-done.refs_0_
  14.8 0.4 collective-permute-start.4
  15.3 0.7 copy-done
  16.0 1.9 %prepare.1 = (f32[2048,128]{1,0:T(8,128)S(1)}, f32[8,8,8,128]{3,2,1,0:T(8,128)S(1)}, f32[8,8,8,128]{3,2,1,0:T(8,128)S(1)}, f32[8,8,8,128]{3,2,1,0:T(8,128)S(1)},...) custom-call(f32[3,6]{1,0:T(4,128)S(1)} %copy-done, f32[5,8,8,128]{3,2,1,0:T(8,128)S(1)} %get-tuple-element.51.pm.inner, ...), custom_call_target="tpu_custom_call" | custom-call | tf_op jit(solution)/shard_map/prepare/pallas_call | solution.py:501
  17.9 1.2 %local1.1.part = f32[4,8,8,8,128]{4,3,2,1,0:T(8,128)S(1)} custom-call(f32[4,8,8,8,128]{4,3,2,1,0:T(8,128)S(1)} %get-tuple-element.50.refs_0_.cur.v0, f32[8,8,8,128]{3,2,1,0:T(8,128)S(1)} %get-tuple-element.52.refs_1_, f32[8,8,8,128]{3,2,1,0:T(8,128)S(1)} %get-tuple-element.53.refs_2_, f32[8,8,8,128]{3,2,1,0:T(8,128)S(1)} %get-tuple-element.54.refs_3_, ...), custom_call_target="tpu_custom_call" | custom-call | flops 6291456 | bytes 3145728 | tf_op jit(solution)/shard_map/local1/pallas_call | solution.py:512
  19.1 0.0 collective-permute-done.1.refs_1_
  19.1 0.0 collective-permute-done.2.refs_2_
  19.1 0.0 collective-permute-done.3.refs_3_
  19.1 0.0 collective-permute-done.5.refs_5_
  19.1 0.0 collective-permute-done.4.refs_4_
  19.1 1.5 %step1.1 = (f32[4,8,8,8,128]{4,3,2,1,0:T(8,128)S(1)}, f32[32,8,128]{2,1,0:T(8,128)S(1)}, f32[32,8,128]{2,1,0:T(8,128)S(1)}, f32[32,8,128]{2,1,0:T(8,128)S(1)}, f...) custom-call(s32[7]{0:T(128)S(1)} %convert_element_type.3.edge.place,, ...), custom_call_target="tpu_custom_call" | custom-call | tf_op jit(solution)/shard_map/step1/pallas_call | solution.py:526
  20.7 0.1 collective-permute-start.6
  20.8 2.7 %collective-permute-start.7 = (f32[32,8,128]{2,1,0:T(8,128)S(1)}, f32[32,8,128]{2,1,0:T(8,128)S(1)}, u32[]{:S(2)}, u32[]{:S(2)}) collective-permute-start(f32[32,8,128]{2,1,0:T(8,128)S(1)} %get-tuple-element.67), channel_id=1, source_target_pairs={{64,0},{128,64},{192,128},{0,192},{65,1},{129,65},{193,129},{1,193... | collective-permute-start | bytes 393224 | tf_op jit(solution)/shard_map/ppermute | solution.py:444
  23.4 0.0 collective-permute-start.8
  23.4 2.7 %collective-permute-start.9 = (f32[32,8,128]{2,1,0:T(8,128)S(1)}, f32[32,8,128]{2,1,0:T(8,128)S(1)}, u32[]{:S(2)}, u32[]{:S(2)}) collective-permute-start(f32[32,8,128]{2,1,0:T(8,128)S(1)} %get-tuple-element.69), channel_id=1, source_target_pairs={{8,0},{16,8},{24,16},{32,24},{40,32},{48,40},{56,48},{0,56},{9,1},... | collective-permute-start | bytes 393224 | tf_op jit(solution)/shard_map/ppermute | solution.py:444
  26.1 2.4 %collective-permute-start.11 = (f32[32,8,128]{2,1,0:T(8,128)S(1)}, f32[32,8,128]{2,1,0:T(8,128)S(1)}, u32[]{:S(2)}, u32[]{:S(2)}) collective-permute-start(f32[32,8,128]{2,1,0:T(8,128)S(1)} %get-tuple-element.70), channel_id=1, source_target_pairs={{0,7},{1,2},{2,1},{3,4},{4,3},{5,6},{6,5},{7,0},{8,15},{9,10},{10,... | collective-permute-start | bytes 393224 | tf_op jit(solution)/shard_map/ppermute | solution.py:448
  28.5 0.0 collective-permute-done.6.refs_0_
  28.5 0.0 collective-permute-start.10
  28.5 1.4 %gram0.1 = (bf16[4,8,8,16,128]{4,3,2,1,0:T(8,128)(2,1)S(1)}, f32[8,128]{1,0:T(8,128)S(1)}) custom-call(f32[4,8,8,8,128]{4,3,2,1,0:T(8,128)S(1)} %get-tuple-element.50.refs_0_.cur.v0), custom_call_target="tpu_custom_call" | custom-call | flops 16777216 | bytes 3145728 | tf_op jit(solution)/shard_map/gram0/pallas_call | solution.py:482
  29.9 1.2 %local2.1.part = f32[4,8,8,8,128]{4,3,2,1,0:T(8,128)S(1)} custom-call(f32[4,8,8,8,128]{4,3,2,1,0:T(8,128)S(1)} %get-tuple-element.62.refs_0_.cur, f32[8,8,8,128]{3,2,1,0:T(8,128)S(1)} %get-tuple-element.52.refs_1_, f32[8,8,8,128]{3,2,1,0:T(8,128)S(1)} %get-tuple-element.53.refs_2_, f32[8,8,8,128]{3,2,1,0:T(8,128)S(1)} %get-tuple-element.54.refs_3_, ...), custom_call_target="tpu_custom_call" | custom-call | flops 6291456 | bytes 3145728 | tf_op jit(solution)/shard_map/local2/pallas_call | solution.py:512
  31.1 1.8 %gram1.1 = (bf16[4,8,8,16,128]{4,3,2,1,0:T(8,128)(2,1)S(1)}, f32[8,128]{1,0:T(8,128)S(1)}) custom-call(f32[4,8,8,8,128]{4,3,2,1,0:T(8,128)S(1)} %get-tuple-element.62.refs_0_.cur, bf16[4,8,8,16,128]{4,3,2,1,0:T(8,128)(2,1)S(1)} %get-tuple-element.63.refs_1_.s0, f32[8,128]{1,0:T(8,128)S(1)} %get-tuple-element.64.refs_2_), custom_call_target="tpu_custom_call" | custom-call | flops 33554432 | bytes 4194304 | tf_op jit(solution)/shard_map/gram1/pallas_call | solution.py:482
  32.9 0.0 collective-permute-done.7.refs_1_
  32.9 0.0 collective-permute-done.8.refs_2_
  32.9 0.0 collective-permute-done.9.refs_3_
  32.9 0.0 collective-permute-done.11.refs_5_
  32.9 0.0 collective-permute-done.10.refs_4_
  32.9 1.5 %step2.1 = (f32[4,8,8,8,128]{4,3,2,1,0:T(8,128)S(1)}, f32[32,8,128]{2,1,0:T(8,128)S(1)}, f32[32,8,128]{2,1,0:T(8,128)S(1)}, f32[32,8,128]{2,1,0:T(8,128)S(1)}, f...) custom-call(s32[7]{0:T(128)S(1)} %convert_element_type.3.edge.place, f32[8,128]{1,0:T(8,128)S(1)} %get-tuple-element.65.piece.refs_3_, ...), custom_call_target="tpu_custom_call" | custom-call | tf_op jit(solution)/shard_map/step2/pallas_call | solution.py:541
  34.4 0.1 collective-permute-start.12
  34.5 2.7 %collective-permute-start.13 = (f32[32,8,128]{2,1,0:T(8,128)S(1)}, f32[32,8,128]{2,1,0:T(8,128)S(1)}, u32[]{:S(2)}, u32[]{:S(2)}) collective-permute-start(f32[32,8,128]{2,1,0:T(8,128)S(1)} %get-tuple-element.78), channel_id=1, source_target_pairs={{64,0},{128,64},{192,128},{0,192},{65,1},{129,65},{193,129},{1,193... | collective-permute-start | bytes 393224 | tf_op jit(solution)/shard_map/ppermute | solution.py:444
  37.2 0.0 collective-permute-start.14
  37.2 2.7 %collective-permute-start.15 = (f32[32,8,128]{2,1,0:T(8,128)S(1)}, f32[32,8,128]{2,1,0:T(8,128)S(1)}, u32[]{:S(2)}, u32[]{:S(2)}) collective-permute-start(f32[32,8,128]{2,1,0:T(8,128)S(1)} %get-tuple-element.80), channel_id=1, source_target_pairs={{8,0},{16,8},{24,16},{32,24},{40,32},{48,40},{56,48},{0,56},{9,1},... | collective-permute-start | bytes 393224 | tf_op jit(solution)/shard_map/ppermute | solution.py:444
  39.8 2.5 %collective-permute-start.17 = (f32[32,8,128]{2,1,0:T(8,128)S(1)}, f32[32,8,128]{2,1,0:T(8,128)S(1)}, u32[]{:S(2)}, u32[]{:S(2)}) collective-permute-start(f32[32,8,128]{2,1,0:T(8,128)S(1)} %get-tuple-element.81), channel_id=1, source_target_pairs={{0,7},{1,2},{2,1},{3,4},{4,3},{5,6},{6,5},{7,0},{8,15},{9,10},{10,... | collective-permute-start | bytes 393224 | tf_op jit(solution)/shard_map/ppermute | solution.py:448
  42.4 0.0 collective-permute-done.12.refs_0_
  42.4 0.0 collective-permute-start.16
  42.4 1.2 %local3.1.part = f32[4,8,8,8,128]{4,3,2,1,0:T(8,128)S(1)} custom-call(f32[4,8,8,8,128]{4,3,2,1,0:T(8,128)S(1)} %get-tuple-element.74.refs_0_.cur, f32[8,8,8,128]{3,2,1,0:T(8,128)S(1)} %get-tuple-element.52.refs_1_, f32[8,8,8,128]{3,2,1,0:T(8,128)S(1)} %get-tuple-element.53.refs_2_, f32[8,8,8,128]{3,2,1,0:T(8,128)S(1)} %get-tuple-element.54.refs_3_, ...), custom_call_target="tpu_custom_call" | custom-call | flops 6291456 | bytes 3145728 | tf_op jit(solution)/shard_map/local3/pallas_call | solution.py:512
  43.6 2.1 %gram2.1 = (bf16[4,8,8,16,128]{4,3,2,1,0:T(8,128)(2,1)S(1)}, f32[8,128]{1,0:T(8,128)S(1)}) custom-call(f32[4,8,8,8,128]{4,3,2,1,0:T(8,128)S(1)} %get-tuple-element.74.refs_0_.cur, bf16[4,8,8,16,128]{4,3,2,1,0:T(8,128)(2,1)S(1)} %get-tuple-element.63.refs_1_.s0, bf16[4,8,8,16,128]{4,3,2,1,0:T(8,128)(2,1)S(1)} %get-tuple-element.75.refs_2_.s1, ...), custom_call_target="tpu_custom_call" | custom-call | flops 50331648 | bytes 5242880 | tf_op jit(solution)/shard_map/gram2/pallas_call | solution.py:482
  45.6 0.0 collective-permute-done.13.refs_1_
  45.6 0.0 collective-permute-done.15.refs_3_
  45.7 0.0 collective-permute-done.17.refs_5_
  45.7 1.5 %step3.1 = (f32[4,8,8,8,128]{4,3,2,1,0:T(8,128)S(1)}, f32[32,8,128]{2,1,0:T(8,128)S(1)}, f32[32,8,128]{2,1,0:T(8,128)S(1)}, f32[32,8,128]{2,1,0:T(8,128)S(1)}, f...) custom-call(s32[7]{0:T(128)S(1)} %convert_element_type.3.edge.place, f32[8,128]{1,0:T(8,128)S(1)} %get-tuple-element.76.piece.refs_4_, ...), custom_call_target="tpu_custom_call" | custom-call | tf_op jit(solution)/shard_map/step3/pallas_call | solution.py:541
  47.1 0.1 collective-permute-start.18
  47.2 2.7 %collective-permute-start.19 = (f32[32,8,128]{2,1,0:T(8,128)S(1)}, f32[32,8,128]{2,1,0:T(8,128)S(1)}, u32[]{:S(2)}, u32[]{:S(2)}) collective-permute-start(f32[32,8,128]{2,1,0:T(8,128)S(1)} %get-tuple-element.86), channel_id=1, source_target_pairs={{64,0},{128,64},{192,128},{0,192},{65,1},{129,65},{193,129},{1,193... | collective-permute-start | bytes 393224 | tf_op jit(solution)/shard_map/ppermute | solution.py:444
  49.9 2.7 %collective-permute-start.21 = (f32[32,8,128]{2,1,0:T(8,128)S(1)}, f32[32,8,128]{2,1,0:T(8,128)S(1)}, u32[]{:S(2)}, u32[]{:S(2)}) collective-permute-start(f32[32,8,128]{2,1,0:T(8,128)S(1)} %get-tuple-element.88), channel_id=1, source_target_pairs={{8,0},{16,8},{24,16},{32,24},{40,32},{48,40},{56,48},{0,56},{9,1},... | collective-permute-start | bytes 393224 | tf_op jit(solution)/shard_map/ppermute | solution.py:444
  52.6 2.2 %collective-permute-start.23 = (f32[32,8,128]{2,1,0:T(8,128)S(1)}, f32[32,8,128]{2,1,0:T(8,128)S(1)}, u32[]{:S(2)}, u32[]{:S(2)}) collective-permute-start(f32[32,8,128]{2,1,0:T(8,128)S(1)} %get-tuple-element.89), channel_id=1, source_target_pairs={{0,7},{1,2},{2,1},{3,4},{4,3},{5,6},{6,5},{7,0},{8,15},{9,10},{10,... | collective-permute-start | bytes 393224 | tf_op jit(solution)/shard_map/ppermute | solution.py:448
  54.8 0.0 collective-permute-done.18.refs_0_
  54.8 0.3 collective-permute-start.22
  55.1 1.2 %local4.1.part = f32[4,8,8,8,128]{4,3,2,1,0:T(8,128)S(1)} custom-call(f32[4,8,8,8,128]{4,3,2,1,0:T(8,128)S(1)} %get-tuple-element.82.refs_0_.cur, f32[8,8,8,128]{3,2,1,0:T(8,128)S(1)} %get-tuple-element.52.refs_1_, f32[8,8,8,128]{3,2,1,0:T(8,128)S(1)} %get-tuple-element.53.refs_2_, f32[8,8,8,128]{3,2,1,0:T(8,128)S(1)} %get-tuple-element.54.refs_3_, ...), custom_call_target="tpu_custom_call" | custom-call | flops 6291456 | bytes 3145728 | tf_op jit(solution)/shard_map/local4/pallas_call | solution.py:512
  56.3 2.4 %gram3.1 = (bf16[4,8,8,16,128]{4,3,2,1,0:T(8,128)(2,1)S(1)}, f32[8,128]{1,0:T(8,128)S(1)}) custom-call(f32[4,8,8,8,128]{4,3,2,1,0:T(8,128)S(1)} %get-tuple-element.82.refs_0_.cur, bf16[4,8,8,16,128]{4,3,2,1,0:T(8,128)(2,1)S(1)} %get-tuple-element.63.refs_1_.s0, bf16[4,8,8,16,128]{4,3,2,1,0:T(8,128)(2,1)S(1)} %get-tuple-element.75.refs_2_.s1, ...), custom_call_target="tpu_custom_call" | custom-call | flops 67108864 | bytes 6291456 | tf_op jit(solution)/shard_map/gram3/pallas_call | solution.py:482
  58.6 0.0 collective-permute-done.19.refs_1_
  58.6 0.0 collective-permute-done.20.refs_2_
  58.7 0.0 collective-permute-done.23.refs_5_
  58.7 0.0 collective-permute-done.22.refs_4_
  58.7 1.0 %step4.1.refs_0_ = f32[4,8,8,8,128]{4,3,2,1,0:T(8,128)S(1)} custom-call(s32[7]{0:T(128)S(1)} %convert_element_type.3.edge.place, f32[8,128]{1,0:T(8,128)S(1)} %get-tuple-element.84.piece.refs_2_, f32[4,8,8,8,128]{4,3,2,1,0:T(8,128)S(1)} %local4.1.part, f32[4,8,8,8,128]{4,3,2,1,0:T(8,128)S(1)} %get-tuple-element.82.refs_0_.cur, ...), custom_call_target="tpu_custom_call" | custom-call | tf_op jit(solution)/shard_map/step4/pallas_call | solution.py:541
  59.7 1.5 %gram4.1 = (bf16[4,8,8,16,128]{4,3,2,1,0:T(8,128)(2,1)S(1)}, f32[32,8,128]{2,1,0:T(8,128)S(1)}) custom-call(f32[4,8,8,8,128]{4,3,2,1,0:T(8,128)S(1)} %step4.1.refs_0_, bf16[4,8,8,16,128]{4,3,2,1,0:T(8,128)(2,1)S(1)} %get-tuple-element.90.refs_1_.s3, f32[8,128]{1,0:T(8,128)S(1)} %get-tuple-element.84.piece.refs_2_), custom_call_target="tpu_custom_call" | custom-call | flops 83886080 | bytes 7340032 | tf_op jit(solution)/shard_map/gram4/pallas_call | solution.py:482
  61.2 12.4 %all_to_all.10.parts = f32[32,8,128]{2,1,0:T(8,128)S(1)} all-to-all(f32[32,8,128]{2,1,0:T(8,128)S(1)} %get-tuple-element.91), channel_id=1, replica_groups=mesh['gx'=4,'gy'=8,'gz'=8] {'gx','gz'}, dimensions={0} | all-to-all | bytes 262144 | tf_op jit(solution)/shard_map/all_to_all | solution.py:552
  73.7 12.3 %all_to_all.11.packed = f32[8,8,128]{2,1,0:T(8,128)S(1)} all-to-all(f32[8,8,128]{2,1,0:T(8,128)S(1)} %relay.1), channel_id=1, replica_groups=mesh['gx'=4,'gy'=8,'gz'=8] {'gy'}, dimensions={0} | all-to-all | bytes 65536 | tf_op jit(solution)/shard_map/all_to_all | solution.py:561
  86.0 5.4 %finish.1 = (f32[32,64,128]{2,1,0:T(8,128)}, f32[32,64,128]{2,1,0:T(8,128)}, f32[128,64,128]{2,1,0:T(8,128)}) custom-call(f32[8,8,128]{2,1,0:T(8,128)S(1)} %all_to_all.11.packed, bf16[4,8,8,16,128]{4,3,2,1,0:T(8,128)(2,1)S(1)} %get-tuple-element.63.refs_1_.s0, bf16[4,8,8,16,128]{4,3,2,1,0:T(8,128)(2,1)S(1)} %get-tuple-element.75.refs_2_.s1, ...), custom_call_target="tpu_custom_call" | custom-call | tf_op jit(solution)/shard_map/finish/pallas_call | solution.py:563
  (7 shorter events, 0.1 us)
Async XLA Ops:
  3.0 11.9 %collective-permute-start = (f32[37,8,128]{2,1,0:T(8,128)S(1)}, f32[37,8,128]{2,1,0:T(8,128)S(1)}, u32[]{:S(2)}, u32[]{:S(2)}) collective-permute-start(f32[37,8,128]{2,1,0:T(8,128)S(1)} %get-tuple-element.57), channel_id=1, source_target_pairs={{0,64},{64,128},{128,192},{192,0},{1,65},{65,129},{129,193},{193,1... | collective-permute-start | bytes 454664 | tf_op jit(solution)/shard_map/ppermute | solution.py:444
  5.1 14.0 %collective-permute-start.1 = (f32[37,8,128]{2,1,0:T(8,128)S(1)}, f32[37,8,128]{2,1,0:T(8,128)S(1)}, u32[]{:S(2)}, u32[]{:S(2)}) collective-permute-start(f32[37,8,128]{2,1,0:T(8,128)S(1)} %get-tuple-element.58), channel_id=1, source_target_pairs={{64,0},{128,64},{192,128},{0,192},{65,1},{129,65},{193,129},{1,193... | collective-permute-start | bytes 454664 | tf_op jit(solution)/shard_map/ppermute | solution.py:444
  6.5 12.6 %collective-permute-start.2 = (f32[37,8,128]{2,1,0:T(8,128)S(1)}, f32[37,8,128]{2,1,0:T(8,128)S(1)}, u32[]{:S(2)}, u32[]{:S(2)}) collective-permute-start(f32[37,8,128]{2,1,0:T(8,128)S(1)} %get-tuple-element.59), channel_id=1, source_target_pairs={{0,8},{8,16},{16,24},{24,32},{32,40},{40,48},{48,56},{56,0},{1,9},... | collective-permute-start | bytes 454664 | tf_op jit(solution)/shard_map/ppermute | solution.py:444
  8.2 10.9 %collective-permute-start.3 = (f32[37,8,128]{2,1,0:T(8,128)S(1)}, f32[37,8,128]{2,1,0:T(8,128)S(1)}, u32[]{:S(2)}, u32[]{:S(2)}) collective-permute-start(f32[37,8,128]{2,1,0:T(8,128)S(1)} %get-tuple-element.60), channel_id=1, source_target_pairs={{8,0},{16,8},{24,16},{32,24},{40,32},{48,40},{56,48},{0,56},{9,1},... | collective-permute-start | bytes 454664 | tf_op jit(solution)/shard_map/ppermute | solution.py:444
  12.1 7.0 %collective-permute-start.5 = (f32[37,8,128]{2,1,0:T(8,128)S(1)}, f32[37,8,128]{2,1,0:T(8,128)S(1)}, u32[]{:S(2)}, u32[]{:S(2)}) collective-permute-start(f32[37,8,128]{2,1,0:T(8,128)S(1)} %get-tuple-element.61), channel_id=1, source_target_pairs={{0,7},{1,2},{2,1},{3,4},{4,3},{5,6},{6,5},{7,0},{8,15},{9,10},{10,... | collective-permute-start | bytes 454664 | tf_op jit(solution)/shard_map/ppermute | solution.py:448
  14.8 4.3 %collective-permute-start.4 = (f32[37,8,128]{2,1,0:T(8,128)S(1)}, f32[37,8,128]{2,1,0:T(8,128)S(1)}, u32[]{:S(2)}, u32[]{:S(2)}) collective-permute-start(f32[37,8,128]{2,1,0:T(8,128)S(1)} %get-tuple-element.61), channel_id=1, source_target_pairs={{0,1},{1,0},{2,3},{3,2},{4,5},{5,4},{6,7},{7,6},{8,9},{9,8},{10,11... | collective-permute-start | bytes 454664 | tf_op jit(solution)/shard_map/ppermute | solution.py:446
  15.3 0.7 copy-start
  20.7 7.8 %collective-permute-start.6 = (f32[32,8,128]{2,1,0:T(8,128)S(1)}, f32[32,8,128]{2,1,0:T(8,128)S(1)}, u32[]{:S(2)}, u32[]{:S(2)}) collective-permute-start(f32[32,8,128]{2,1,0:T(8,128)S(1)} %get-tuple-element.66), channel_id=1, source_target_pairs={{0,64},{64,128},{128,192},{192,0},{1,65},{65,129},{129,193},{193,1... | collective-permute-start | bytes 393224 | tf_op jit(solution)/shard_map/ppermute | solution.py:444
  20.8 12.1 %collective-permute-start.7 = (f32[32,8,128]{2,1,0:T(8,128)S(1)}, f32[32,8,128]{2,1,0:T(8,128)S(1)}, u32[]{:S(2)}, u32[]{:S(2)}) collective-permute-start(f32[32,8,128]{2,1,0:T(8,128)S(1)} %get-tuple-element.67), channel_id=1, source_target_pairs={{64,0},{128,64},{192,128},{0,192},{65,1},{129,65},{193,129},{1,193... | collective-permute-start | bytes 393224 | tf_op jit(solution)/shard_map/ppermute | solution.py:444
  23.4 9.5 %collective-permute-start.8 = (f32[32,8,128]{2,1,0:T(8,128)S(1)}, f32[32,8,128]{2,1,0:T(8,128)S(1)}, u32[]{:S(2)}, u32[]{:S(2)}) collective-permute-start(f32[32,8,128]{2,1,0:T(8,128)S(1)} %get-tuple-element.68), channel_id=1, source_target_pairs={{0,8},{8,16},{16,24},{24,32},{32,40},{40,48},{48,56},{56,0},{1,9},... | collective-permute-start | bytes 393224 | tf_op jit(solution)/shard_map/ppermute | solution.py:444
  23.4 9.5 %collective-permute-start.9 = (f32[32,8,128]{2,1,0:T(8,128)S(1)}, f32[32,8,128]{2,1,0:T(8,128)S(1)}, u32[]{:S(2)}, u32[]{:S(2)}) collective-permute-start(f32[32,8,128]{2,1,0:T(8,128)S(1)} %get-tuple-element.69), channel_id=1, source_target_pairs={{8,0},{16,8},{24,16},{32,24},{40,32},{48,40},{56,48},{0,56},{9,1},... | collective-permute-start | bytes 393224 | tf_op jit(solution)/shard_map/ppermute | solution.py:444
  26.1 6.8 %collective-permute-start.11 = (f32[32,8,128]{2,1,0:T(8,128)S(1)}, f32[32,8,128]{2,1,0:T(8,128)S(1)}, u32[]{:S(2)}, u32[]{:S(2)}) collective-permute-start(f32[32,8,128]{2,1,0:T(8,128)S(1)} %get-tuple-element.70), channel_id=1, source_target_pairs={{0,7},{1,2},{2,1},{3,4},{4,3},{5,6},{6,5},{7,0},{8,15},{9,10},{10,... | collective-permute-start | bytes 393224 | tf_op jit(solution)/shard_map/ppermute | solution.py:448
  28.5 4.4 %collective-permute-start.10 = (f32[32,8,128]{2,1,0:T(8,128)S(1)}, f32[32,8,128]{2,1,0:T(8,128)S(1)}, u32[]{:S(2)}, u32[]{:S(2)}) collective-permute-start(f32[32,8,128]{2,1,0:T(8,128)S(1)} %get-tuple-element.70), channel_id=1, source_target_pairs={{0,1},{1,0},{2,3},{3,2},{4,5},{5,4},{6,7},{7,6},{8,9},{9,8},{10,11... | collective-permute-start | bytes 393224 | tf_op jit(solution)/shard_map/ppermute | solution.py:446
  34.4 7.9 %collective-permute-start.12 = (f32[32,8,128]{2,1,0:T(8,128)S(1)}, f32[32,8,128]{2,1,0:T(8,128)S(1)}, u32[]{:S(2)}, u32[]{:S(2)}) collective-permute-start(f32[32,8,128]{2,1,0:T(8,128)S(1)} %get-tuple-element.77), channel_id=1, source_target_pairs={{0,64},{64,128},{128,192},{192,0},{1,65},{65,129},{129,193},{193,1... | collective-permute-start | bytes 393224 | tf_op jit(solution)/shard_map/ppermute | solution.py:444
  34.5 11.1 %collective-permute-start.13 = (f32[32,8,128]{2,1,0:T(8,128)S(1)}, f32[32,8,128]{2,1,0:T(8,128)S(1)}, u32[]{:S(2)}, u32[]{:S(2)}) collective-permute-start(f32[32,8,128]{2,1,0:T(8,128)S(1)} %get-tuple-element.78), channel_id=1, source_target_pairs={{64,0},{128,64},{192,128},{0,192},{65,1},{129,65},{193,129},{1,193... | collective-permute-start | bytes 393224 | tf_op jit(solution)/shard_map/ppermute | solution.py:444
  37.2 8.5 %collective-permute-start.14 = (f32[32,8,128]{2,1,0:T(8,128)S(1)}, f32[32,8,128]{2,1,0:T(8,128)S(1)}, u32[]{:S(2)}, u32[]{:S(2)}) collective-permute-start(f32[32,8,128]{2,1,0:T(8,128)S(1)} %get-tuple-element.79), channel_id=1, source_target_pairs={{0,8},{8,16},{16,24},{24,32},{32,40},{40,48},{48,56},{56,0},{1,9},... | collective-permute-start | bytes 393224 | tf_op jit(solution)/shard_map/ppermute | solution.py:444
  37.2 8.5 %collective-permute-start.15 = (f32[32,8,128]{2,1,0:T(8,128)S(1)}, f32[32,8,128]{2,1,0:T(8,128)S(1)}, u32[]{:S(2)}, u32[]{:S(2)}) collective-permute-start(f32[32,8,128]{2,1,0:T(8,128)S(1)} %get-tuple-element.80), channel_id=1, source_target_pairs={{8,0},{16,8},{24,16},{32,24},{40,32},{48,40},{56,48},{0,56},{9,1},... | collective-permute-start | bytes 393224 | tf_op jit(solution)/shard_map/ppermute | solution.py:444
  39.8 5.8 %collective-permute-start.17 = (f32[32,8,128]{2,1,0:T(8,128)S(1)}, f32[32,8,128]{2,1,0:T(8,128)S(1)}, u32[]{:S(2)}, u32[]{:S(2)}) collective-permute-start(f32[32,8,128]{2,1,0:T(8,128)S(1)} %get-tuple-element.81), channel_id=1, source_target_pairs={{0,7},{1,2},{2,1},{3,4},{4,3},{5,6},{6,5},{7,0},{8,15},{9,10},{10,... | collective-permute-start | bytes 393224 | tf_op jit(solution)/shard_map/ppermute | solution.py:448
  42.4 3.3 %collective-permute-start.16 = (f32[32,8,128]{2,1,0:T(8,128)S(1)}, f32[32,8,128]{2,1,0:T(8,128)S(1)}, u32[]{:S(2)}, u32[]{:S(2)}) collective-permute-start(f32[32,8,128]{2,1,0:T(8,128)S(1)} %get-tuple-element.81), channel_id=1, source_target_pairs={{0,1},{1,0},{2,3},{3,2},{4,5},{5,4},{6,7},{7,6},{8,9},{9,8},{10,11... | collective-permute-start | bytes 393224 | tf_op jit(solution)/shard_map/ppermute | solution.py:446
  47.1 7.6 %collective-permute-start.18 = (f32[32,8,128]{2,1,0:T(8,128)S(1)}, f32[32,8,128]{2,1,0:T(8,128)S(1)}, u32[]{:S(2)}, u32[]{:S(2)}) collective-permute-start(f32[32,8,128]{2,1,0:T(8,128)S(1)} %get-tuple-element.85), channel_id=1, source_target_pairs={{0,64},{64,128},{128,192},{192,0},{1,65},{65,129},{129,193},{193,1... | collective-permute-start | bytes 393224 | tf_op jit(solution)/shard_map/ppermute | solution.py:444
  47.2 11.4 %collective-permute-start.19 = (f32[32,8,128]{2,1,0:T(8,128)S(1)}, f32[32,8,128]{2,1,0:T(8,128)S(1)}, u32[]{:S(2)}, u32[]{:S(2)}) collective-permute-start(f32[32,8,128]{2,1,0:T(8,128)S(1)} %get-tuple-element.86), channel_id=1, source_target_pairs={{64,0},{128,64},{192,128},{0,192},{65,1},{129,65},{193,129},{1,193... | collective-permute-start | bytes 393224 | tf_op jit(solution)/shard_map/ppermute | solution.py:444
  49.9 8.8 %collective-permute-start.20 = (f32[32,8,128]{2,1,0:T(8,128)S(1)}, f32[32,8,128]{2,1,0:T(8,128)S(1)}, u32[]{:S(2)}, u32[]{:S(2)}) collective-permute-start(f32[32,8,128]{2,1,0:T(8,128)S(1)} %get-tuple-element.87), channel_id=1, source_target_pairs={{0,8},{8,16},{16,24},{24,32},{32,40},{40,48},{48,56},{56,0},{1,9},... | collective-permute-start | bytes 393224 | tf_op jit(solution)/shard_map/ppermute | solution.py:444
  49.9 8.8 %collective-permute-start.21 = (f32[32,8,128]{2,1,0:T(8,128)S(1)}, f32[32,8,128]{2,1,0:T(8,128)S(1)}, u32[]{:S(2)}, u32[]{:S(2)}) collective-permute-start(f32[32,8,128]{2,1,0:T(8,128)S(1)} %get-tuple-element.88), channel_id=1, source_target_pairs={{8,0},{16,8},{24,16},{32,24},{40,32},{48,40},{56,48},{0,56},{9,1},... | collective-permute-start | bytes 393224 | tf_op jit(solution)/shard_map/ppermute | solution.py:444
  52.6 6.1 %collective-permute-start.23 = (f32[32,8,128]{2,1,0:T(8,128)S(1)}, f32[32,8,128]{2,1,0:T(8,128)S(1)}, u32[]{:S(2)}, u32[]{:S(2)}) collective-permute-start(f32[32,8,128]{2,1,0:T(8,128)S(1)} %get-tuple-element.89), channel_id=1, source_target_pairs={{0,7},{1,2},{2,1},{3,4},{4,3},{5,6},{6,5},{7,0},{8,15},{9,10},{10,... | collective-permute-start | bytes 393224 | tf_op jit(solution)/shard_map/ppermute | solution.py:448
  54.8 3.9 %collective-permute-start.22 = (f32[32,8,128]{2,1,0:T(8,128)S(1)}, f32[32,8,128]{2,1,0:T(8,128)S(1)}, u32[]{:S(2)}, u32[]{:S(2)}) collective-permute-start(f32[32,8,128]{2,1,0:T(8,128)S(1)} %get-tuple-element.89), channel_id=1, source_target_pairs={{0,1},{1,0},{2,3},{3,2},{4,5},{5,4},{6,7},{7,6},{8,9},{9,8},{10,11... | collective-permute-start | bytes 393224 | tf_op jit(solution)/shard_map/ppermute | solution.py:446

commit v3 on v2

--- a/solution.py
+++ b/solution.py
@@ -34,6 +34,16 @@
     return jnp.where((lane >> 1) == slot, pltpu.roll(tile, 2 * slot + 1, 1), acc)
 
 
+def chooser(place, axis):
+    odd = (jnp.zeros((8, NZ), jnp.int32) + place[6 + axis]) == 1
+
+    def pick(side, first, second):
+        mask = odd[: first.shape[0]]
+        return jnp.where(mask, second, first) if side else jnp.where(mask, first, second)
+
+    return pick
+
+
 def join(lines, lane):
     while len(lines) > 1:
         half = 128 // len(lines)
@@ -50,8 +60,11 @@
     return copies
 
 
-def pack_kernel(edge, res_hbm, perm_hbm, mask_hbm, v0, xlo, xhi, ylo, yhi, ends, pm, res, mask, sems):
+def pack_kernel(place, res_hbm, perm_hbm, mask_hbm, v0, xa, xb, ya, yb, ends, pm, res, mask, sems):
     lane = lane_ids((8, NZ))
+    last_x, last_y = NX - 1, NY - 1
+    first_x, first_y = last_x * (1 - place[6]), last_y * (1 - place[7])
+    pick_y = chooser(place, 1)
     spaced = res.reshape(COMP * RHS, PITCH, NZ)
     spans = [pl.ds(RHS * c, RHS) for c in range(COMP)]
     copies = fetch(
@@ -68,13 +81,13 @@
         acc = jnp.zeros((8, NZ), F32)
         for x in range(NX):
             tile = pm[f, x]
-            ylo[FACE + f, x : x + 1, :] = tile[0:1]
-            yhi[FACE + f, x : x + 1, :] = tile[7:8]
+            ya[FACE + f, x : x + 1, :] = pick_y(0, tile[0:1], tile[7:8])
+            yb[FACE + f, x : x + 1, :] = pick_y(1, tile[0:1], tile[7:8])
             acc = put_ends(acc, tile, lane, x)
         ends[COMP + f] = acc
     for f in range(5):
-        xlo[FACE + f] = pm[f, 0]
-        xhi[FACE + f] = pm[f, NX - 1]
+        xa[FACE + f] = pm[f, first_x]
+        xb[FACE + f] = pm[f, last_x - first_x]
 
     for c in range(COMP):
         copies[2 + c].wait()
@@ -85,12 +98,13 @@
                 tile = res[pl.ds(c * RHS * PITCH + x * 8 + y, 8, stride=PITCH), :]
                 v0[c, x, y] = tile
                 acc = put_ends(acc, tile, lane, x * 8 + y)
-                if y in (0, NY - 1):
-                    (yhi if y else ylo)[c * 8 + x] = tile
-                if x in (0, NX - 1):
-                    (xhi if x else xlo)[c * 8 + y] = tile
             lines.append(acc)
         ends[c] = join(lines, lane)
+        for i in range(8):
+            xa[c * 8 + i] = v0[c, first_x, i]
+            xb[c * 8 + i] = v0[c, last_x - first_x, i]
+            ya[c * 8 + i] = v0[c, i, first_y]
+            yb[c * 8 + i] = v0[c, i, last_y - first_y]
 
 
 def face(own, other, masks):
@@ -168,28 +182,31 @@
 
 
 def ghost_tile(place, first, second, lane):
-    return jnp.where(((lane + place[6]) & 1) == 0, second, first)
+    return jnp.where(((lane + place[8]) & 1) == 0, second, first)
 
 
 def edge_kernel(place, inner, halo, bx, by, bz):
-    xl, xh, yl, yh, z0, z1 = halo
+    xa, xb, ya, yb, z0, z1 = halo
+    pick_x, pick_y = chooser(place, 0), chooser(place, 1)
     lane = lane_ids((8, NZ))
     keep = [place[i].astype(F32) for i in range(6)]
     tiles = [ghost_tile(place, z0[COMP + f], z1[COMP + f], lane) for f in range(5)]
     tiles[4] = tiles[4] * jnp.where((lane & 1) == 0, keep[4], keep[5])
-    for side, (halo_x, halo_y) in enumerate(((xl, yl), (xh, yh))):
+    for side in range(2):
         x = side * (NX - 1)
-        mask = inner[COMP, x] * halo_x[FACE + COMP] * keep[side]
+        near_x = [pick_x(side, xa[FACE + f], xb[FACE + f]) for f in range(5)]
+        mask = inner[COMP, x] * near_x[COMP] * keep[side]
         for c in range(COMP):
-            bx[side, c] = face(inner[c, x], halo_x[FACE + c], mask)
+            bx[side, c] = face(inner[c, x], near_x[c], mask)
 
     for x in range(NX):
         row = pl.ds(x, 1)
-        for side, halo_y in enumerate((yl, yh)):
+        for side in range(2):
             own = pl.ds(side * (NY - 1), 1)
-            mask = inner[COMP, x, own, :] * halo_y[FACE + COMP, row, :] * keep[2 + side]
+            near_y = [pick_y(side, ya[FACE + f, row, :], yb[FACE + f, row, :]) for f in range(5)]
+            mask = inner[COMP, x, own, :] * near_y[COMP] * keep[2 + side]
             for c in range(COMP):
-                by[side, c, row, :] = face(inner[c, x, own, :], halo_y[FACE + c, row, :], mask)
+                by[side, c, row, :] = face(inner[c, x, own, :], near_y[c], mask)
         near_x = [pltpu.roll(t, (128 - 2 * x) & 127, 1) for t in tiles]
         ghosts = [jnp.where(lane == 0, t, pltpu.roll(t, 126, 1)) for t in near_x]
         mask = jnp.where((lane == 0) | (lane == 127), inner[COMP, x] * ghosts[4], 0.0)
@@ -198,7 +215,8 @@
 
 
 def close_step(place, part, cur, halo, bx, by, bz, out, sends):
-    xl, xh, yl, yh, z0, z1 = halo
+    xa, xb, ya, yb, z0, z1 = halo
+    pick_x, pick_y = chooser(place, 0), chooser(place, 1)
     lane = lane_ids((8, NZ))
     ghosts, lines = [], [[] for _ in range(COMP)]
     for c in range(COMP):
@@ -214,24 +232,28 @@
                 value = part[c, x, y] + bz[c, x, pl.ds(y, 1), :] * (g - p)
                 if y in (0, NY - 1):
                     side = 1 if y else 0
-                    other = (yl, yh)[side][c * 8 + x]
+                    other = pick_y(side, ya[c * 8 + x], yb[c * 8 + x])
                     value = value + by[side, c, pl.ds(x, 1), :] * (other - p)
                 if x in (0, NX - 1):
                     side = 1 if x else 0
-                    other = (xl, xh)[side][c * 8 + y]
+                    other = pick_x(side, xa[c * 8 + y], xb[c * 8 + y])
                     value = value + bx[side, c, pl.ds(y, 1), :] * (other - p)
                 out[c, x, y] = value
                 if sends is not None:
                     accs[c] = put_ends(accs[c], value, lane, slot)
-                    if y in (0, NY - 1):
-                        sends[2 + (1 if y else 0)][c * 8 + x] = value
-                    if x in (0, NX - 1):
-                        sends[1 if x else 0][c * 8 + y] = value
         for c in range(COMP):
             lines[c].append(accs[c])
     if sends is not None:
         for c in range(COMP):
             sends[4][c] = join(lines[c], lane)
+        last_x, last_y = NX - 1, NY - 1
+        first_x, first_y = last_x * (1 - place[6]), last_y * (1 - place[7])
+        for c in range(COMP):
+            for i in range(8):
+                sends[0][c * 8 + i] = out[c, first_x, i]
+                sends[1][c * 8 + i] = out[c, last_x - first_x, i]
+                sends[2][c * 8 + i] = out[c, i, first_y]
+                sends[3][c * 8 + i] = out[c, i, last_y - first_y]
 
 
 def first_kernel(place, part, cur, inner, *refs):
@@ -435,17 +457,12 @@
 
 def exchange(sends):
     moved = []
-    for number, (axis, up) in enumerate((("gx", 1), ("gx", 0), ("gy", 1), ("gy", 0))):
+    for axis, pair in (("gx", sends[0:2]), ("gy", sends[2:4]), ("gz", (sends[4], sends[4]))):
         count = lax.axis_size(axis)
-        if up:
-            links = [(i, (i + 1) % count) for i in range(count)]
-        else:
-            links = [((i + 1) % count, i) for i in range(count)]
-        moved.append(lax.ppermute(sends[number + 1 if up else number - 1], axis, links))
-    count = lax.axis_size("gz")
-    moved.append(lax.ppermute(sends[4], "gz", [(i, i ^ 1) for i in range(count)]))
-    links = [(i, (i + (1 if i % 2 else -1)) % count) for i in range(count)]
-    moved.append(lax.ppermute(sends[4], "gz", links))
+        first = [(i, i ^ 1) for i in range(count)]
+        second = [(i, (i + (1 if i % 2 else -1)) % count) for i in range(count)]
+        moved.append(lax.ppermute(pair[0], axis, first))
+        moved.append(lax.ppermute(pair[1], axis, second))
     return moved
 
 
@@ -455,7 +472,7 @@
     for axis in ("gx", "gy", "gz"):
         place = lax.axis_index(axis)
         edge += [place > 0, place < lax.axis_size(axis) - 1]
-    edge.append(place % 2 == 1)
+    edge += [lax.axis_index(axis) % 2 == 1 for axis in ("gx", "gy", "gz")]
     edge = jnp.stack(edge).astype(jnp.int32)
     field = near(COMP, NX, NY, RHS, NZ)
     face = near(FACE + 5, 8, NZ)

time: 91.8 us -> 87 us (0.948)
  starting transfers between devices: 36 us -> 31.8 us
    ppermute x24, starting transfers between devices: 36 us -> 31.8 us  [the longest x12 23.1 us: exchange(): moved.append(lax.ppermute(pair[1], axis, second))]
    all_to_all x1, blocking collectives: 12.3 us -> 11.1 us  [body(): packed = lax.all_to_all(parts, ('gy',), 0, 0)]
where the time goes in v3:
time: 87 us; the launch traced here: 86.8 us
  starting transfers between devices  31.8 us (37%)
  Pallas kernels  29 us (33%)
  blocking collectives  24.1 us (28%)
  between operations  1.06 us (1%)
    ppermute x12, starting transfers between devices, exchange(): moved.append(lax.ppermute(pair[1], axis, second))  23.1 us
    all_to_all x1, blocking collectives, body(): parts = lax.all_to_all(piece, ('gx', 'gz'), 0, 0)  12.9 us
    all_to_all x1, blocking collectives, body(): packed = lax.all_to_all(parts, ('gy',), 0, 0)  11.1 us
    pallas_call x5, Pallas kernels, gram(): pl.pallas_call(lambda *refs: gram_kernel(index, *refs), out_shape=(near(C...  9.08 us
    ppermute x12, starting transfers between devices, exchange(): moved.append(lax.ppermute(pair[0], axis, first))  8.72 us
    pallas_call x1, Pallas kernels, body(): pl.pallas_call(finish_kernel, out_shape=(shaped(count, NX * NY, NZ), shap...  5.38 us
    pallas_call x4, Pallas kernels, local(): pl.pallas_call(lambda *refs: local_kernel(index, *refs), out_shape=field,...  4.81 us
    pallas_call x3, Pallas kernels, body(): pl.pallas_call(step_kernel, out_shape=outs, in_specs=[SMEM] + [VMEM] * 12...  4.01 us
  transfers between devices with their start and end apart: 24, of which 0 were waited for; matrix products, arithmetic and copies ran while one was open for 0% of the time, Pallas kernels for 16%

profile of v3, /device:TPU:1, one launch (start us, length us, event | category | flops | bytes accessed | tf_op | source)
XLA Modules:
  0.0 86.8 jit_solution(12135674624745701789)
XLA Ops:
  0.7 0.1 stack.39
  0.8 2.3 %pack.1 = (f32[4,8,8,8,128]{4,3,2,1,0:T(8,128)S(1)}, f32[37,8,128]{2,1,0:T(8,128)S(1)}, f32[37,8,128]{2,1,0:T(8,128)S(1)}, f32[37,8,128]{2,1,0:T(8,128)S(1)}, f3...) custom-call(s32[9]{0:T(128)S(1)} %convert_element_type.3.place, ...), custom_call_target="tpu_custom_call" | custom-call | tf_op jit(solution)/shard_map/pack/pallas_call | solution.py:481
  3.1 2.1 %collective-permute-start = (f32[37,8,128]{2,1,0:T(8,128)S(1)}, f32[37,8,128]{2,1,0:T(8,128)S(1)}, u32[]{:S(2)}, u32[]{:S(2)}) collective-permute-start(f32[37,8,128]{2,1,0:T(8,128)S(1)} %get-tuple-element.57), channel_id=1, source_target_pairs={{0,64},{64,0},{128,192},{192,128},{1,65},{65,1},{129,193},{193,129... | collective-permute-start | bytes 454664 | tf_op jit(solution)/shard_map/ppermute | solution.py:464
  5.2 1.8 %collective-permute-start.1 = (f32[37,8,128]{2,1,0:T(8,128)S(1)}, f32[37,8,128]{2,1,0:T(8,128)S(1)}, u32[]{:S(2)}, u32[]{:S(2)}) collective-permute-start(f32[37,8,128]{2,1,0:T(8,128)S(1)} %get-tuple-element.58), channel_id=1, source_target_pairs={{0,192},{64,128},{128,64},{192,0},{1,193},{65,129},{129,65},{193,1... | collective-permute-start | bytes 454664 | tf_op jit(solution)/shard_map/ppermute | solution.py:465
  7.0 1.6 %collective-permute-start.2 = (f32[37,8,128]{2,1,0:T(8,128)S(1)}, f32[37,8,128]{2,1,0:T(8,128)S(1)}, u32[]{:S(2)}, u32[]{:S(2)}) collective-permute-start(f32[37,8,128]{2,1,0:T(8,128)S(1)} %get-tuple-element.59), channel_id=1, source_target_pairs={{0,8},{8,0},{16,24},{24,16},{32,40},{40,32},{48,56},{56,48},{1,9},... | collective-permute-start | bytes 454664 | tf_op jit(solution)/shard_map/ppermute | solution.py:464
  8.6 4.7 %collective-permute-start.3 = (f32[37,8,128]{2,1,0:T(8,128)S(1)}, f32[37,8,128]{2,1,0:T(8,128)S(1)}, u32[]{:S(2)}, u32[]{:S(2)}) collective-permute-start(f32[37,8,128]{2,1,0:T(8,128)S(1)} %get-tuple-element.60), channel_id=1, source_target_pairs={{0,56},{8,16},{16,8},{24,32},{32,24},{40,48},{48,40},{56,0},{1,57}... | collective-permute-start | bytes 454664 | tf_op jit(solution)/shard_map/ppermute | solution.py:465
  13.3 3.0 %collective-permute-start.5 = (f32[37,8,128]{2,1,0:T(8,128)S(1)}, f32[37,8,128]{2,1,0:T(8,128)S(1)}, u32[]{:S(2)}, u32[]{:S(2)}) collective-permute-start(f32[37,8,128]{2,1,0:T(8,128)S(1)} %get-tuple-element.61), channel_id=1, source_target_pairs={{0,7},{1,2},{2,1},{3,4},{4,3},{5,6},{6,5},{7,0},{8,15},{9,10},{10,... | collective-permute-start | bytes 454664 | tf_op jit(solution)/shard_map/ppermute | solution.py:465
  16.3 0.0 collective-permute-done.refs_0_
  16.3 0.2 collective-permute-start.4
  16.4 0.7 copy-done
  17.1 1.9 %prepare.1 = (f32[2048,128]{1,0:T(8,128)S(1)}, f32[8,8,8,128]{3,2,1,0:T(8,128)S(1)}, f32[8,8,8,128]{3,2,1,0:T(8,128)S(1)}, f32[8,8,8,128]{3,2,1,0:T(8,128)S(1)},...) custom-call(f32[3,6]{1,0:T(4,128)S(1)} %copy-done, f32[5,8,8,128]{3,2,1,0:T(8,128)S(1)} %get-tuple-element.51.pm.inner, ...), custom_call_target="tpu_custom_call" | custom-call | tf_op jit(solution)/shard_map/prepare/pallas_call | solution.py:518
  19.0 1.2 %local1.1.part = f32[4,8,8,8,128]{4,3,2,1,0:T(8,128)S(1)} custom-call(f32[4,8,8,8,128]{4,3,2,1,0:T(8,128)S(1)} %get-tuple-element.50.refs_0_.cur.v0, f32[8,8,8,128]{3,2,1,0:T(8,128)S(1)} %get-tuple-element.52.refs_1_, f32[8,8,8,128]{3,2,1,0:T(8,128)S(1)} %get-tuple-element.53.refs_2_, f32[8,8,8,128]{3,2,1,0:T(8,128)S(1)} %get-tuple-element.54.refs_3_, ...), custom_call_target="tpu_custom_call" | custom-call | flops 6291456 | bytes 3145728 | tf_op jit(solution)/shard_map/local1/pallas_call | solution.py:529
  20.3 0.0 collective-permute-done.1.refs_1_
  20.3 0.0 collective-permute-done.2.refs_2_
  20.3 0.0 collective-permute-done.3.refs_3_
  20.3 0.0 collective-permute-done.5.refs_5_
  20.3 0.0 collective-permute-done.4.refs_4_
  20.3 1.5 %step1.1 = (f32[4,8,8,8,128]{4,3,2,1,0:T(8,128)S(1)}, f32[32,8,128]{2,1,0:T(8,128)S(1)}, f32[32,8,128]{2,1,0:T(8,128)S(1)}, f32[32,8,128]{2,1,0:T(8,128)S(1)}, f...) custom-call(s32[9]{0:T(128)S(1)} %convert_element_type.3.place, ...), custom_call_target="tpu_custom_call" | custom-call | tf_op jit(solution)/shard_map/step1/pallas_call | solution.py:543
  21.9 0.4 collective-permute-start.6
  22.3 0.6 collective-permute-start.7
  22.9 0.0 collective-permute-start.8
  22.9 2.3 %collective-permute-start.9 = (f32[32,8,128]{2,1,0:T(8,128)S(1)}, f32[32,8,128]{2,1,0:T(8,128)S(1)}, u32[]{:S(2)}, u32[]{:S(2)}) collective-permute-start(f32[32,8,128]{2,1,0:T(8,128)S(1)} %get-tuple-element.69), channel_id=1, source_target_pairs={{0,56},{8,16},{16,8},{24,32},{32,24},{40,48},{48,40},{56,0},{1,57}... | collective-permute-start | bytes 393224 | tf_op jit(solution)/shard_map/ppermute | solution.py:465
  25.2 2.3 %collective-permute-start.11 = (f32[32,8,128]{2,1,0:T(8,128)S(1)}, f32[32,8,128]{2,1,0:T(8,128)S(1)}, u32[]{:S(2)}, u32[]{:S(2)}) collective-permute-start(f32[32,8,128]{2,1,0:T(8,128)S(1)} %get-tuple-element.70), channel_id=1, source_target_pairs={{0,7},{1,2},{2,1},{3,4},{4,3},{5,6},{6,5},{7,0},{8,15},{9,10},{10,... | collective-permute-start | bytes 393224 | tf_op jit(solution)/shard_map/ppermute | solution.py:465
  27.5 0.0 collective-permute-done.6.refs_0_
  27.5 0.8 collective-permute-start.10
  28.3 1.4 %gram0.1 = (bf16[4,8,8,16,128]{4,3,2,1,0:T(8,128)(2,1)S(1)}, f32[8,128]{1,0:T(8,128)S(1)}) custom-call(f32[4,8,8,8,128]{4,3,2,1,0:T(8,128)S(1)} %get-tuple-element.50.refs_0_.cur.v0), custom_call_target="tpu_custom_call" | custom-call | flops 16777216 | bytes 3145728 | tf_op jit(solution)/shard_map/gram0/pallas_call | solution.py:499
  29.7 1.2 %local2.1.part = f32[4,8,8,8,128]{4,3,2,1,0:T(8,128)S(1)} custom-call(f32[4,8,8,8,128]{4,3,2,1,0:T(8,128)S(1)} %get-tuple-element.62.refs_0_.cur, f32[8,8,8,128]{3,2,1,0:T(8,128)S(1)} %get-tuple-element.52.refs_1_, f32[8,8,8,128]{3,2,1,0:T(8,128)S(1)} %get-tuple-element.53.refs_2_, f32[8,8,8,128]{3,2,1,0:T(8,128)S(1)} %get-tuple-element.54.refs_3_, ...), custom_call_target="tpu_custom_call" | custom-call | flops 6291456 | bytes 3145728 | tf_op jit(solution)/shard_map/local2/pallas_call | solution.py:529
  30.9 1.8 %gram1.1 = (bf16[4,8,8,16,128]{4,3,2,1,0:T(8,128)(2,1)S(1)}, f32[8,128]{1,0:T(8,128)S(1)}) custom-call(f32[4,8,8,8,128]{4,3,2,1,0:T(8,128)S(1)} %get-tuple-element.62.refs_0_.cur, bf16[4,8,8,16,128]{4,3,2,1,0:T(8,128)(2,1)S(1)} %get-tuple-element.63.refs_1_.s0, f32[8,128]{1,0:T(8,128)S(1)} %get-tuple-element.64.refs_2_), custom_call_target="tpu_custom_call" | custom-call | flops 33554432 | bytes 4194304 | tf_op jit(solution)/shard_map/gram1/pallas_call | solution.py:499
  32.7 0.0 collective-permute-done.7.refs_1_
  32.7 0.0 collective-permute-done.8.refs_2_
  32.7 0.0 collective-permute-done.9.refs_3_
  32.7 0.0 collective-permute-done.11.refs_5_
  32.7 1.5 %step2.1 = (f32[4,8,8,8,128]{4,3,2,1,0:T(8,128)S(1)}, f32[32,8,128]{2,1,0:T(8,128)S(1)}, f32[32,8,128]{2,1,0:T(8,128)S(1)}, f32[32,8,128]{2,1,0:T(8,128)S(1)}, f...) custom-call(s32[9]{0:T(128)S(1)} %convert_element_type.3.place, f32[8,128]{1,0:T(8,128)S(1)} %get-tuple-element.65.piece.refs_3_, ...), custom_call_target="tpu_custom_call" | custom-call | tf_op jit(solution)/shard_map/step2/pallas_call | solution.py:558
  34.2 0.4 collective-permute-start.12
  34.6 1.0 %collective-permute-start.13 = (f32[32,8,128]{2,1,0:T(8,128)S(1)}, f32[32,8,128]{2,1,0:T(8,128)S(1)}, u32[]{:S(2)}, u32[]{:S(2)}) collective-permute-start(f32[32,8,128]{2,1,0:T(8,128)S(1)} %get-tuple-element.78), channel_id=1, source_target_pairs={{0,192},{64,128},{128,64},{192,0},{1,193},{65,129},{129,65},{193,1... | collective-permute-start | bytes 393224 | tf_op jit(solution)/shard_map/ppermute | solution.py:465
  35.6 0.7 collective-permute-start.14
  36.4 0.7 collective-permute-start.15
  37.1 2.6 %collective-permute-start.17 = (f32[32,8,128]{2,1,0:T(8,128)S(1)}, f32[32,8,128]{2,1,0:T(8,128)S(1)}, u32[]{:S(2)}, u32[]{:S(2)}) collective-permute-start(f32[32,8,128]{2,1,0:T(8,128)S(1)} %get-tuple-element.81), channel_id=1, source_target_pairs={{0,7},{1,2},{2,1},{3,4},{4,3},{5,6},{6,5},{7,0},{8,15},{9,10},{10,... | collective-permute-start | bytes 393224 | tf_op jit(solution)/shard_map/ppermute | solution.py:465
  39.7 0.0 collective-permute-done.12.refs_0_
  39.7 0.5 collective-permute-start.16
  40.2 1.2 %local3.1.part = f32[4,8,8,8,128]{4,3,2,1,0:T(8,128)S(1)} custom-call(f32[4,8,8,8,128]{4,3,2,1,0:T(8,128)S(1)} %get-tuple-element.74.refs_0_.cur, f32[8,8,8,128]{3,2,1,0:T(8,128)S(1)} %get-tuple-element.52.refs_1_, f32[8,8,8,128]{3,2,1,0:T(8,128)S(1)} %get-tuple-element.53.refs_2_, f32[8,8,8,128]{3,2,1,0:T(8,128)S(1)} %get-tuple-element.54.refs_3_, ...), custom_call_target="tpu_custom_call" | custom-call | flops 6291456 | bytes 3145728 | tf_op jit(solution)/shard_map/local3/pallas_call | solution.py:529
  41.4 2.1 %gram2.1 = (bf16[4,8,8,16,128]{4,3,2,1,0:T(8,128)(2,1)S(1)}, f32[8,128]{1,0:T(8,128)S(1)}) custom-call(f32[4,8,8,8,128]{4,3,2,1,0:T(8,128)S(1)} %get-tuple-element.74.refs_0_.cur, bf16[4,8,8,16,128]{4,3,2,1,0:T(8,128)(2,1)S(1)} %get-tuple-element.63.refs_1_.s0, bf16[4,8,8,16,128]{4,3,2,1,0:T(8,128)(2,1)S(1)} %get-tuple-element.75.refs_2_.s1, ...), custom_call_target="tpu_custom_call" | custom-call | flops 50331648 | bytes 5242880 | tf_op jit(solution)/shard_map/gram2/pallas_call | solution.py:499
  43.5 0.0 collective-permute-done.13.refs_1_
  43.5 0.0 collective-permute-done.15.refs_3_
  43.5 0.0 collective-permute-done.16.refs_4_
  43.6 1.5 %step3.1 = (f32[4,8,8,8,128]{4,3,2,1,0:T(8,128)S(1)}, f32[32,8,128]{2,1,0:T(8,128)S(1)}, f32[32,8,128]{2,1,0:T(8,128)S(1)}, f32[32,8,128]{2,1,0:T(8,128)S(1)}, f...) custom-call(s32[9]{0:T(128)S(1)} %convert_element_type.3.place, f32[8,128]{1,0:T(8,128)S(1)} %get-tuple-element.76.piece.refs_4_, ...), custom_call_target="tpu_custom_call" | custom-call | tf_op jit(solution)/shard_map/step3/pallas_call | solution.py:558
  45.0 0.4 collective-permute-start.18
  45.4 1.0 %collective-permute-start.19 = (f32[32,8,128]{2,1,0:T(8,128)S(1)}, f32[32,8,128]{2,1,0:T(8,128)S(1)}, u32[]{:S(2)}, u32[]{:S(2)}) collective-permute-start(f32[32,8,128]{2,1,0:T(8,128)S(1)} %get-tuple-element.86), channel_id=1, source_target_pairs={{0,192},{64,128},{128,64},{192,0},{1,193},{65,129},{129,65},{193,1... | collective-permute-start | bytes 393224 | tf_op jit(solution)/shard_map/ppermute | solution.py:465
  46.4 0.7 collective-permute-start.20
  47.2 0.7 collective-permute-start.21
  47.9 2.3 %collective-permute-start.23 = (f32[32,8,128]{2,1,0:T(8,128)S(1)}, f32[32,8,128]{2,1,0:T(8,128)S(1)}, u32[]{:S(2)}, u32[]{:S(2)}) collective-permute-start(f32[32,8,128]{2,1,0:T(8,128)S(1)} %get-tuple-element.89), channel_id=1, source_target_pairs={{0,7},{1,2},{2,1},{3,4},{4,3},{5,6},{6,5},{7,0},{8,15},{9,10},{10,... | collective-permute-start | bytes 393224 | tf_op jit(solution)/shard_map/ppermute | solution.py:465
  50.2 0.0 collective-permute-done.18.refs_0_
  50.2 0.8 collective-permute-start.22
  51.0 1.2 %local4.1.part = f32[4,8,8,8,128]{4,3,2,1,0:T(8,128)S(1)} custom-call(f32[4,8,8,8,128]{4,3,2,1,0:T(8,128)S(1)} %get-tuple-element.82.refs_0_.cur, f32[8,8,8,128]{3,2,1,0:T(8,128)S(1)} %get-tuple-element.52.refs_1_, f32[8,8,8,128]{3,2,1,0:T(8,128)S(1)} %get-tuple-element.53.refs_2_, f32[8,8,8,128]{3,2,1,0:T(8,128)S(1)} %get-tuple-element.54.refs_3_, ...), custom_call_target="tpu_custom_call" | custom-call | flops 6291456 | bytes 3145728 | tf_op jit(solution)/shard_map/local4/pallas_call | solution.py:529
  52.3 2.3 %gram3.1 = (bf16[4,8,8,16,128]{4,3,2,1,0:T(8,128)(2,1)S(1)}, f32[8,128]{1,0:T(8,128)S(1)}) custom-call(f32[4,8,8,8,128]{4,3,2,1,0:T(8,128)S(1)} %get-tuple-element.82.refs_0_.cur, bf16[4,8,8,16,128]{4,3,2,1,0:T(8,128)(2,1)S(1)} %get-tuple-element.63.refs_1_.s0, bf16[4,8,8,16,128]{4,3,2,1,0:T(8,128)(2,1)S(1)} %get-tuple-element.75.refs_2_.s1, ...), custom_call_target="tpu_custom_call" | custom-call | flops 67108864 | bytes 6291456 | tf_op jit(solution)/shard_map/gram3/pallas_call | solution.py:499
  54.6 0.0 collective-permute-done.19.refs_1_
  54.6 0.0 collective-permute-done.20.refs_2_
  54.6 0.0 collective-permute-done.21.refs_3_
  54.6 0.0 collective-permute-done.22.refs_4_
  54.6 1.0 %step4.1.refs_0_ = f32[4,8,8,8,128]{4,3,2,1,0:T(8,128)S(1)} custom-call(s32[9]{0:T(128)S(1)} %convert_element_type.3.place, f32[8,128]{1,0:T(8,128)S(1)} %get-tuple-element.84.piece.refs_2_, f32[4,8,8,8,128]{4,3,2,1,0:T(8,128)S(1)} %local4.1.part, f32[4,8,8,8,128]{4,3,2,1,0:T(8,128)S(1)} %get-tuple-element.82.refs_0_.cur, ...), custom_call_target="tpu_custom_call" | custom-call | tf_op jit(solution)/shard_map/step4/pallas_call | solution.py:558
  55.7 1.5 %gram4.1 = (bf16[4,8,8,16,128]{4,3,2,1,0:T(8,128)(2,1)S(1)}, f32[32,8,128]{2,1,0:T(8,128)S(1)}) custom-call(f32[4,8,8,8,128]{4,3,2,1,0:T(8,128)S(1)} %step4.1.refs_0_, bf16[4,8,8,16,128]{4,3,2,1,0:T(8,128)(2,1)S(1)} %get-tuple-element.90.refs_1_.s3, f32[8,128]{1,0:T(8,128)S(1)} %get-tuple-element.84.piece.refs_2_), custom_call_target="tpu_custom_call" | custom-call | flops 83886080 | bytes 7340032 | tf_op jit(solution)/shard_map/gram4/pallas_call | solution.py:499
  57.2 12.9 %all_to_all.10.parts = f32[32,8,128]{2,1,0:T(8,128)S(1)} all-to-all(f32[32,8,128]{2,1,0:T(8,128)S(1)} %get-tuple-element.91), channel_id=1, replica_groups=mesh['gx'=4,'gy'=8,'gz'=8] {'gx','gz'}, dimensions={0} | all-to-all | bytes 262144 | tf_op jit(solution)/shard_map/all_to_all | solution.py:569
  70.1 11.1 %all_to_all.11.packed = f32[8,8,128]{2,1,0:T(8,128)S(1)} all-to-all(f32[8,8,128]{2,1,0:T(8,128)S(1)} %relay.1), channel_id=1, replica_groups=mesh['gx'=4,'gy'=8,'gz'=8] {'gy'}, dimensions={0} | all-to-all | bytes 65536 | tf_op jit(solution)/shard_map/all_to_all | solution.py:578
  81.3 5.4 %finish.1 = (f32[32,64,128]{2,1,0:T(8,128)}, f32[32,64,128]{2,1,0:T(8,128)}, f32[128,64,128]{2,1,0:T(8,128)}) custom-call(f32[8,8,128]{2,1,0:T(8,128)S(1)} %all_to_all.11.packed, bf16[4,8,8,16,128]{4,3,2,1,0:T(8,128)(2,1)S(1)} %get-tuple-element.63.refs_1_.s0, bf16[4,8,8,16,128]{4,3,2,1,0:T(8,128)(2,1)S(1)} %get-tuple-element.75.refs_2_.s1, ...), custom_call_target="tpu_custom_call" | custom-call | tf_op jit(solution)/shard_map/finish/pallas_call | solution.py:580
  (7 shorter events, 0.1 us)
Async XLA Ops:
  3.1 13.2 %collective-permute-start = (f32[37,8,128]{2,1,0:T(8,128)S(1)}, f32[37,8,128]{2,1,0:T(8,128)S(1)}, u32[]{:S(2)}, u32[]{:S(2)}) collective-permute-start(f32[37,8,128]{2,1,0:T(8,128)S(1)} %get-tuple-element.57), channel_id=1, source_target_pairs={{0,64},{64,0},{128,192},{192,128},{1,65},{65,1},{129,193},{193,129... | collective-permute-start | bytes 454664 | tf_op jit(solution)/shard_map/ppermute | solution.py:464
  5.2 15.1 %collective-permute-start.1 = (f32[37,8,128]{2,1,0:T(8,128)S(1)}, f32[37,8,128]{2,1,0:T(8,128)S(1)}, u32[]{:S(2)}, u32[]{:S(2)}) collective-permute-start(f32[37,8,128]{2,1,0:T(8,128)S(1)} %get-tuple-element.58), channel_id=1, source_target_pairs={{0,192},{64,128},{128,64},{192,0},{1,193},{65,129},{129,65},{193,1... | collective-permute-start | bytes 454664 | tf_op jit(solution)/shard_map/ppermute | solution.py:465
  7.0 13.3 %collective-permute-start.2 = (f32[37,8,128]{2,1,0:T(8,128)S(1)}, f32[37,8,128]{2,1,0:T(8,128)S(1)}, u32[]{:S(2)}, u32[]{:S(2)}) collective-permute-start(f32[37,8,128]{2,1,0:T(8,128)S(1)} %get-tuple-element.59), channel_id=1, source_target_pairs={{0,8},{8,0},{16,24},{24,16},{32,40},{40,32},{48,56},{56,48},{1,9},... | collective-permute-start | bytes 454664 | tf_op jit(solution)/shard_map/ppermute | solution.py:464
  8.6 11.6 %collective-permute-start.3 = (f32[37,8,128]{2,1,0:T(8,128)S(1)}, f32[37,8,128]{2,1,0:T(8,128)S(1)}, u32[]{:S(2)}, u32[]{:S(2)}) collective-permute-start(f32[37,8,128]{2,1,0:T(8,128)S(1)} %get-tuple-element.60), channel_id=1, source_target_pairs={{0,56},{8,16},{16,8},{24,32},{32,24},{40,48},{48,40},{56,0},{1,57}... | collective-permute-start | bytes 454664 | tf_op jit(solution)/shard_map/ppermute | solution.py:465
  13.3 7.0 %collective-permute-start.5 = (f32[37,8,128]{2,1,0:T(8,128)S(1)}, f32[37,8,128]{2,1,0:T(8,128)S(1)}, u32[]{:S(2)}, u32[]{:S(2)}) collective-permute-start(f32[37,8,128]{2,1,0:T(8,128)S(1)} %get-tuple-element.61), channel_id=1, source_target_pairs={{0,7},{1,2},{2,1},{3,4},{4,3},{5,6},{6,5},{7,0},{8,15},{9,10},{10,... | collective-permute-start | bytes 454664 | tf_op jit(solution)/shard_map/ppermute | solution.py:465
  16.3 4.0 %collective-permute-start.4 = (f32[37,8,128]{2,1,0:T(8,128)S(1)}, f32[37,8,128]{2,1,0:T(8,128)S(1)}, u32[]{:S(2)}, u32[]{:S(2)}) collective-permute-start(f32[37,8,128]{2,1,0:T(8,128)S(1)} %get-tuple-element.61), channel_id=1, source_target_pairs={{0,1},{1,0},{2,3},{3,2},{4,5},{5,4},{6,7},{7,6},{8,9},{9,8},{10,11... | collective-permute-start | bytes 454664 | tf_op jit(solution)/shard_map/ppermute | solution.py:464
  16.4 0.7 copy-start
  21.9 5.6 %collective-permute-start.6 = (f32[32,8,128]{2,1,0:T(8,128)S(1)}, f32[32,8,128]{2,1,0:T(8,128)S(1)}, u32[]{:S(2)}, u32[]{:S(2)}) collective-permute-start(f32[32,8,128]{2,1,0:T(8,128)S(1)} %get-tuple-element.66), channel_id=1, source_target_pairs={{0,64},{64,0},{128,192},{192,128},{1,65},{65,1},{129,193},{193,129... | collective-permute-start | bytes 393224 | tf_op jit(solution)/shard_map/ppermute | solution.py:464
  22.3 10.4 %collective-permute-start.7 = (f32[32,8,128]{2,1,0:T(8,128)S(1)}, f32[32,8,128]{2,1,0:T(8,128)S(1)}, u32[]{:S(2)}, u32[]{:S(2)}) collective-permute-start(f32[32,8,128]{2,1,0:T(8,128)S(1)} %get-tuple-element.67), channel_id=1, source_target_pairs={{0,192},{64,128},{128,64},{192,0},{1,193},{65,129},{129,65},{193,1... | collective-permute-start | bytes 393224 | tf_op jit(solution)/shard_map/ppermute | solution.py:465
  22.9 9.8 %collective-permute-start.8 = (f32[32,8,128]{2,1,0:T(8,128)S(1)}, f32[32,8,128]{2,1,0:T(8,128)S(1)}, u32[]{:S(2)}, u32[]{:S(2)}) collective-permute-start(f32[32,8,128]{2,1,0:T(8,128)S(1)} %get-tuple-element.68), channel_id=1, source_target_pairs={{0,8},{8,0},{16,24},{24,16},{32,40},{40,32},{48,56},{56,48},{1,9},... | collective-permute-start | bytes 393224 | tf_op jit(solution)/shard_map/ppermute | solution.py:464
  22.9 9.8 %collective-permute-start.9 = (f32[32,8,128]{2,1,0:T(8,128)S(1)}, f32[32,8,128]{2,1,0:T(8,128)S(1)}, u32[]{:S(2)}, u32[]{:S(2)}) collective-permute-start(f32[32,8,128]{2,1,0:T(8,128)S(1)} %get-tuple-element.69), channel_id=1, source_target_pairs={{0,56},{8,16},{16,8},{24,32},{32,24},{40,48},{48,40},{56,0},{1,57}... | collective-permute-start | bytes 393224 | tf_op jit(solution)/shard_map/ppermute | solution.py:465
  25.2 7.6 %collective-permute-start.11 = (f32[32,8,128]{2,1,0:T(8,128)S(1)}, f32[32,8,128]{2,1,0:T(8,128)S(1)}, u32[]{:S(2)}, u32[]{:S(2)}) collective-permute-start(f32[32,8,128]{2,1,0:T(8,128)S(1)} %get-tuple-element.70), channel_id=1, source_target_pairs={{0,7},{1,2},{2,1},{3,4},{4,3},{5,6},{6,5},{7,0},{8,15},{9,10},{10,... | collective-permute-start | bytes 393224 | tf_op jit(solution)/shard_map/ppermute | solution.py:465
  27.5 5.3 %collective-permute-start.10 = (f32[32,8,128]{2,1,0:T(8,128)S(1)}, f32[32,8,128]{2,1,0:T(8,128)S(1)}, u32[]{:S(2)}, u32[]{:S(2)}) collective-permute-start(f32[32,8,128]{2,1,0:T(8,128)S(1)} %get-tuple-element.70), channel_id=1, source_target_pairs={{0,1},{1,0},{2,3},{3,2},{4,5},{5,4},{6,7},{7,6},{8,9},{9,8},{10,11... | collective-permute-start | bytes 393224 | tf_op jit(solution)/shard_map/ppermute | solution.py:464
  34.2 5.5 %collective-permute-start.12 = (f32[32,8,128]{2,1,0:T(8,128)S(1)}, f32[32,8,128]{2,1,0:T(8,128)S(1)}, u32[]{:S(2)}, u32[]{:S(2)}) collective-permute-start(f32[32,8,128]{2,1,0:T(8,128)S(1)} %get-tuple-element.77), channel_id=1, source_target_pairs={{0,64},{64,0},{128,192},{192,128},{1,65},{65,1},{129,193},{193,129... | collective-permute-start | bytes 393224 | tf_op jit(solution)/shard_map/ppermute | solution.py:464
  34.6 8.9 %collective-permute-start.13 = (f32[32,8,128]{2,1,0:T(8,128)S(1)}, f32[32,8,128]{2,1,0:T(8,128)S(1)}, u32[]{:S(2)}, u32[]{:S(2)}) collective-permute-start(f32[32,8,128]{2,1,0:T(8,128)S(1)} %get-tuple-element.78), channel_id=1, source_target_pairs={{0,192},{64,128},{128,64},{192,0},{1,193},{65,129},{129,65},{193,1... | collective-permute-start | bytes 393224 | tf_op jit(solution)/shard_map/ppermute | solution.py:465
  35.6 7.9 %collective-permute-start.14 = (f32[32,8,128]{2,1,0:T(8,128)S(1)}, f32[32,8,128]{2,1,0:T(8,128)S(1)}, u32[]{:S(2)}, u32[]{:S(2)}) collective-permute-start(f32[32,8,128]{2,1,0:T(8,128)S(1)} %get-tuple-element.79), channel_id=1, source_target_pairs={{0,8},{8,0},{16,24},{24,16},{32,40},{40,32},{48,56},{56,48},{1,9},... | collective-permute-start | bytes 393224 | tf_op jit(solution)/shard_map/ppermute | solution.py:464
  36.4 7.2 %collective-permute-start.15 = (f32[32,8,128]{2,1,0:T(8,128)S(1)}, f32[32,8,128]{2,1,0:T(8,128)S(1)}, u32[]{:S(2)}, u32[]{:S(2)}) collective-permute-start(f32[32,8,128]{2,1,0:T(8,128)S(1)} %get-tuple-element.80), channel_id=1, source_target_pairs={{0,56},{8,16},{16,8},{24,32},{32,24},{40,48},{48,40},{56,0},{1,57}... | collective-permute-start | bytes 393224 | tf_op jit(solution)/shard_map/ppermute | solution.py:465
  37.1 6.4 %collective-permute-start.17 = (f32[32,8,128]{2,1,0:T(8,128)S(1)}, f32[32,8,128]{2,1,0:T(8,128)S(1)}, u32[]{:S(2)}, u32[]{:S(2)}) collective-permute-start(f32[32,8,128]{2,1,0:T(8,128)S(1)} %get-tuple-element.81), channel_id=1, source_target_pairs={{0,7},{1,2},{2,1},{3,4},{4,3},{5,6},{6,5},{7,0},{8,15},{9,10},{10,... | collective-permute-start | bytes 393224 | tf_op jit(solution)/shard_map/ppermute | solution.py:465
  39.7 3.8 %collective-permute-start.16 = (f32[32,8,128]{2,1,0:T(8,128)S(1)}, f32[32,8,128]{2,1,0:T(8,128)S(1)}, u32[]{:S(2)}, u32[]{:S(2)}) collective-permute-start(f32[32,8,128]{2,1,0:T(8,128)S(1)} %get-tuple-element.81), channel_id=1, source_target_pairs={{0,1},{1,0},{2,3},{3,2},{4,5},{5,4},{6,7},{7,6},{8,9},{9,8},{10,11... | collective-permute-start | bytes 393224 | tf_op jit(solution)/shard_map/ppermute | solution.py:464
  45.0 5.2 %collective-permute-start.18 = (f32[32,8,128]{2,1,0:T(8,128)S(1)}, f32[32,8,128]{2,1,0:T(8,128)S(1)}, u32[]{:S(2)}, u32[]{:S(2)}) collective-permute-start(f32[32,8,128]{2,1,0:T(8,128)S(1)} %get-tuple-element.85), channel_id=1, source_target_pairs={{0,64},{64,0},{128,192},{192,128},{1,65},{65,1},{129,193},{193,129... | collective-permute-start | bytes 393224 | tf_op jit(solution)/shard_map/ppermute | solution.py:464
  45.4 9.2 %collective-permute-start.19 = (f32[32,8,128]{2,1,0:T(8,128)S(1)}, f32[32,8,128]{2,1,0:T(8,128)S(1)}, u32[]{:S(2)}, u32[]{:S(2)}) collective-permute-start(f32[32,8,128]{2,1,0:T(8,128)S(1)} %get-tuple-element.86), channel_id=1, source_target_pairs={{0,192},{64,128},{128,64},{192,0},{1,193},{65,129},{129,65},{193,1... | collective-permute-start | bytes 393224 | tf_op jit(solution)/shard_map/ppermute | solution.py:465
  46.4 8.2 %collective-permute-start.20 = (f32[32,8,128]{2,1,0:T(8,128)S(1)}, f32[32,8,128]{2,1,0:T(8,128)S(1)}, u32[]{:S(2)}, u32[]{:S(2)}) collective-permute-start(f32[32,8,128]{2,1,0:T(8,128)S(1)} %get-tuple-element.87), channel_id=1, source_target_pairs={{0,8},{8,0},{16,24},{24,16},{32,40},{40,32},{48,56},{56,48},{1,9},... | collective-permute-start | bytes 393224 | tf_op jit(solution)/shard_map/ppermute | solution.py:464
  47.2 7.4 %collective-permute-start.21 = (f32[32,8,128]{2,1,0:T(8,128)S(1)}, f32[32,8,128]{2,1,0:T(8,128)S(1)}, u32[]{:S(2)}, u32[]{:S(2)}) collective-permute-start(f32[32,8,128]{2,1,0:T(8,128)S(1)} %get-tuple-element.88), channel_id=1, source_target_pairs={{0,56},{8,16},{16,8},{24,32},{32,24},{40,48},{48,40},{56,0},{1,57}... | collective-permute-start | bytes 393224 | tf_op jit(solution)/shard_map/ppermute | solution.py:465
  47.9 6.7 %collective-permute-start.23 = (f32[32,8,128]{2,1,0:T(8,128)S(1)}, f32[32,8,128]{2,1,0:T(8,128)S(1)}, u32[]{:S(2)}, u32[]{:S(2)}) collective-permute-start(f32[32,8,128]{2,1,0:T(8,128)S(1)} %get-tuple-element.89), channel_id=1, source_target_pairs={{0,7},{1,2},{2,1},{3,4},{4,3},{5,6},{6,5},{7,0},{8,15},{9,10},{10,... | collective-permute-start | bytes 393224 | tf_op jit(solution)/shard_map/ppermute | solution.py:465
  50.2 4.4 %collective-permute-start.22 = (f32[32,8,128]{2,1,0:T(8,128)S(1)}, f32[32,8,128]{2,1,0:T(8,128)S(1)}, u32[]{:S(2)}, u32[]{:S(2)}) collective-permute-start(f32[32,8,128]{2,1,0:T(8,128)S(1)} %get-tuple-element.89), channel_id=1, source_target_pairs={{0,1},{1,0},{2,3},{3,2},{4,5},{5,4},{6,7},{7,6},{8,9},{9,8},{10,11... | collective-permute-start | bytes 393224 | tf_op jit(solution)/shard_map/ppermute | solution.py:464

commit v4 on v3

--- a/solution.py
+++ b/solution.py
@@ -492,7 +492,7 @@
         name="pack",
     )(edge, far(flat), far(permeability), far(tissue_mask))
 
-    wide, tall = lax.axis_size("gx") * lax.axis_size("gz"), lax.axis_size("gy")
+    tall, wide = lax.axis_size("gx") * lax.axis_size("gz"), lax.axis_size("gy")
 
     def gram(index, current, older, before):
         inputs = [current, *(older if index < S else older[-1:]), *before]
@@ -566,7 +566,7 @@
         current, sends = results[0], results[1:]
     split, piece = gram(S, current, splits, [piece])
     splits.append(split)
-    parts = lax.all_to_all(piece, ("gx", "gz"), 0, 0)
+    parts = lax.all_to_all(piece, ("gy",), 0, 0)
     parts = pl.pallas_call(
         relay_kernel,
         out_shape=near(tall, 8, NZ),
@@ -575,7 +575,7 @@
         compiler_params=params(2),
         name="relay",
     )(parts)
-    packed = lax.all_to_all(parts, ("gy",), 0, 0)
+    packed = lax.all_to_all(parts, ("gx", "gz"), 0, 0)
     count = COMP * RHS
     new_sol, new_res, basis = pl.pallas_call(
         finish_kernel,

time: 87 us -> 88.4 us (1.016)
  blocking collectives: 24.1 us -> 25.4 us
    all_to_all x2, blocking collectives: 24.1 us -> 25.4 us  [the longest x1 14.2 us: body(): packed = lax.all_to_all(parts, ('gx', 'gz'), 0, 0)]
where the time goes in v4:
time: 88.4 us; the launch traced here: 88.2 us
  starting transfers between devices  31.8 us (36%)
  Pallas kernels  29 us (33%)
  blocking collectives  25.4 us (29%)
  between operations  1.05 us (1%)
    ppermute x12, starting transfers between devices, exchange(): moved.append(lax.ppermute(pair[1], axis, second))  23.1 us
    all_to_all x1, blocking collectives, body(): packed = lax.all_to_all(parts, ('gx', 'gz'), 0, 0)  14.2 us
    all_to_all x1, blocking collectives, body(): parts = lax.all_to_all(piece, ('gy',), 0, 0)  11.2 us
    pallas_call x5, Pallas kernels, gram(): pl.pallas_call(lambda *refs: gram_kernel(index, *refs), out_shape=(near(C...  9.07 us
    ppermute x12, starting transfers between devices, exchange(): moved.append(lax.ppermute(pair[0], axis, first))  8.72 us
    pallas_call x1, Pallas kernels, body(): pl.pallas_call(finish_kernel, out_shape=(shaped(count, NX * NY, NZ), shap...  5.42 us
    pallas_call x4, Pallas kernels, local(): pl.pallas_call(lambda *refs: local_kernel(index, *refs), out_shape=field,...  4.81 us
    pallas_call x3, Pallas kernels, body(): pl.pallas_call(step_kernel, out_shape=outs, in_specs=[SMEM] + [VMEM] * 12...  4.01 us
  transfers between devices with their start and end apart: 24, of which 0 were waited for; matrix products, arithmetic and copies ran while one was open for 0% of the time, Pallas kernels for 16%

profile of v4, /device:TPU:1, one launch (start us, length us, event | category | flops | bytes accessed | tf_op | source)
XLA Modules:
  0.0 88.2 jit_solution(3487691084908008055)
XLA Ops:
  0.7 0.1 stack.39
  0.8 2.3 %pack.1 = (f32[4,8,8,8,128]{4,3,2,1,0:T(8,128)S(1)}, f32[37,8,128]{2,1,0:T(8,128)S(1)}, f32[37,8,128]{2,1,0:T(8,128)S(1)}, f32[37,8,128]{2,1,0:T(8,128)S(1)}, f3...) custom-call(s32[9]{0:T(128)S(1)} %convert_element_type.3.place, ...), custom_call_target="tpu_custom_call" | custom-call | tf_op jit(solution)/shard_map/pack/pallas_call | solution.py:481
  3.1 2.1 %collective-permute-start = (f32[37,8,128]{2,1,0:T(8,128)S(1)}, f32[37,8,128]{2,1,0:T(8,128)S(1)}, u32[]{:S(2)}, u32[]{:S(2)}) collective-permute-start(f32[37,8,128]{2,1,0:T(8,128)S(1)} %get-tuple-element.57), channel_id=1, source_target_pairs={{0,64},{64,0},{128,192},{192,128},{1,65},{65,1},{129,193},{193,129... | collective-permute-start | bytes 454664 | tf_op jit(solution)/shard_map/ppermute | solution.py:464
  5.2 1.8 %collective-permute-start.1 = (f32[37,8,128]{2,1,0:T(8,128)S(1)}, f32[37,8,128]{2,1,0:T(8,128)S(1)}, u32[]{:S(2)}, u32[]{:S(2)}) collective-permute-start(f32[37,8,128]{2,1,0:T(8,128)S(1)} %get-tuple-element.58), channel_id=1, source_target_pairs={{0,192},{64,128},{128,64},{192,0},{1,193},{65,129},{129,65},{193,1... | collective-permute-start | bytes 454664 | tf_op jit(solution)/shard_map/ppermute | solution.py:465
  7.0 1.6 %collective-permute-start.2 = (f32[37,8,128]{2,1,0:T(8,128)S(1)}, f32[37,8,128]{2,1,0:T(8,128)S(1)}, u32[]{:S(2)}, u32[]{:S(2)}) collective-permute-start(f32[37,8,128]{2,1,0:T(8,128)S(1)} %get-tuple-element.59), channel_id=1, source_target_pairs={{0,8},{8,0},{16,24},{24,16},{32,40},{40,32},{48,56},{56,48},{1,9},... | collective-permute-start | bytes 454664 | tf_op jit(solution)/shard_map/ppermute | solution.py:464
  8.6 4.7 %collective-permute-start.3 = (f32[37,8,128]{2,1,0:T(8,128)S(1)}, f32[37,8,128]{2,1,0:T(8,128)S(1)}, u32[]{:S(2)}, u32[]{:S(2)}) collective-permute-start(f32[37,8,128]{2,1,0:T(8,128)S(1)} %get-tuple-element.60), channel_id=1, source_target_pairs={{0,56},{8,16},{16,8},{24,32},{32,24},{40,48},{48,40},{56,0},{1,57}... | collective-permute-start | bytes 454664 | tf_op jit(solution)/shard_map/ppermute | solution.py:465
  13.3 3.0 %collective-permute-start.5 = (f32[37,8,128]{2,1,0:T(8,128)S(1)}, f32[37,8,128]{2,1,0:T(8,128)S(1)}, u32[]{:S(2)}, u32[]{:S(2)}) collective-permute-start(f32[37,8,128]{2,1,0:T(8,128)S(1)} %get-tuple-element.61), channel_id=1, source_target_pairs={{0,7},{1,2},{2,1},{3,4},{4,3},{5,6},{6,5},{7,0},{8,15},{9,10},{10,... | collective-permute-start | bytes 454664 | tf_op jit(solution)/shard_map/ppermute | solution.py:465
  16.3 0.0 collective-permute-done.refs_0_
  16.3 0.2 collective-permute-start.4
  16.4 0.7 copy-done
  17.1 1.9 %prepare.1 = (f32[2048,128]{1,0:T(8,128)S(1)}, f32[8,8,8,128]{3,2,1,0:T(8,128)S(1)}, f32[8,8,8,128]{3,2,1,0:T(8,128)S(1)}, f32[8,8,8,128]{3,2,1,0:T(8,128)S(1)},...) custom-call(f32[3,6]{1,0:T(4,128)S(1)} %copy-done, f32[5,8,8,128]{3,2,1,0:T(8,128)S(1)} %get-tuple-element.51.pm.inner, ...), custom_call_target="tpu_custom_call" | custom-call | tf_op jit(solution)/shard_map/prepare/pallas_call | solution.py:518
  19.0 1.2 %local1.1.part = f32[4,8,8,8,128]{4,3,2,1,0:T(8,128)S(1)} custom-call(f32[4,8,8,8,128]{4,3,2,1,0:T(8,128)S(1)} %get-tuple-element.50.refs_0_.cur.v0, f32[8,8,8,128]{3,2,1,0:T(8,128)S(1)} %get-tuple-element.52.refs_1_, f32[8,8,8,128]{3,2,1,0:T(8,128)S(1)} %get-tuple-element.53.refs_2_, f32[8,8,8,128]{3,2,1,0:T(8,128)S(1)} %get-tuple-element.54.refs_3_, ...), custom_call_target="tpu_custom_call" | custom-call | flops 6291456 | bytes 3145728 | tf_op jit(solution)/shard_map/local1/pallas_call | solution.py:529
  20.3 0.0 collective-permute-done.1.refs_1_
  20.3 0.0 collective-permute-done.2.refs_2_
  20.3 0.0 collective-permute-done.3.refs_3_
  20.3 0.0 collective-permute-done.5.refs_5_
  20.3 0.0 collective-permute-done.4.refs_4_
  20.3 1.5 %step1.1 = (f32[4,8,8,8,128]{4,3,2,1,0:T(8,128)S(1)}, f32[32,8,128]{2,1,0:T(8,128)S(1)}, f32[32,8,128]{2,1,0:T(8,128)S(1)}, f32[32,8,128]{2,1,0:T(8,128)S(1)}, f...) custom-call(s32[9]{0:T(128)S(1)} %convert_element_type.3.place, ...), custom_call_target="tpu_custom_call" | custom-call | tf_op jit(solution)/shard_map/step1/pallas_call | solution.py:543
  21.9 0.4 collective-permute-start.6
  22.3 0.6 collective-permute-start.7
  22.9 0.0 collective-permute-start.8
  22.9 2.3 %collective-permute-start.9 = (f32[32,8,128]{2,1,0:T(8,128)S(1)}, f32[32,8,128]{2,1,0:T(8,128)S(1)}, u32[]{:S(2)}, u32[]{:S(2)}) collective-permute-start(f32[32,8,128]{2,1,0:T(8,128)S(1)} %get-tuple-element.69), channel_id=1, source_target_pairs={{0,56},{8,16},{16,8},{24,32},{32,24},{40,48},{48,40},{56,0},{1,57}... | collective-permute-start | bytes 393224 | tf_op jit(solution)/shard_map/ppermute | solution.py:465
  25.2 2.3 %collective-permute-start.11 = (f32[32,8,128]{2,1,0:T(8,128)S(1)}, f32[32,8,128]{2,1,0:T(8,128)S(1)}, u32[]{:S(2)}, u32[]{:S(2)}) collective-permute-start(f32[32,8,128]{2,1,0:T(8,128)S(1)} %get-tuple-element.70), channel_id=1, source_target_pairs={{0,7},{1,2},{2,1},{3,4},{4,3},{5,6},{6,5},{7,0},{8,15},{9,10},{10,... | collective-permute-start | bytes 393224 | tf_op jit(solution)/shard_map/ppermute | solution.py:465
  27.5 0.0 collective-permute-done.6.refs_0_
  27.5 0.8 collective-permute-start.10
  28.3 1.4 %gram0.1 = (bf16[4,8,8,16,128]{4,3,2,1,0:T(8,128)(2,1)S(1)}, f32[8,128]{1,0:T(8,128)S(1)}) custom-call(f32[4,8,8,8,128]{4,3,2,1,0:T(8,128)S(1)} %get-tuple-element.50.refs_0_.cur.v0), custom_call_target="tpu_custom_call" | custom-call | flops 16777216 | bytes 3145728 | tf_op jit(solution)/shard_map/gram0/pallas_call | solution.py:499
  29.7 1.2 %local2.1.part = f32[4,8,8,8,128]{4,3,2,1,0:T(8,128)S(1)} custom-call(f32[4,8,8,8,128]{4,3,2,1,0:T(8,128)S(1)} %get-tuple-element.62.refs_0_.cur, f32[8,8,8,128]{3,2,1,0:T(8,128)S(1)} %get-tuple-element.52.refs_1_, f32[8,8,8,128]{3,2,1,0:T(8,128)S(1)} %get-tuple-element.53.refs_2_, f32[8,8,8,128]{3,2,1,0:T(8,128)S(1)} %get-tuple-element.54.refs_3_, ...), custom_call_target="tpu_custom_call" | custom-call | flops 6291456 | bytes 3145728 | tf_op jit(solution)/shard_map/local2/pallas_call | solution.py:529
  30.9 1.8 %gram1.1 = (bf16[4,8,8,16,128]{4,3,2,1,0:T(8,128)(2,1)S(1)}, f32[8,128]{1,0:T(8,128)S(1)}) custom-call(f32[4,8,8,8,128]{4,3,2,1,0:T(8,128)S(1)} %get-tuple-element.62.refs_0_.cur, bf16[4,8,8,16,128]{4,3,2,1,0:T(8,128)(2,1)S(1)} %get-tuple-element.63.refs_1_.s0, f32[8,128]{1,0:T(8,128)S(1)} %get-tuple-element.64.refs_2_), custom_call_target="tpu_custom_call" | custom-call | flops 33554432 | bytes 4194304 | tf_op jit(solution)/shard_map/gram1/pallas_call | solution.py:499
  32.7 0.0 collective-permute-done.7.refs_1_
  32.7 0.0 collective-permute-done.8.refs_2_
  32.7 0.0 collective-permute-done.9.refs_3_
  32.7 0.0 collective-permute-done.11.refs_5_
  32.7 0.0 collective-permute-done.10.refs_4_
  32.7 1.5 %step2.1 = (f32[4,8,8,8,128]{4,3,2,1,0:T(8,128)S(1)}, f32[32,8,128]{2,1,0:T(8,128)S(1)}, f32[32,8,128]{2,1,0:T(8,128)S(1)}, f32[32,8,128]{2,1,0:T(8,128)S(1)}, f...) custom-call(s32[9]{0:T(128)S(1)} %convert_element_type.3.place, f32[8,128]{1,0:T(8,128)S(1)} %get-tuple-element.65.piece.refs_3_, ...), custom_call_target="tpu_custom_call" | custom-call | tf_op jit(solution)/shard_map/step2/pallas_call | solution.py:558
  34.2 0.4 collective-permute-start.12
  34.6 1.0 %collective-permute-start.13 = (f32[32,8,128]{2,1,0:T(8,128)S(1)}, f32[32,8,128]{2,1,0:T(8,128)S(1)}, u32[]{:S(2)}, u32[]{:S(2)}) collective-permute-start(f32[32,8,128]{2,1,0:T(8,128)S(1)} %get-tuple-element.78), channel_id=1, source_target_pairs={{0,192},{64,128},{128,64},{192,0},{1,193},{65,129},{129,65},{193,1... | collective-permute-start | bytes 393224 | tf_op jit(solution)/shard_map/ppermute | solution.py:465
  35.6 0.7 collective-permute-start.14
  36.4 0.7 collective-permute-start.15
  37.1 2.6 %collective-permute-start.17 = (f32[32,8,128]{2,1,0:T(8,128)S(1)}, f32[32,8,128]{2,1,0:T(8,128)S(1)}, u32[]{:S(2)}, u32[]{:S(2)}) collective-permute-start(f32[32,8,128]{2,1,0:T(8,128)S(1)} %get-tuple-element.81), channel_id=1, source_target_pairs={{0,7},{1,2},{2,1},{3,4},{4,3},{5,6},{6,5},{7,0},{8,15},{9,10},{10,... | collective-permute-start | bytes 393224 | tf_op jit(solution)/shard_map/ppermute | solution.py:465
  39.7 0.0 collective-permute-done.12.refs_0_
  39.7 0.5 collective-permute-start.16
  40.2 1.2 %local3.1.part = f32[4,8,8,8,128]{4,3,2,1,0:T(8,128)S(1)} custom-call(f32[4,8,8,8,128]{4,3,2,1,0:T(8,128)S(1)} %get-tuple-element.74.refs_0_.cur, f32[8,8,8,128]{3,2,1,0:T(8,128)S(1)} %get-tuple-element.52.refs_1_, f32[8,8,8,128]{3,2,1,0:T(8,128)S(1)} %get-tuple-element.53.refs_2_, f32[8,8,8,128]{3,2,1,0:T(8,128)S(1)} %get-tuple-element.54.refs_3_, ...), custom_call_target="tpu_custom_call" | custom-call | flops 6291456 | bytes 3145728 | tf_op jit(solution)/shard_map/local3/pallas_call | solution.py:529
  41.4 2.1 %gram2.1 = (bf16[4,8,8,16,128]{4,3,2,1,0:T(8,128)(2,1)S(1)}, f32[8,128]{1,0:T(8,128)S(1)}) custom-call(f32[4,8,8,8,128]{4,3,2,1,0:T(8,128)S(1)} %get-tuple-element.74.refs_0_.cur, bf16[4,8,8,16,128]{4,3,2,1,0:T(8,128)(2,1)S(1)} %get-tuple-element.63.refs_1_.s0, bf16[4,8,8,16,128]{4,3,2,1,0:T(8,128)(2,1)S(1)} %get-tuple-element.75.refs_2_.s1, ...), custom_call_target="tpu_custom_call" | custom-call | flops 50331648 | bytes 5242880 | tf_op jit(solution)/shard_map/gram2/pallas_call | solution.py:499
  43.5 0.0 collective-permute-done.13.refs_1_
  43.5 0.0 collective-permute-done.14.refs_2_
  43.5 0.0 collective-permute-done.15.refs_3_
  43.5 0.0 collective-permute-done.17.refs_5_
  43.5 0.0 collective-permute-done.16.refs_4_
  43.6 1.5 %step3.1 = (f32[4,8,8,8,128]{4,3,2,1,0:T(8,128)S(1)}, f32[32,8,128]{2,1,0:T(8,128)S(1)}, f32[32,8,128]{2,1,0:T(8,128)S(1)}, f32[32,8,128]{2,1,0:T(8,128)S(1)}, f...) custom-call(s32[9]{0:T(128)S(1)} %convert_element_type.3.place, f32[8,128]{1,0:T(8,128)S(1)} %get-tuple-element.76.piece.refs_4_, ...), custom_call_target="tpu_custom_call" | custom-call | tf_op jit(solution)/shard_map/step3/pallas_call | solution.py:558
  45.0 0.4 collective-permute-start.18
  45.4 1.0 %collective-permute-start.19 = (f32[32,8,128]{2,1,0:T(8,128)S(1)}, f32[32,8,128]{2,1,0:T(8,128)S(1)}, u32[]{:S(2)}, u32[]{:S(2)}) collective-permute-start(f32[32,8,128]{2,1,0:T(8,128)S(1)} %get-tuple-element.86), channel_id=1, source_target_pairs={{0,192},{64,128},{128,64},{192,0},{1,193},{65,129},{129,65},{193,1... | collective-permute-start | bytes 393224 | tf_op jit(solution)/shard_map/ppermute | solution.py:465
  46.4 0.7 collective-permute-start.20
  47.2 0.7 collective-permute-start.21
  47.9 2.3 %collective-permute-start.23 = (f32[32,8,128]{2,1,0:T(8,128)S(1)}, f32[32,8,128]{2,1,0:T(8,128)S(1)}, u32[]{:S(2)}, u32[]{:S(2)}) collective-permute-start(f32[32,8,128]{2,1,0:T(8,128)S(1)} %get-tuple-element.89), channel_id=1, source_target_pairs={{0,7},{1,2},{2,1},{3,4},{4,3},{5,6},{6,5},{7,0},{8,15},{9,10},{10,... | collective-permute-start | bytes 393224 | tf_op jit(solution)/shard_map/ppermute | solution.py:465
  50.2 0.8 collective-permute-start.22
  51.0 1.2 %local4.1.part = f32[4,8,8,8,128]{4,3,2,1,0:T(8,128)S(1)} custom-call(f32[4,8,8,8,128]{4,3,2,1,0:T(8,128)S(1)} %get-tuple-element.82.refs_0_.cur, f32[8,8,8,128]{3,2,1,0:T(8,128)S(1)} %get-tuple-element.52.refs_1_, f32[8,8,8,128]{3,2,1,0:T(8,128)S(1)} %get-tuple-element.53.refs_2_, f32[8,8,8,128]{3,2,1,0:T(8,128)S(1)} %get-tuple-element.54.refs_3_, ...), custom_call_target="tpu_custom_call" | custom-call | flops 6291456 | bytes 3145728 | tf_op jit(solution)/shard_map/local4/pallas_call | solution.py:529
  52.3 2.3 %gram3.1 = (bf16[4,8,8,16,128]{4,3,2,1,0:T(8,128)(2,1)S(1)}, f32[8,128]{1,0:T(8,128)S(1)}) custom-call(f32[4,8,8,8,128]{4,3,2,1,0:T(8,128)S(1)} %get-tuple-element.82.refs_0_.cur, bf16[4,8,8,16,128]{4,3,2,1,0:T(8,128)(2,1)S(1)} %get-tuple-element.63.refs_1_.s0, bf16[4,8,8,16,128]{4,3,2,1,0:T(8,128)(2,1)S(1)} %get-tuple-element.75.refs_2_.s1, ...), custom_call_target="tpu_custom_call" | custom-call | flops 67108864 | bytes 6291456 | tf_op jit(solution)/shard_map/gram3/pallas_call | solution.py:499
  54.6 0.0 collective-permute-done.19.refs_1_
  54.6 0.0 collective-permute-done.21.refs_3_
  54.6 1.0 %step4.1.refs_0_ = f32[4,8,8,8,128]{4,3,2,1,0:T(8,128)S(1)} custom-call(s32[9]{0:T(128)S(1)} %convert_element_type.3.place, f32[8,128]{1,0:T(8,128)S(1)} %get-tuple-element.84.piece.refs_2_, f32[4,8,8,8,128]{4,3,2,1,0:T(8,128)S(1)} %local4.1.part, f32[4,8,8,8,128]{4,3,2,1,0:T(8,128)S(1)} %get-tuple-element.82.refs_0_.cur, ...), custom_call_target="tpu_custom_call" | custom-call | tf_op jit(solution)/shard_map/step4/pallas_call | solution.py:558
  55.7 1.5 %gram4.1 = (bf16[4,8,8,16,128]{4,3,2,1,0:T(8,128)(2,1)S(1)}, f32[8,8,128]{2,1,0:T(8,128)S(1)}) custom-call(f32[4,8,8,8,128]{4,3,2,1,0:T(8,128)S(1)} %step4.1.refs_0_, bf16[4,8,8,16,128]{4,3,2,1,0:T(8,128)(2,1)S(1)} %get-tuple-element.90.refs_1_.s3, f32[8,128]{1,0:T(8,128)S(1)} %get-tuple-element.84.piece.refs_2_), custom_call_target="tpu_custom_call" | custom-call | flops 83886080 | bytes 7340032 | tf_op jit(solution)/shard_map/gram4/pallas_call | solution.py:499
  57.2 11.2 %all_to_all.10.parts = f32[8,8,128]{2,1,0:T(8,128)S(1)} all-to-all(f32[8,8,128]{2,1,0:T(8,128)S(1)} %get-tuple-element.91), channel_id=1, replica_groups=mesh['gx'=4,'gy'=8,'gz'=8] {'gy'}, dimensions={0} | all-to-all | bytes 65536 | tf_op jit(solution)/shard_map/all_to_all | solution.py:569
  68.4 14.2 %all_to_all.11.packed = f32[32,8,128]{2,1,0:T(8,128)S(1)} all-to-all(f32[32,8,128]{2,1,0:T(8,128)S(1)} %relay.1), channel_id=1, replica_groups=mesh['gx'=4,'gy'=8,'gz'=8] {'gx','gz'}, dimensions={0} | all-to-all | bytes 262144 | tf_op jit(solution)/shard_map/all_to_all | solution.py:578
  82.6 5.4 %finish.1 = (f32[32,64,128]{2,1,0:T(8,128)}, f32[32,64,128]{2,1,0:T(8,128)}, f32[128,64,128]{2,1,0:T(8,128)}) custom-call(f32[32,8,128]{2,1,0:T(8,128)S(1)} %all_to_all.11.packed, bf16[4,8,8,16,128]{4,3,2,1,0:T(8,128)(2,1)S(1)} %get-tuple-element.63.refs_1_.s0, bf16[4,8,8,16,128]{4,3,2,1,0:T(8,128)(2,1)S(1)} %get-tuple-element.75.refs_2_.s1, ...), custom_call_target="tpu_custom_call" | custom-call | tf_op jit(solution)/shard_map/finish/pallas_call | solution.py:580
  (7 shorter events, 0.0 us)
Async XLA Ops:
  3.1 13.2 %collective-permute-start = (f32[37,8,128]{2,1,0:T(8,128)S(1)}, f32[37,8,128]{2,1,0:T(8,128)S(1)}, u32[]{:S(2)}, u32[]{:S(2)}) collective-permute-start(f32[37,8,128]{2,1,0:T(8,128)S(1)} %get-tuple-element.57), channel_id=1, source_target_pairs={{0,64},{64,0},{128,192},{192,128},{1,65},{65,1},{129,193},{193,129... | collective-permute-start | bytes 454664 | tf_op jit(solution)/shard_map/ppermute | solution.py:464
  5.2 15.1 %collective-permute-start.1 = (f32[37,8,128]{2,1,0:T(8,128)S(1)}, f32[37,8,128]{2,1,0:T(8,128)S(1)}, u32[]{:S(2)}, u32[]{:S(2)}) collective-permute-start(f32[37,8,128]{2,1,0:T(8,128)S(1)} %get-tuple-element.58), channel_id=1, source_target_pairs={{0,192},{64,128},{128,64},{192,0},{1,193},{65,129},{129,65},{193,1... | collective-permute-start | bytes 454664 | tf_op jit(solution)/shard_map/ppermute | solution.py:465
  7.0 13.3 %collective-permute-start.2 = (f32[37,8,128]{2,1,0:T(8,128)S(1)}, f32[37,8,128]{2,1,0:T(8,128)S(1)}, u32[]{:S(2)}, u32[]{:S(2)}) collective-permute-start(f32[37,8,128]{2,1,0:T(8,128)S(1)} %get-tuple-element.59), channel_id=1, source_target_pairs={{0,8},{8,0},{16,24},{24,16},{32,40},{40,32},{48,56},{56,48},{1,9},... | collective-permute-start | bytes 454664 | tf_op jit(solution)/shard_map/ppermute | solution.py:464
  8.6 11.6 %collective-permute-start.3 = (f32[37,8,128]{2,1,0:T(8,128)S(1)}, f32[37,8,128]{2,1,0:T(8,128)S(1)}, u32[]{:S(2)}, u32[]{:S(2)}) collective-permute-start(f32[37,8,128]{2,1,0:T(8,128)S(1)} %get-tuple-element.60), channel_id=1, source_target_pairs={{0,56},{8,16},{16,8},{24,32},{32,24},{40,48},{48,40},{56,0},{1,57}... | collective-permute-start | bytes 454664 | tf_op jit(solution)/shard_map/ppermute | solution.py:465
  13.3 7.0 %collective-permute-start.5 = (f32[37,8,128]{2,1,0:T(8,128)S(1)}, f32[37,8,128]{2,1,0:T(8,128)S(1)}, u32[]{:S(2)}, u32[]{:S(2)}) collective-permute-start(f32[37,8,128]{2,1,0:T(8,128)S(1)} %get-tuple-element.61), channel_id=1, source_target_pairs={{0,7},{1,2},{2,1},{3,4},{4,3},{5,6},{6,5},{7,0},{8,15},{9,10},{10,... | collective-permute-start | bytes 454664 | tf_op jit(solution)/shard_map/ppermute | solution.py:465
  16.3 4.0 %collective-permute-start.4 = (f32[37,8,128]{2,1,0:T(8,128)S(1)}, f32[37,8,128]{2,1,0:T(8,128)S(1)}, u32[]{:S(2)}, u32[]{:S(2)}) collective-permute-start(f32[37,8,128]{2,1,0:T(8,128)S(1)} %get-tuple-element.61), channel_id=1, source_target_pairs={{0,1},{1,0},{2,3},{3,2},{4,5},{5,4},{6,7},{7,6},{8,9},{9,8},{10,11... | collective-permute-start | bytes 454664 | tf_op jit(solution)/shard_map/ppermute | solution.py:464
  16.4 0.7 copy-start
  21.9 5.6 %collective-permute-start.6 = (f32[32,8,128]{2,1,0:T(8,128)S(1)}, f32[32,8,128]{2,1,0:T(8,128)S(1)}, u32[]{:S(2)}, u32[]{:S(2)}) collective-permute-start(f32[32,8,128]{2,1,0:T(8,128)S(1)} %get-tuple-element.66), channel_id=1, source_target_pairs={{0,64},{64,0},{128,192},{192,128},{1,65},{65,1},{129,193},{193,129... | collective-permute-start | bytes 393224 | tf_op jit(solution)/shard_map/ppermute | solution.py:464
  22.3 10.4 %collective-permute-start.7 = (f32[32,8,128]{2,1,0:T(8,128)S(1)}, f32[32,8,128]{2,1,0:T(8,128)S(1)}, u32[]{:S(2)}, u32[]{:S(2)}) collective-permute-start(f32[32,8,128]{2,1,0:T(8,128)S(1)} %get-tuple-element.67), channel_id=1, source_target_pairs={{0,192},{64,128},{128,64},{192,0},{1,193},{65,129},{129,65},{193,1... | collective-permute-start | bytes 393224 | tf_op jit(solution)/shard_map/ppermute | solution.py:465
  22.9 9.8 %collective-permute-start.8 = (f32[32,8,128]{2,1,0:T(8,128)S(1)}, f32[32,8,128]{2,1,0:T(8,128)S(1)}, u32[]{:S(2)}, u32[]{:S(2)}) collective-permute-start(f32[32,8,128]{2,1,0:T(8,128)S(1)} %get-tuple-element.68), channel_id=1, source_target_pairs={{0,8},{8,0},{16,24},{24,16},{32,40},{40,32},{48,56},{56,48},{1,9},... | collective-permute-start | bytes 393224 | tf_op jit(solution)/shard_map/ppermute | solution.py:464
  22.9 9.8 %collective-permute-start.9 = (f32[32,8,128]{2,1,0:T(8,128)S(1)}, f32[32,8,128]{2,1,0:T(8,128)S(1)}, u32[]{:S(2)}, u32[]{:S(2)}) collective-permute-start(f32[32,8,128]{2,1,0:T(8,128)S(1)} %get-tuple-element.69), channel_id=1, source_target_pairs={{0,56},{8,16},{16,8},{24,32},{32,24},{40,48},{48,40},{56,0},{1,57}... | collective-permute-start | bytes 393224 | tf_op jit(solution)/shard_map/ppermute | solution.py:465
  25.2 7.6 %collective-permute-start.11 = (f32[32,8,128]{2,1,0:T(8,128)S(1)}, f32[32,8,128]{2,1,0:T(8,128)S(1)}, u32[]{:S(2)}, u32[]{:S(2)}) collective-permute-start(f32[32,8,128]{2,1,0:T(8,128)S(1)} %get-tuple-element.70), channel_id=1, source_target_pairs={{0,7},{1,2},{2,1},{3,4},{4,3},{5,6},{6,5},{7,0},{8,15},{9,10},{10,... | collective-permute-start | bytes 393224 | tf_op jit(solution)/shard_map/ppermute | solution.py:465
  27.5 5.3 %collective-permute-start.10 = (f32[32,8,128]{2,1,0:T(8,128)S(1)}, f32[32,8,128]{2,1,0:T(8,128)S(1)}, u32[]{:S(2)}, u32[]{:S(2)}) collective-permute-start(f32[32,8,128]{2,1,0:T(8,128)S(1)} %get-tuple-element.70), channel_id=1, source_target_pairs={{0,1},{1,0},{2,3},{3,2},{4,5},{5,4},{6,7},{7,6},{8,9},{9,8},{10,11... | collective-permute-start | bytes 393224 | tf_op jit(solution)/shard_map/ppermute | solution.py:464
  34.2 5.5 %collective-permute-start.12 = (f32[32,8,128]{2,1,0:T(8,128)S(1)}, f32[32,8,128]{2,1,0:T(8,128)S(1)}, u32[]{:S(2)}, u32[]{:S(2)}) collective-permute-start(f32[32,8,128]{2,1,0:T(8,128)S(1)} %get-tuple-element.77), channel_id=1, source_target_pairs={{0,64},{64,0},{128,192},{192,128},{1,65},{65,1},{129,193},{193,129... | collective-permute-start | bytes 393224 | tf_op jit(solution)/shard_map/ppermute | solution.py:464
  34.6 8.9 %collective-permute-start.13 = (f32[32,8,128]{2,1,0:T(8,128)S(1)}, f32[32,8,128]{2,1,0:T(8,128)S(1)}, u32[]{:S(2)}, u32[]{:S(2)}) collective-permute-start(f32[32,8,128]{2,1,0:T(8,128)S(1)} %get-tuple-element.78), channel_id=1, source_target_pairs={{0,192},{64,128},{128,64},{192,0},{1,193},{65,129},{129,65},{193,1... | collective-permute-start | bytes 393224 | tf_op jit(solution)/shard_map/ppermute | solution.py:465
  35.6 7.9 %collective-permute-start.14 = (f32[32,8,128]{2,1,0:T(8,128)S(1)}, f32[32,8,128]{2,1,0:T(8,128)S(1)}, u32[]{:S(2)}, u32[]{:S(2)}) collective-permute-start(f32[32,8,128]{2,1,0:T(8,128)S(1)} %get-tuple-element.79), channel_id=1, source_target_pairs={{0,8},{8,0},{16,24},{24,16},{32,40},{40,32},{48,56},{56,48},{1,9},... | collective-permute-start | bytes 393224 | tf_op jit(solution)/shard_map/ppermute | solution.py:464
  36.4 7.2 %collective-permute-start.15 = (f32[32,8,128]{2,1,0:T(8,128)S(1)}, f32[32,8,128]{2,1,0:T(8,128)S(1)}, u32[]{:S(2)}, u32[]{:S(2)}) collective-permute-start(f32[32,8,128]{2,1,0:T(8,128)S(1)} %get-tuple-element.80), channel_id=1, source_target_pairs={{0,56},{8,16},{16,8},{24,32},{32,24},{40,48},{48,40},{56,0},{1,57}... | collective-permute-start | bytes 393224 | tf_op jit(solution)/shard_map/ppermute | solution.py:465
  37.1 6.4 %collective-permute-start.17 = (f32[32,8,128]{2,1,0:T(8,128)S(1)}, f32[32,8,128]{2,1,0:T(8,128)S(1)}, u32[]{:S(2)}, u32[]{:S(2)}) collective-permute-start(f32[32,8,128]{2,1,0:T(8,128)S(1)} %get-tuple-element.81), channel_id=1, source_target_pairs={{0,7},{1,2},{2,1},{3,4},{4,3},{5,6},{6,5},{7,0},{8,15},{9,10},{10,... | collective-permute-start | bytes 393224 | tf_op jit(solution)/shard_map/ppermute | solution.py:465
  39.7 3.8 %collective-permute-start.16 = (f32[32,8,128]{2,1,0:T(8,128)S(1)}, f32[32,8,128]{2,1,0:T(8,128)S(1)}, u32[]{:S(2)}, u32[]{:S(2)}) collective-permute-start(f32[32,8,128]{2,1,0:T(8,128)S(1)} %get-tuple-element.81), channel_id=1, source_target_pairs={{0,1},{1,0},{2,3},{3,2},{4,5},{5,4},{6,7},{7,6},{8,9},{9,8},{10,11... | collective-permute-start | bytes 393224 | tf_op jit(solution)/shard_map/ppermute | solution.py:464
  45.0 5.2 %collective-permute-start.18 = (f32[32,8,128]{2,1,0:T(8,128)S(1)}, f32[32,8,128]{2,1,0:T(8,128)S(1)}, u32[]{:S(2)}, u32[]{:S(2)}) collective-permute-start(f32[32,8,128]{2,1,0:T(8,128)S(1)} %get-tuple-element.85), channel_id=1, source_target_pairs={{0,64},{64,0},{128,192},{192,128},{1,65},{65,1},{129,193},{193,129... | collective-permute-start | bytes 393224 | tf_op jit(solution)/shard_map/ppermute | solution.py:464
  45.4 9.2 %collective-permute-start.19 = (f32[32,8,128]{2,1,0:T(8,128)S(1)}, f32[32,8,128]{2,1,0:T(8,128)S(1)}, u32[]{:S(2)}, u32[]{:S(2)}) collective-permute-start(f32[32,8,128]{2,1,0:T(8,128)S(1)} %get-tuple-element.86), channel_id=1, source_target_pairs={{0,192},{64,128},{128,64},{192,0},{1,193},{65,129},{129,65},{193,1... | collective-permute-start | bytes 393224 | tf_op jit(solution)/shard_map/ppermute | solution.py:465
  46.4 8.2 %collective-permute-start.20 = (f32[32,8,128]{2,1,0:T(8,128)S(1)}, f32[32,8,128]{2,1,0:T(8,128)S(1)}, u32[]{:S(2)}, u32[]{:S(2)}) collective-permute-start(f32[32,8,128]{2,1,0:T(8,128)S(1)} %get-tuple-element.87), channel_id=1, source_target_pairs={{0,8},{8,0},{16,24},{24,16},{32,40},{40,32},{48,56},{56,48},{1,9},... | collective-permute-start | bytes 393224 | tf_op jit(solution)/shard_map/ppermute | solution.py:464
  47.2 7.4 %collective-permute-start.21 = (f32[32,8,128]{2,1,0:T(8,128)S(1)}, f32[32,8,128]{2,1,0:T(8,128)S(1)}, u32[]{:S(2)}, u32[]{:S(2)}) collective-permute-start(f32[32,8,128]{2,1,0:T(8,128)S(1)} %get-tuple-element.88), channel_id=1, source_target_pairs={{0,56},{8,16},{16,8},{24,32},{32,24},{40,48},{48,40},{56,0},{1,57}... | collective-permute-start | bytes 393224 | tf_op jit(solution)/shard_map/ppermute | solution.py:465
  47.9 6.7 %collective-permute-start.23 = (f32[32,8,128]{2,1,0:T(8,128)S(1)}, f32[32,8,128]{2,1,0:T(8,128)S(1)}, u32[]{:S(2)}, u32[]{:S(2)}) collective-permute-start(f32[32,8,128]{2,1,0:T(8,128)S(1)} %get-tuple-element.89), channel_id=1, source_target_pairs={{0,7},{1,2},{2,1},{3,4},{4,3},{5,6},{6,5},{7,0},{8,15},{9,10},{10,... | collective-permute-start | bytes 393224 | tf_op jit(solution)/shard_map/ppermute | solution.py:465
  50.2 4.4 %collective-permute-start.22 = (f32[32,8,128]{2,1,0:T(8,128)S(1)}, f32[32,8,128]{2,1,0:T(8,128)S(1)}, u32[]{:S(2)}, u32[]{:S(2)}) collective-permute-start(f32[32,8,128]{2,1,0:T(8,128)S(1)} %get-tuple-element.89), channel_id=1, source_target_pairs={{0,1},{1,0},{2,3},{3,2},{4,5},{5,4},{6,7},{7,6},{8,9},{9,8},{10,11... | collective-permute-start | bytes 393224 | tf_op jit(solution)/shard_map/ppermute | solution.py:464
